TPU v7x, 32 devices: a whole 2x2x4 slice. The times are simulated.
32 devices in a mesh: row: 4 (over y, x), col: 8 (over z, core).
Axes of the slice: x: 2, y: 2, z: 4, core: 2. Of those that a mesh axis runs over, the one named last changes fastest.
Arguments:
- image: bfloat16 [64, 128, 1280], P('row', 'col'), may hold values from -15 to 15
- stale_first: bfloat16 [64, 128, 1280], P('row', 'col'), may hold values from -6 to 6
- stale_normed: bfloat16 [64, 128, 1280], P('row', 'col'), may hold values from -5 to 5
- timestep: int32 [1], replicated, may hold values from 0 to 999
- time_weight: bfloat16 [320, 1280], replicated, may hold values from -0.3125 to 0.3125
- gain_first: float32 [1280], replicated, may hold values from 0.5 to 1.5
- shift_first: float32 [1280], replicated, may hold values from -3 to 3
- codes_first: int32 [9, 320, 1280], replicated, may hold values from 0 to 65535
- table_first: float32 [16, 1280], replicated, may hold values from -0.0546875 to 0.0546875
- bias_first: float32 [1280], replicated, may hold values from -3 to 3
- attn_gain: float32 [1280], replicated, may hold values from 0.5 to 1.5
- query_codes: int32 [320, 1280], replicated, may hold values from 0 to 65535
- query_table: float32 [16, 1280], replicated
- key_codes: int32 [320, 1280], replicated, may hold values from 0 to 65535
- key_table: float32 [16, 1280], replicated, may hold values from -0.15625 to 0.15625
- value_codes: int32 [320, 1280], replicated, may hold values from 0 to 65535
- value_table: float32 [16, 1280], replicated, may hold values from -0.15625 to 0.15625
- out_codes: int32 [320, 1280], replicated, may hold values from 0 to 65535
- out_table: float32 [16, 1280], replicated, may hold values from -0.15625 to 0.15625
Outputs:
- output: bfloat16 [64, 128, 1280], P('row', 'col')
Inputs may be any that keep to these rules, and one draw needn't show every extreme that they name: `codes_first`: each word packs four 4-bit codes: the code of input channel 4 g + b lies in bits 4 b to 4 b + 3 of word g. `query_codes`: packed as codes_first. `key_codes`: packed as codes_first. `value_codes`: packed as codes_first. `out_codes`: packed as codes_first.
All inputs are finite; a program needn't handle non-finite values.
Results may differ from a plain program's by a relative error of at most 0.012.
Values may be sent and summed in bfloat16 or wider, within the bound.
No kernel may reach another device: no remote copies, remote signals or barrier semaphores. Data moves between devices by JAX's collectives and lax.ppermute only.
A program may use at most 192 MiB of HBM per device.

v0:
```python
import math

import jax
import jax.numpy as jnp
from jax import lax
from jax.sharding import PartitionSpec as P

HEADS = 20
HEAD_DIM = 64
GROUPS = 32
TEMB = 320
POOL = 4


def extended(cells, sides, width):
    for axis, dim in sides:
        count = lax.axis_size(axis)
        ends = count - 1
        head = lax.slice_in_dim(cells, 0, width, axis=dim)
        tail = lax.slice_in_dim(cells, cells.shape[dim] - width, cells.shape[dim], axis=dim)
        cells = jnp.concatenate(
            [
                lax.ppermute(tail, axis, [(i, (i + 1) % count) for i in range(ends)]),
                cells,
                lax.ppermute(head, axis, [((i + 1) % count, i) for i in range(ends)]),
            ],
            axis=dim,
        )
    return cells


def unpack_weight(packed, table):
    out_width = packed.shape[-1]
    shifts = 4 * jnp.arange(4, dtype=jnp.int32)
    nibbles = jnp.right_shift(packed[..., :, None, :], shifts[:, None]) & 15
    nibbles = nibbles.reshape(packed.shape[:-2] + (packed.shape[-2] * 4, out_width))
    levels = table.astype(jnp.bfloat16)
    weight = jnp.zeros(nibbles.shape, jnp.bfloat16)
    for code_value in range(16):
        weight = jnp.where(nibbles == code_value, levels[code_value], weight)
    return weight


def time_vector(timestep, time_weight):
    half_width = TEMB // 2
    frequency = jnp.exp(-math.log(10000.0) * jnp.arange(half_width, dtype=jnp.float32) / half_width)
    angles = timestep.astype(jnp.float32)[:, None] * frequency[None, :]
    sinusoid = jnp.concatenate([jnp.cos(angles), jnp.sin(angles)], axis=1).astype(jnp.bfloat16)
    return jax.nn.silu(jnp.dot(sinusoid, time_weight, preferred_element_type=jnp.float32))[0]


def group_terms(values):
    grouped = values.reshape(-1, GROUPS, values.shape[-1] // GROUPS)
    return (jnp.sum(grouped, axis=(0, 2)), jnp.sum(grouped * grouped, axis=(0, 2)))


def apply_norm(values, group_sums, members, gain, shift):
    grouped = values.reshape(-1, GROUPS, values.shape[-1] // GROUPS)
    average = group_sums[0] / members
    mean_square = group_sums[1] / members
    inv_std = lax.rsqrt(mean_square - average * average + 1e-05)
    normalized = ((grouped - average[None, :, None]) * inv_std[None, :, None]).reshape(values.shape)
    return jax.nn.silu(normalized * gain + shift).astype(jnp.bfloat16)


def patch_conv(current, rim_cells, packed, table):
    height, across, channels = current.shape
    padded = rim_cells.at[1 : height + 1, 1 : across + 1].set(current)
    summed = jnp.zeros((height * across, packed.shape[-1]), jnp.float32)
    for tap_index in range(9):
        row_start = tap_index // 3
        col_start = tap_index % 3
        source = padded[row_start : row_start + height, col_start : col_start + across].reshape(
            -1, channels
        )
        summed = summed + jnp.dot(
            source, unpack_weight(packed[tap_index], table), preferred_element_type=jnp.float32
        )
    return summed.reshape(height, across, -1)


def layer_norm(values, gain):
    average = jnp.mean(values, axis=-1, keepdims=True)
    centred = values - average
    spread = jnp.mean(centred * centred, axis=-1, keepdims=True)
    return (centred * lax.rsqrt(spread + 1e-05) * gain).astype(jnp.bfloat16)


def project(inputs, weight):
    return jnp.dot(inputs, weight, preferred_element_type=jnp.float32).astype(jnp.bfloat16)


def attend(queries, key_rows, value_rows):
    count_rows, channels = queries.shape
    query_heads = queries.reshape(count_rows, HEADS, HEAD_DIM)
    key_heads = key_rows.reshape(-1, HEADS, HEAD_DIM)
    value_heads = value_rows.reshape(-1, HEADS, HEAD_DIM)
    scores = jnp.einsum(
        "qhd,khd->hqk", query_heads, key_heads, preferred_element_type=jnp.float32
    ) / math.sqrt(HEAD_DIM)
    highest = jnp.max(scores, axis=-1, keepdims=True)
    exponent = jnp.exp(scores - highest)
    weights = (exponent / jnp.sum(exponent, axis=-1, keepdims=True)).astype(jnp.bfloat16)
    mixture = jnp.einsum("hqk,khd->qhd", weights, value_heads, preferred_element_type=jnp.float32)
    return mixture.reshape(count_rows, channels).astype(jnp.bfloat16)


def on_device(
    image,
    stale_first,
    stale_normed,
    timestep,
    time_weight,
    gain_first,
    shift_first,
    codes_first,
    table_first,
    bias_first,
    attn_gain,
    query_codes,
    query_table,
    key_codes,
    key_table,
    value_codes,
    value_table,
    out_codes,
    out_table,
):
    height, across, channels = image.shape
    members = height * lax.axis_size("row") * across * lax.axis_size("col") * (channels // GROUPS)
    time_shift = time_vector(timestep, time_weight)
    current = image.astype(jnp.float32)
    sums_first = lax.psum(group_terms(current), ("row", "col"))
    first_act = apply_norm(current, sums_first, members, gain_first, shift_first)
    rim_one = extended(stale_first, (("row", 0), ("col", 1)), 1)
    conv_one = patch_conv(first_act, rim_one, codes_first, table_first) + bias_first + time_shift
    residual = (current + conv_one).astype(jnp.bfloat16)
    normed = layer_norm(residual.astype(jnp.float32), attn_gain).reshape(-1, channels)
    query_weight = unpack_weight(query_codes, query_table)
    key_weight = unpack_weight(key_codes, key_table)
    value_weight = unpack_weight(value_codes, value_table)
    out_weight = unpack_weight(out_codes, out_table)
    queries = project(normed, query_weight)
    fresh_keys = project(normed, key_weight)
    fresh_values = project(normed, value_weight)
    pooled = stale_normed.astype(jnp.float32).reshape(
        height // POOL, POOL, across // POOL, POOL, channels
    )
    pooled = jnp.mean(pooled, axis=(1, 3)).reshape(-1, channels).astype(jnp.bfloat16)
    outgoing = jnp.stack([project(pooled, key_weight), project(pooled, value_weight)])
    arrived = lax.all_gather(outgoing, ("row", "col"), axis=1, tiled=True)
    stale_keys = arrived[0]
    stale_values = arrived[1]
    mixture = attend(
        queries,
        jnp.concatenate([fresh_keys, stale_keys], axis=0),
        jnp.concatenate([fresh_values, stale_values], axis=0),
    )
    output = residual.reshape(-1, channels).astype(jnp.float32) + jnp.dot(
        mixture, out_weight, preferred_element_type=jnp.float32
    )
    return output.reshape(height, across, channels).astype(jnp.bfloat16)


def solution(mesh):
    in_specs = (
        P("row", "col", None),
        P("row", "col", None),
        P("row", "col", None),
        P(),
        P(),
        P(),
        P(),
        P(),
        P(),
        P(),
        P(),
        P(),
        P(),
        P(),
        P(),
        P(),
        P(),
        P(),
        P(),
    )
    out_specs = P("row", "col", None)
    return jax.shard_map(
        on_device, mesh=mesh, in_specs=in_specs, out_specs=out_specs, check_vma=False
    )
```

profile of v0, /device:TPU:0, one launch (start us, length us, event | category | flops | bytes accessed | tf_op | source)
XLA Modules:
  0.0 466.8 jit_solution(5841637032405392007)
XLA Ops:
  7.4 4.8 %collective-permute-start = (bf16[1,16,1280]{2,1,0:T(8,128)(2,1)S(1)}, bf16[1,16,1280]{2,1,0:T(8,128)(2,1)S(1)}, u32[]{:S(2)}, u32[]{:S(2)}) collective-permute-start(bf16[1,16,1280]{2,1,0:T(8,128)(2,1)S(1)} %get-tuple-element.125), channel_id=1, source_target_pairs={{0,8},{8,16},{16,24},{1,9},{9,17},{17,25},{2,10},{10,18},{18,26},{... | collective-permute-start | bytes 122888 | tf_op jit(solution)/shard_map/ppermute | solution.py:23
  12.3 1.3 collective-permute-start.1
  13.6 1.6 reshape.5469
  15.9 17.3 %fusion.358 = bf16[320,4,1280]{2,1,0:T(4,128)(2,1)} fusion(s32[320,1280]{1,0:T(8,128)} %param.36, s32[4]{0:T(128)S(1)} %iota_multiply_fusion, bf16[1280]{0:T(1024)(128)(2,1)S(1)} %get-tuple-element.52, bf16[1280]{0:T(1024)(128)(2,1)S(1)} %get-tuple-element.53, bf16[1280]{0:T(1024)(128)(2,1)S(1)} %get-tuple-element.54, ...), kind=kLoop, calls=%fused_computation.372 | loop fusion | flops 55705600 | bytes 4956176 | tf_op jit(solution)/shard_map/jit(_where)/select_n | solution.py:40
  33.2 6.4 %select_n.2404 = bf16[1280,1280]{1,0:T(8,128)(2,1)} reshape(bf16[320,4,1280]{2,1,0:T(4,128)(2,1)} %fusion.358) | data formatting | bytes 6553600 | tf_op jit(solution)/shard_map/jit(_where)/select_n | solution.py:40
  39.9 16.3 %fusion.374 = bf16[320,4,1280]{2,1,0:T(4,128)(2,1)} fusion(s32[320,1280]{1,0:T(8,128)S(1)} %copy-done.23, s32[4]{0:T(128)S(1)} %iota_multiply_fusion, bf16[1280]{0:T(1024)(128)(2,1)S(1)} %get-tuple-element.36, bf16[1280]{0:T(1024)(128)(2,1)S(1)} %get-tuple-element.37, bf16[1280]{0:T(1024)(128)(2,1)S(1)} %get-tuple-element.38, ...), kind=kLoop, calls=%fused_computation.388 | loop fusion | flops 55705600 | bytes 4956176 | tf_op jit(solution)/shard_map/jit(_where)/select_n | solution.py:40
  56.2 6.2 %select_n.2421 = bf16[1280,1280]{1,0:T(8,128)(2,1)} reshape(bf16[320,4,1280]{2,1,0:T(4,128)(2,1)} %fusion.374) | data formatting | bytes 6553600 | tf_op jit(solution)/shard_map/jit(_where)/select_n | solution.py:40
  62.4 2.6 fusion.424
  68.0 42.2 %all-reduce = (f32[32]{0:T(128)S(1)}, f32[32]{0:T(128)S(1)}) all-reduce(f32[32]{0:T(128)S(1)} %reduce_sum.73, f32[32]{0:T(128)S(1)} %reduce_sum.70), channel_id=1, replica_groups=mesh['row'=4,'col'=8] {'row','col'}, use_global_device_ids=true, to_apply=%region_5.6 | all-reduce | flops 64 | bytes 512 | tf_op jit(solution)/shard_map/psum | solution.py:133
  110.5 10.5 %slice_bitcast_fusion = (s32[320,1280]{1,0:T(8,128)}, s32[320,1280]{1,0:T(8,128)}, s32[320,1280]{1,0:T(8,128)S(1)}, s32[320,1280]{1,0:T(8,128)}, s32[320,1280]{1...) fusion(s32[9,320,1280]{2,1,0:T(8,128)} %param.28), kind=kLoop, calls=%fused_computation.464 | loop fusion | bytes 29491200 | tf_op jit(solution)/shard_map/shift_right_arithmetic | solution.py:35
  121.8 17.6 %fusion.214 = bf16[320,4,1280]{2,1,0:T(4,128)(2,1)} fusion(s32[4]{0:T(128)S(1)} %iota_multiply_fusion, s32[320,1280]{1,0:T(8,128)} %get-tuple-element.110, bf16[1280]{0:T(1024)(128)(2,1)S(1)} %get-tuple-element.84, bf16[1280]{0:T(1024)(128)(2,1)S(1)} %get-tuple-element.85, bf16[1280]{0:T(1024)(128)(2,1)S(1)} %get-tuple-element.86, ...), kind=kLoop, calls=%fused_computation.228 | loop fusion | flops 55705600 | bytes 4956176 | tf_op jit(solution)/shard_map/jit(_where)/select_n | solution.py:40
  139.3 32.2 %fusion.342 = (bf16[320,4,1280]{2,1,0:T(4,128)(2,1)}, bf16[320,4,1280]{2,1,0:T(4,128)(2,1)}) fusion(s32[320,1280]{1,0:T(8,128)S(1)} %copy-done.16, s32[4]{0:T(128)S(1)} %iota_multiply_fusion, bf16[1280]{0:T(1024)(128)(2,1)S(1)} %get-tuple-element.84, bf16[1280]{0:T(1024)(128)(2,1)S(1)} %get-tuple-element.85, bf16[1280]{0:T(1024)(128)(2,1)S(1)} %get-tuple-element.86, ...), kind=kLoop, calls=%fused_computation.356 | loop fusion | flops 111411200 | bytes 9871376 | tf_op jit(solution)/shard_map/jit(_where)/select_n | solution.py:40
  171.6 32.2 %fusion.326 = (bf16[320,4,1280]{2,1,0:T(4,128)(2,1)}, bf16[320,4,1280]{2,1,0:T(4,128)(2,1)}) fusion(s32[320,1280]{1,0:T(8,128)S(1)} %copy-done.15, s32[4]{0:T(128)S(1)} %iota_multiply_fusion, bf16[1280]{0:T(1024)(128)(2,1)S(1)} %get-tuple-element.84, bf16[1280]{0:T(1024)(128)(2,1)S(1)} %get-tuple-element.85, bf16[1280]{0:T(1024)(128)(2,1)S(1)} %get-tuple-element.86, ...), kind=kLoop, calls=%fused_computation.340 | loop fusion | flops 111411200 | bytes 9871376 | tf_op jit(solution)/shard_map/jit(_where)/select_n | solution.py:40
  203.8 32.2 %fusion.310 = (bf16[320,4,1280]{2,1,0:T(4,128)(2,1)}, bf16[320,4,1280]{2,1,0:T(4,128)(2,1)}) fusion(s32[320,1280]{1,0:T(8,128)S(1)} %copy-done.12, s32[4]{0:T(128)S(1)} %iota_multiply_fusion, bf16[1280]{0:T(1024)(128)(2,1)S(1)} %get-tuple-element.84, bf16[1280]{0:T(1024)(128)(2,1)S(1)} %get-tuple-element.85, bf16[1280]{0:T(1024)(128)(2,1)S(1)} %get-tuple-element.86, ...), kind=kLoop, calls=%fused_computation.324 | loop fusion | flops 111411200 | bytes 9871376 | tf_op jit(solution)/shard_map/jit(_where)/select_n | solution.py:40
  236.0 32.2 %fusion.294 = (bf16[320,4,1280]{2,1,0:T(4,128)(2,1)}, bf16[320,4,1280]{2,1,0:T(4,128)(2,1)}) fusion(s32[320,1280]{1,0:T(8,128)S(1)} %get-tuple-element.105, s32[4]{0:T(128)S(1)} %iota_multiply_fusion, bf16[1280]{0:T(1024)(128)(2,1)S(1)} %get-tuple-element.84, bf16[1280]{0:T(1024)(128)(2,1)S(1)} %get-tuple-element.85, ...), kind=kLoop, calls=%fused_computation.308 | loop fusion | flops 111411200 | bytes 9871376 | tf_op jit(solution)/shard_map/jit(_where)/select_n | solution.py:40
  268.3 1.3 fusion.443
  269.6 16.5 %fusion.390 = bf16[320,4,1280]{2,1,0:T(4,128)(2,1)} fusion(s32[320,1280]{1,0:T(8,128)S(1)} %copy-done.24, s32[4]{0:T(128)S(1)} %iota_multiply_fusion, bf16[1280]{0:T(1024)(128)(2,1)S(1)} %get-tuple-element.68, bf16[1280]{0:T(1024)(128)(2,1)S(1)} %get-tuple-element.69, bf16[1280]{0:T(1024)(128)(2,1)S(1)} %get-tuple-element.70, ...), kind=kLoop, calls=%fused_computation.404 | loop fusion | flops 55705600 | bytes 4956176 | tf_op jit(solution)/shard_map/jit(_where)/select_n | solution.py:40
  286.1 16.3 %fusion.406 = bf16[320,4,1280]{2,1,0:T(4,128)(2,1)} fusion(s32[320,1280]{1,0:T(8,128)S(1)} %copy-done.25, s32[4]{0:T(128)S(1)} %iota_multiply_fusion, bf16[1280]{0:T(1024)(128)(2,1)S(1)} %get-tuple-element.20, bf16[1280]{0:T(1024)(128)(2,1)S(1)} %get-tuple-element.21, bf16[1280]{0:T(1024)(128)(2,1)S(1)} %get-tuple-element.22, ...), kind=kLoop, calls=%fused_computation.420 | loop fusion | flops 55705600 | bytes 4956176 | tf_op jit(solution)/shard_map/jit(_where)/select_n | solution.py:40
  302.9 1.3 collective-permute-start.3
  304.2 3.0 collective-permute-start.2
  307.2 6.3 %select_n.2251 = bf16[1280,1280]{1,0:T(8,128)(2,1)} reshape(bf16[320,4,1280]{2,1,0:T(4,128)(2,1)} %fusion.214) | data formatting | bytes 6553600 | tf_op jit(solution)/shard_map/jit(_where)/select_n | solution.py:40
  313.5 6.2 %select_n.2268 = bf16[1280,1280]{1,0:T(8,128)(2,1)} reshape(bf16[320,4,1280]{2,1,0:T(4,128)(2,1)} %get-tuple-element.127) | data formatting | bytes 6553600 | tf_op jit(solution)/shard_map/jit(_where)/select_n | solution.py:40
  319.7 6.2 %select_n.2285 = bf16[1280,1280]{1,0:T(8,128)(2,1)} reshape(bf16[320,4,1280]{2,1,0:T(4,128)(2,1)} %get-tuple-element.129) | data formatting | bytes 6553600 | tf_op jit(solution)/shard_map/jit(_where)/select_n | solution.py:40
  326.0 6.3 %select_n.2302 = bf16[1280,1280]{1,0:T(8,128)(2,1)} reshape(bf16[320,4,1280]{2,1,0:T(4,128)(2,1)} %get-tuple-element.131) | data formatting | bytes 6553600 | tf_op jit(solution)/shard_map/jit(_where)/select_n | solution.py:40
  332.2 6.2 %select_n.2319 = bf16[1280,1280]{1,0:T(8,128)(2,1)} reshape(bf16[320,4,1280]{2,1,0:T(4,128)(2,1)} %get-tuple-element.133) | data formatting | bytes 6553600 | tf_op jit(solution)/shard_map/jit(_where)/select_n | solution.py:40
  338.5 6.2 %select_n.2336 = bf16[1280,1280]{1,0:T(8,128)(2,1)} reshape(bf16[320,4,1280]{2,1,0:T(4,128)(2,1)} %get-tuple-element.132) | data formatting | bytes 6553600 | tf_op jit(solution)/shard_map/jit(_where)/select_n | solution.py:40
  344.7 6.2 %select_n.2353 = bf16[1280,1280]{1,0:T(8,128)(2,1)} reshape(bf16[320,4,1280]{2,1,0:T(4,128)(2,1)} %get-tuple-element.130) | data formatting | bytes 6553600 | tf_op jit(solution)/shard_map/jit(_where)/select_n | solution.py:40
  351.0 6.2 %select_n.2370 = bf16[1280,1280]{1,0:T(8,128)(2,1)} reshape(bf16[320,4,1280]{2,1,0:T(4,128)(2,1)} %get-tuple-element.128) | data formatting | bytes 6553600 | tf_op jit(solution)/shard_map/jit(_where)/select_n | solution.py:40
  357.2 6.3 %select_n.2387 = bf16[1280,1280]{1,0:T(8,128)(2,1)} reshape(bf16[320,4,1280]{2,1,0:T(4,128)(2,1)} %get-tuple-element.126) | data formatting | bytes 6553600 | tf_op jit(solution)/shard_map/jit(_where)/select_n | solution.py:40
  363.4 6.2 %select_n.2438 = bf16[1280,1280]{1,0:T(8,128)(2,1)} reshape(bf16[320,4,1280]{2,1,0:T(4,128)(2,1)} %fusion.390) | data formatting | bytes 6553600 | tf_op jit(solution)/shard_map/jit(_where)/select_n | solution.py:40
  369.7 6.3 %select_n.2455 = bf16[1280,1280]{1,0:T(8,128)(2,1)} reshape(bf16[320,4,1280]{2,1,0:T(4,128)(2,1)} %fusion.406) | data formatting | bytes 6553600 | tf_op jit(solution)/shard_map/jit(_where)/select_n | solution.py:40
  376.0 1.6 pad_maximum_fusion
  377.6 2.5 scatter.4
  380.7 1.4 copy-done.22
  385.1 1.0 convolution_add_fusion.7
  387.0 1.0 convolution_add_fusion.6
  394.8 1.0 convolution_add_fusion.2
  396.7 1.0 convolution_add_fusion.1
  400.9 2.9 convolution_convert_fusion
  404.1 2.9 convolution_convert_fusion.2
  407.1 1.1 copy.30
  408.2 3.4 fusion.457
  411.5 1.8 copy.34
  413.4 7.7 %fusion.428 = f32[20,256,768]{2,1,0:T(8,128)} fusion(bf16[256,20,64]{0,2,1:T(8,128)(2,1)S(1)} %bitcast.89, bf16[512,20,64]{0,2,1:T(8,128)(2,1)S(1)} %bitcast.80, bf16[256,20,64]{0,2,1:T(8,128)(2,1)S(1)} %bitcast.90), kind=kOutput, calls=%fused_computation.460 | convolution fusion | flops 507248640 | bytes 18350080 | tf_op jit(solution)/shard_map/qhd,khd->hqk/dot_general | solution.py:98
  421.1 13.4 %fusion.461 = f32[20,256]{1,0:T(8,128)S(1)} fusion(f32[20,256,768]{2,1,0:T(8,128)} %fusion.428), kind=kOutput, calls=%fused_computation.594 | output fusion | flops 15729407 | bytes 15749120 | tf_op jit(solution)/shard_map/sub | solution.py:102
  434.6 1.5 copy.31
  436.1 19.6 %fusion.432 = bf16[20,64,256]{2,1,0:T(8,128)(2,1)S(1)} fusion(f32[20,256]{1,0:T(8,128)S(1)} %fusion.461, bf16[512,20,64]{0,2,1:T(8,128)(2,1)} %bitcast.91, bf16[256,20,64]{0,2,1:T(8,128)(2,1)S(1)} %bitcast.93, f32[20,256,768]{2,1,0:T(8,128)} %fusion.428), kind=kOutput, calls=%fused_computation.473 | convolution fusion | flops 527243008 | bytes 18370560 | tf_op jit(solution)/shard_map/hqk,khd->qhd/dot_general | solution.py:104
  455.7 3.8 fusion.422
  (132 shorter events, 20.9 us)
Async XLA Ops:
  6.5 295.8 %copy-start = (bf16[320,1280]{1,0:T(8,128)(2,1)S(1)}, bf16[320,1280]{1,0:T(8,128)(2,1)}, u32[]{:S(2)}) copy-start(bf16[320,1280]{1,0:T(8,128)(2,1)} %param.25) | copy-start | bytes 2457604
  6.5 9.1 %copy-start.29 = (f32[16,1280]{1,0:T(8,128)S(1)}, f32[16,1280]{1,0:T(8,128)}, u32[]{:S(2)}) copy-start(f32[16,1280]{1,0:T(8,128)} %param.37) | copy-start | bytes 245764
  6.5 401.6 %all-gather.2.cloned.1.call-start = ((), (), s32[]{:S(2)}) async-start(), calls=%async_computation | async-start | bytes 2703360 | tf_op jit(solution)/shard_map/all_gather | solution.py:151
  7.4 295.2 %collective-permute-start = (bf16[1,16,1280]{2,1,0:T(8,128)(2,1)S(1)}, bf16[1,16,1280]{2,1,0:T(8,128)(2,1)S(1)}, u32[]{:S(2)}, u32[]{:S(2)}) collective-permute-start(bf16[1,16,1280]{2,1,0:T(8,128)(2,1)S(1)} %get-tuple-element.125), channel_id=1, source_target_pairs={{0,8},{8,16},{16,24},{1,9},{9,17},{17,25},{2,10},{10,18},{18,26},{... | collective-permute-start | bytes 122888 | tf_op jit(solution)/shard_map/ppermute | solution.py:23
  12.3 290.4 %collective-permute-start.1 = (bf16[1,16,1280]{2,1,0:T(8,128)(2,1)S(1)}, bf16[1,16,1280]{2,1,0:T(8,128)(2,1)S(1)}, u32[]{:S(2)}, u32[]{:S(2)}) collective-permute-start(bf16[1,16,1280]{2,1,0:T(8,128)(2,1)S(1)} %get-tuple-element.124), channel_id=1, source_target_pairs={{8,0},{16,8},{24,16},{9,1},{17,9},{25,17},{10,2},{18,10},{26,18},{... | collective-permute-start | bytes 122888 | tf_op jit(solution)/shard_map/ppermute | solution.py:25
  33.2 6.4 %copy-start.30 = (f32[16,1280]{1,0:T(8,128)S(1)}, f32[16,1280]{1,0:T(8,128)}, u32[]{:S(2)}) copy-start(f32[16,1280]{1,0:T(8,128)} %param.35) | copy-start | bytes 245764
  33.2 6.6 %copy-start.23 = (s32[320,1280]{1,0:T(8,128)S(1)}, s32[320,1280]{1,0:T(8,128)}, u32[]{:S(2)}) copy-start(s32[320,1280]{1,0:T(8,128)} %param.34) | copy-start | bytes 4915204
  62.4 2.9 copy-start.2
  62.4 4.8 %copy-start.18 = (bf16[16,16,1280]{2,1,0:T(8,128)(2,1)S(1)}, bf16[16,16,1280]{2,1,0:T(8,128)(2,1)}, u32[]{:S(2)}) copy-start(bf16[16,16,1280]{2,1,0:T(8,128)(2,1)} %param.21) | copy-start | bytes 1966084
  110.5 10.5 %copy-start.31 = (f32[16,1280]{1,0:T(8,128)S(1)}, f32[16,1280]{1,0:T(8,128)}, u32[]{:S(2)}) copy-start(f32[16,1280]{1,0:T(8,128)} %param.29) | copy-start | bytes 245764
  110.5 10.7 %copy-start.32 = (f32[16,1280]{1,0:T(8,128)S(1)}, f32[16,1280]{1,0:T(8,128)}, u32[]{:S(2)}) copy-start(f32[16,1280]{1,0:T(8,128)} %param.33) | copy-start | bytes 245764
  110.5 11.0 %copy-start.33 = (f32[16,1280]{1,0:T(8,128)S(1)}, f32[16,1280]{1,0:T(8,128)}, u32[]{:S(2)}) copy-start(f32[16,1280]{1,0:T(8,128)} %param.39) | copy-start | bytes 245764
  121.0 18.3 %copy-start.16 = (s32[320,1280]{1,0:T(8,128)S(1)}, s32[320,1280]{1,0:T(8,128)}, u32[]{:S(2)}) copy-start(s32[320,1280]{1,0:T(8,128)} %get-tuple-element.103) | copy-start | bytes 4915204
  121.0 18.3 %copy-start.17 = (s32[320,1280]{1,0:T(8,128)S(1)}, s32[320,1280]{1,0:T(8,128)}, u32[]{:S(2)}) copy-start(s32[320,1280]{1,0:T(8,128)} %get-tuple-element.109) | copy-start | bytes 4915204
  139.3 32.2 %copy-start.14 = (s32[320,1280]{1,0:T(8,128)S(1)}, s32[320,1280]{1,0:T(8,128)}, u32[]{:S(2)}) copy-start(s32[320,1280]{1,0:T(8,128)} %get-tuple-element.108) | copy-start | bytes 4915204
  139.3 32.2 %copy-start.15 = (s32[320,1280]{1,0:T(8,128)S(1)}, s32[320,1280]{1,0:T(8,128)}, u32[]{:S(2)}) copy-start(s32[320,1280]{1,0:T(8,128)} %get-tuple-element.111) | copy-start | bytes 4915204
  171.6 32.2 %copy-start.12 = (s32[320,1280]{1,0:T(8,128)S(1)}, s32[320,1280]{1,0:T(8,128)}, u32[]{:S(2)}) copy-start(s32[320,1280]{1,0:T(8,128)} %get-tuple-element.104) | copy-start | bytes 4915204
  171.6 32.2 %copy-start.13 = (s32[320,1280]{1,0:T(8,128)S(1)}, s32[320,1280]{1,0:T(8,128)}, u32[]{:S(2)}) copy-start(s32[320,1280]{1,0:T(8,128)} %get-tuple-element.107) | copy-start | bytes 4915204
  203.8 32.2 %copy-start.11 = (s32[320,1280]{1,0:T(8,128)S(1)}, s32[320,1280]{1,0:T(8,128)}, u32[]{:S(2)}) copy-start(s32[320,1280]{1,0:T(8,128)} %get-tuple-element.106) | copy-start | bytes 4915204
  236.0 32.3 %copy-start.34 = (f32[1280]{0:T(1024)S(1)}, f32[1280]{0:T(1024)}, u32[]{:S(2)}) copy-start(f32[1280]{0:T(1024)} %param.27) | copy-start | bytes 15364
  236.0 32.3 %copy-start.35 = (f32[1280]{0:T(1024)S(1)}, f32[1280]{0:T(1024)}, u32[]{:S(2)}) copy-start(f32[1280]{0:T(1024)} %param.26) | copy-start | bytes 15364
  236.0 33.6 %copy-start.24 = (s32[320,1280]{1,0:T(8,128)S(1)}, s32[320,1280]{1,0:T(8,128)}, u32[]{:S(2)}) copy-start(s32[320,1280]{1,0:T(8,128)} %param.32) | copy-start | bytes 4915204
  268.3 17.8 %copy-start.25 = (s32[320,1280]{1,0:T(8,128)S(1)}, s32[320,1280]{1,0:T(8,128)}, u32[]{:S(2)}) copy-start(s32[320,1280]{1,0:T(8,128)} %param.38) | copy-start | bytes 4915204
  286.1 16.6 %copy-start.27 = (bf16[16,16,1280]{2,1,0:T(8,128)(2,1)S(1)}, bf16[16,16,1280]{2,1,0:T(8,128)(2,1)}, u32[]{:S(2)}) copy-start(bf16[16,16,1280]{2,1,0:T(8,128)(2,1)} %param.22) | copy-start | bytes 1966084
  302.7 10.8 %copy-start.26 = (bf16[18,16,1280]{2,1,0:T(8,128)(2,1)}, bf16[18,16,1280]{2,1,0:T(8,128)(2,1)S(1)}, u32[]{:S(2)}) copy-start(bf16[18,16,1280]{2,1,0:T(8,128)(2,1)S(1)} %constant_dynamic-update-slice_fusion) | copy-start | bytes 2211844
  302.9 73.1 %collective-permute-start.3 = (bf16[18,1,1280]{2,1,0:T(2,128)(2,1)S(1)}, bf16[18,1,1280]{2,1,0:T(2,128)(2,1)S(1)}, u32[]{:S(2)}, u32[]{:S(2)}) collective-permute-start(bf16[18,1,1280]{2,1,0:T(2,128)(2,1)S(1)} %get-tuple-element.123), channel_id=1, source_target_pairs={{1,0},{2,1},{3,2},{4,3},{5,4},{6,5},{7,6},{9,8},{10,9},{11,10},{12... | collective-permute-start | bytes 138248 | tf_op jit(solution)/shard_map/ppermute | solution.py:25
  304.2 71.8 %collective-permute-start.2 = (bf16[18,1,1280]{2,1,0:T(2,128)(2,1)S(1)}, bf16[18,1,1280]{2,1,0:T(2,128)(2,1)S(1)}, u32[]{:S(2)}, u32[]{:S(2)}) collective-permute-start(bf16[18,1,1280]{2,1,0:T(2,128)(2,1)S(1)} %get-tuple-element.122), channel_id=1, source_target_pairs={{0,1},{1,2},{2,3},{3,4},{4,5},{5,6},{6,7},{8,9},{9,10},{10,11},{11... | collective-permute-start | bytes 138248 | tf_op jit(solution)/shard_map/ppermute | solution.py:23
  369.7 7.9 %copy-start.19 = (bf16[16,16,1280]{2,1,0:T(8,128)(2,1)S(1)}, bf16[16,16,1280]{2,1,0:T(8,128)(2,1)}, u32[]{:S(2)}) copy-start(bf16[16,16,1280]{2,1,0:T(8,128)(2,1)} %fusion.443) | copy-start | bytes 1966084
  380.1 1.9 copy-start.22
  380.6 2.5 copy-start.10
  383.2 1.9 copy-start.9
  385.1 1.9 copy-start.8
  387.0 1.9 copy-start.6
  389.0 1.9 copy-start.7
  390.9 1.9 copy-start.5
  392.8 1.9 copy-start.4
  394.7 1.9 copy-start.3
  396.7 1.1 copy-start.36
  397.7 0.7 copy-start.37
  397.7 1.9 copy-start.21
  421.1 13.4 %copy-start.20 = (bf16[1,512,1280]{2,1,0:T(8,128)(2,1)S(1)}, bf16[1,512,1280]{2,1,0:T(8,128)(2,1)}, u32[]{:S(2)}) copy-start(bf16[1,512,1280]{2,1,0:T(8,128)(2,1)} %get-tuple-element.112) | copy-start | bytes 3932164
  421.1 14.9 %copy-start.28 = (bf16[256,1280]{0,1:T(8,128)(2,1)S(1)}, bf16[256,1280]{0,1:T(8,128)(2,1)}, u32[]{:S(2)}) copy-start(bf16[256,1280]{0,1:T(8,128)(2,1)} %copy.30) | copy-start | bytes 1966084
  436.0 23.5 %copy-start.1 = (bf16[320,1280]{1,0:T(8,128)(2,1)S(1)}, bf16[320,1280]{1,0:T(8,128)(2,1)}, u32[]{:S(2)}) copy-start(bf16[320,1280]{1,0:T(8,128)(2,1)} %param.25) | copy-start | bytes 2457604
Sparse Core Ops, SparseCore 0:
  66.7 60.4 all-gather.1
where the time goes:
time: 476 us; the launch traced here: 467 us
  other arithmetic  232 us (49%)
  local copies, waits for them, and re-layouts  117 us (25%)
  matrix products  50.7 us (11%)
  blocking collectives  42.2 us (9%)
  between operations  15.2 us (3%)
  starting transfers between devices  10.5 us (2%)
    select_n x9, other arithmetic, unpack_weight(): weight = jnp.where(nibbles == code_value, levels[code_value], weight)  213 us
    select_n x13, local copies, waits for them, and re-layouts, unpack_weight(): weight = jnp.where(nibbles == code_value, levels[code_value], weight)  81.4 us
    psum x1, blocking collectives, on_device(): sums_first = lax.psum(group_terms(current), ('row', 'col'))  42.2 us
    dot_general x1, matrix products, attend(): jnp.einsum('hqk,khd->qhd', weights, value_heads, preferred_element_type=j...  19.6 us
    sub x1, other arithmetic, attend(): exponent = jnp.exp(scores - highest)  13.4 us
    shift_right_arithmetic x1, local copies, waits for them, and re-layouts, unpack_weight(): nibbles = jnp.right_shift(packed[..., :, None, :], shifts[:, None]) & 15  10.5 us
    dot_general x5, matrix products, project(): jnp.dot(inputs, weight, preferred_element_type=jnp.float32)  10.1 us
  transfers between devices with their start and end apart: 5, of which 0 were waited for; matrix products, arithmetic and copies ran while one was open for 72% of the time, Pallas kernels for 0%

commit v1 on v0

v1 whole, which is shorter than its diff:
```python
import functools
import math

import jax
import jax.numpy as jnp
from jax import lax
from jax.experimental import pallas as pl
from jax.experimental.pallas import tpu as pltpu
from jax.sharding import PartitionSpec as P

HEAD_DIM = 64
GROUPS = 32
TEMB = 320
POOL = 4
LANES = 128
BF = jnp.bfloat16
F32 = jnp.float32
VMEM_LIMIT = 56 * 2**20


def params(**extra):
    return pltpu.CompilerParams(vmem_limit_bytes=VMEM_LIMIT, **extra)


def dot(a, b, **extra):
    return jnp.dot(a, b, preferred_element_type=F32, **extra)


def dot_t(a, b):
    return lax.dot_general(a, b, (((1,), (1,)), ((), ())), preferred_element_type=F32)


def iota(shape, dim):
    return lax.broadcasted_iota(jnp.int32, shape, dim)


def shuffle_matrix(words):
    size = 4 * words
    row = iota((size, size), 0)
    col = iota((size, size), 1)
    return (row == 4 * (col % words) + col // words).astype(F32).astype(BF)


def shuffle(values, words):
    size = 4 * words
    matrix = shuffle_matrix(words)
    return jnp.concatenate(
        [dot(values[:, k : k + size], matrix) for k in range(0, values.shape[1], size)], axis=1
    )


def group_matrix(channels, transposed):
    members = channels // GROUPS
    shape = (LANES, channels) if transposed else (channels, LANES)
    channel = iota(shape, 1 if transposed else 0)
    group = iota(shape, 0 if transposed else 1)
    return ((channel >= group * members) & (channel < (group + 1) * members)).astype(F32)


def first_kernel(core_ref, step_ref, image_ref, first_ref, normed_ref, time_ref, sums_ref, edge_ref, pool_ref, shift_ref):
    channels = image_ref.shape[-1]
    height, across = first_ref.shape[:2]
    cells = height * across
    core = core_ref[0]
    image = image_ref[...].reshape(cells, channels).astype(F32)
    sums = jnp.sum(image, axis=0, keepdims=True)
    squares = jnp.sum(image * image, axis=0, keepdims=True)
    row8 = iota((8, channels), 0)
    both = jnp.where(row8 == 0, sums, jnp.where(row8 == 1, squares, 0.0))
    sums_ref[...] = dot(both, group_matrix(channels, False), precision=lax.Precision.HIGHEST)

    cells_first = first_ref[...].reshape(cells, channels)
    row = iota((height, cells), 0)
    cell = iota((height, cells), 1)
    outer = jnp.where(core == 0, 0, across - 1)
    pick_outer = (cell == row * across + outer).astype(F32).astype(BF)
    pick_inner = (cell == row * across + (across - 1 - outer)).astype(F32).astype(BF)
    edge_ref[0] = dot(pick_outer, cells_first).astype(BF)
    edge_ref[1] = dot(pick_inner, cells_first).astype(BF)
    edge_ref[2] = first_ref[0]
    edge_ref[3] = first_ref[height - 1]

    pools = pool_ref.shape[0]
    pool = iota((pools, cells), 0)
    cell = iota((pools, cells), 1)
    in_row = cell // across // POOL == pool // (across // POOL)
    in_col = cell % across // POOL == pool % (across // POOL)
    average = jnp.where(in_row & in_col, 1.0 / (POOL * POOL), 0.0).astype(BF)
    pooled = dot(average, normed_ref[...].reshape(cells, channels)).astype(BF)
    pool_ref[...] = shuffle(pooled, 64).astype(BF)

    half = TEMB // 2
    place = iota((8, TEMB), 1)
    index = jnp.where(place < half, place, place - half).astype(F32)
    frequency = jnp.exp(-math.log(10000.0) * index / half)
    angle = step_ref[0].astype(F32) * frequency
    sinusoid = jnp.where(place < half, jnp.cos(angle), jnp.sin(angle)).astype(BF)
    shift = dot(sinusoid, time_ref[...])
    shift_ref[...] = shift * jax.nn.sigmoid(shift)


def first_pass(core, timestep, image, stale_first, stale_normed, time_weight):
    height, across, channels = image.shape
    pools = (height // POOL) * (across // POOL)
    whole = pl.BlockSpec(memory_space=pltpu.VMEM)
    small = pl.BlockSpec(memory_space=pltpu.SMEM)
    return pl.pallas_call(
        first_kernel,
        in_specs=[small, small] + [whole] * 4,
        out_specs=[whole] * 4,
        out_shape=[
            jax.ShapeDtypeStruct((8, LANES), F32),
            jax.ShapeDtypeStruct((4, height, channels), BF),
            jax.ShapeDtypeStruct((pools, channels), BF),
            jax.ShapeDtypeStruct((8, channels), F32),
        ],
        compiler_params=params(),
    )(core, timestep, image, stale_first, stale_normed, time_weight)


def decode_tile(words, words16, low, high, place):
    lows = []
    highs = []
    for k in range(0, words.shape[0], 8):
        index = words[k : k + 8]
        if place:
            index = index >> (4 * place)
        index = index & 7
        lows.append(jnp.take_along_axis(low, index, axis=0, mode="promise_in_bounds"))
        highs.append(jnp.take_along_axis(high, index, axis=0, mode="promise_in_bounds"))
    bit = 4 * place + 3
    upper = (words16 & jnp.int16(1 << bit if bit < 15 else -(1 << 15))) != 0
    return jnp.where(
        upper, jnp.concatenate(highs, axis=0).astype(BF), jnp.concatenate(lows, axis=0).astype(BF)
    )


def decode_kernel(core_ref, *refs, count, block):
    for k in range(count):
        codes_ref, table_ref, weight_ref = refs[2 * k], refs[2 * k + 1], refs[2 * count + k]
        decode_into(codes_ref, table_ref, weight_ref, block)


def decode_into(codes_ref, table_ref, weight_ref, block):
    words_all, columns = codes_ref.shape[-2:]
    lead = (0,) * (len(codes_ref.shape) - 2)
    for c in range(columns // LANES):
        lanes = pl.ds(c * LANES, LANES)
        low = table_ref[0:8, lanes]
        high = table_ref[8:16, lanes]
        for g in range(words_all // block):
            words = codes_ref[lead + (pl.ds(g * block, block), lanes)]
            words16 = words.astype(jnp.int16)
            for place in range(4):
                weight_ref[lead + (pl.ds((4 * g + place) * block, block), lanes)] = decode_tile(
                    words, words16, low, high, place
                )


def decode_cost(weights):
    return pl.CostEstimate(flops=8 * weights, bytes_accessed=3 * weights, transcendentals=0)


def decode_taps(core, codes, table, start, stop):
    words, channels = codes.shape[1:]
    half = channels // 2
    return pl.pallas_call(
        functools.partial(decode_kernel, count=1, block=64),
        grid_spec=pltpu.PrefetchScalarGridSpec(
            num_scalar_prefetch=1,
            grid=(stop - start,),
            in_specs=[
                pl.BlockSpec((1, words, half), lambda t, c: (start + t, 0, c[0])),
                pl.BlockSpec((16, half), lambda t, c: (0, c[0])),
            ],
            out_specs=[pl.BlockSpec((1, 4 * words, half), lambda t, c: (t, 0, 0))],
        ),
        out_shape=[jax.ShapeDtypeStruct((stop - start, 4 * words, half), BF)],
        compiler_params=params(),
        cost_estimate=decode_cost((stop - start) * 4 * words * half),
    )(core, codes, table)[0]


def decode_columns(core, *pairs):
    count = len(pairs) // 2
    words, channels = pairs[0].shape
    half = channels // 2
    return pl.pallas_call(
        functools.partial(decode_kernel, count=count, block=64),
        grid_spec=pltpu.PrefetchScalarGridSpec(
            num_scalar_prefetch=1,
            grid=(1,),
            in_specs=[
                pl.BlockSpec((words, half), lambda t, c: (0, c[0])),
                pl.BlockSpec((16, half), lambda t, c: (0, c[0])),
            ]
            * count,
            out_specs=[pl.BlockSpec((4 * words, half), lambda t, c: (0, 0))] * count,
        ),
        out_shape=[jax.ShapeDtypeStruct((4 * words, half), BF)] * count,
        compiler_params=params(),
        cost_estimate=decode_cost(count * 4 * words * half),
    )(core, *pairs)


def decode_rows(core, codes, table):
    words, channels = codes.shape
    half = words // 2
    return pl.pallas_call(
        functools.partial(decode_kernel, count=1, block=32),
        grid_spec=pltpu.PrefetchScalarGridSpec(
            num_scalar_prefetch=1,
            grid=(1,),
            in_specs=[
                pl.BlockSpec((half, channels), lambda t, c: (c[0], 0)),
                pl.BlockSpec((16, channels), lambda t, c: (0, 0)),
            ],
            out_specs=[pl.BlockSpec((4 * half, channels), lambda t, c: (0, 0))],
        ),
        out_shape=[jax.ShapeDtypeStruct((4 * half, channels), BF)],
        compiler_params=params(),
        cost_estimate=decode_cost(4 * half * channels),
    )(core, codes, table)[0]


def conv_kernel(
    core_ref, sums_ref, mine_ref, theirs_ref, rim_mine_ref, rim_theirs_ref, gain_ref, shift_ref, bias_ref, time_ref,
    half_mine_ref, half_theirs_ref, weight_ref, out_ref, act_ref, rim_ref, padded_ref, total_ref, *, members, split,
):
    tap = pl.program_id(0)
    taps = pl.num_programs(0)
    channels = gain_ref.shape[-1]
    height, across = mine_ref.shape[:2]
    cells = height * across
    core = core_ref[0]

    @pl.when(tap == 0)
    def _():
        spread = dot(sums_ref[...], group_matrix(channels, True), precision=lax.Precision.HIGHEST)
        average = spread[0:1] / members
        mean_square = spread[1:2] / members
        scale = lax.rsqrt(mean_square - average * average + 1e-05) * gain_ref[...]
        offset = shift_ref[...] - average * scale
        size = 256
        matrix = shuffle_matrix(64)
        for side, ref in enumerate((mine_ref, theirs_ref)):
            for k in range(0, channels, size):
                lanes = slice(k, k + size)
                value = ref[:, :, lanes].reshape(cells, size).astype(F32)
                value = value * scale[:, lanes] + offset[:, lanes]
                value = (0.5 * value) * (1.0 + jnp.tanh(0.5 * value))
                act_ref[side, :, lanes] = dot(value.astype(BF), matrix)
        for side, ref in enumerate((rim_mine_ref, rim_theirs_ref)):
            for k in range(0, channels, size):
                lanes = slice(k, k + size)
                rim_ref[side, :, lanes] = dot(ref[:, lanes], matrix)

        column = iota((across, channels), 0)

        def spread_row(side, line, value, left, right):
            padded_ref[side, 0, line] = jnp.where(column == 0, left, pltpu.roll(value, 1, 0)).astype(BF)
            padded_ref[side, 1, line] = value.astype(BF)
            padded_ref[side, 2, line] = jnp.where(
                column == across - 1, right, pltpu.roll(value, across - 1, 0)
            ).astype(BF)

        for side in range(2):
            other = 1 - side
            is_left = core == side
            for line, base in ((0, 0), (height + 1, 2 * across)):
                corner = across + (height - 1 if line == 0 else 0)
                far = rim_ref[side, base + corner : base + corner + 1]
                next_last = rim_ref[other, base + across - 1 : base + across]
                next_first = rim_ref[other, base : base + 1]
                value = rim_ref[side, base : base + across]
                spread_row(
                    side, line, value, jnp.where(is_left, far, next_last), jnp.where(is_left, next_first, far)
                )
            outer_at = 4 * across
            inner_at = 4 * across + height

            @pl.loop(0, height)
            def _(r):
                outer = rim_ref[side, pl.ds(outer_at + r, 1)]
                inner = rim_ref[other, pl.ds(inner_at + r, 1)]
                value = act_ref[side, pl.ds(pl.multiple_of(r * across, across), across)]
                spread_row(
                    side, r + 1, value, jnp.where(is_left, outer, inner), jnp.where(is_left, inner, outer)
                )

    row_start = tap // 3
    col_start = tap % 3
    source = padded_ref[:, col_start, pl.ds(row_start, height)].reshape(2 * cells, channels)
    part = dot(source, weight_ref[0])

    @pl.when(tap == 0)
    def _():
        total_ref[...] = part

    @pl.when((tap > 0) & (tap < taps - 1))
    def _():
        total_ref[...] += part

    @pl.when(tap == taps - 1)
    def _():
        extra = bias_ref[...] + time_ref[0:1]
        for side, ref in enumerate((half_mine_ref, half_theirs_ref)):
            image = ref[...].reshape(cells, -1).astype(F32)
            rows = slice(side * cells, (side + 1) * cells)
            conv = total_ref[rows] + part[rows] + extra
            out_ref[rows] = (image + conv).astype(BF)


def convolve(core, sums, mine, theirs, rim_mine, rim_theirs, gain, shift, bias, time_shift, weights, members):
    height, across, channels = mine.shape
    cells = height * across
    half = channels // 2
    whole = lambda *shape: pl.BlockSpec(shape, lambda t, c: (0,) * len(shape))
    part = lambda *shape: pl.BlockSpec(shape, lambda t, c: (0,) * (len(shape) - 1) + (c[0],))
    rim_rows = rim_mine.shape[0]
    return pl.pallas_call(
        functools.partial(conv_kernel, members=members, split=0),
        grid_spec=pltpu.PrefetchScalarGridSpec(
            num_scalar_prefetch=1,
            grid=(9,),
            in_specs=[
                whole(8, LANES),
                whole(height, across, channels),
                whole(height, across, channels),
                whole(rim_rows, channels),
                whole(rim_rows, channels),
                whole(1, channels),
                whole(1, channels),
                part(1, half),
                part(8, half),
                part(height, across, half),
                part(height, across, half),
                pl.BlockSpec((1, channels, half), lambda t, c: (t, 0, 0)),
            ],
            out_specs=whole(2 * cells, half),
            scratch_shapes=[
                pltpu.VMEM((2, cells, channels), F32),
                pltpu.VMEM((2, rim_rows, channels), F32),
                pltpu.VMEM((2, 3, height + 2, across, channels), BF),
                pltpu.VMEM((2 * cells, half), F32),
            ],
        ),
        out_shape=jax.ShapeDtypeStruct((2 * cells, half), BF),
        compiler_params=params(),
    )(core, sums, mine, theirs, rim_mine, rim_theirs, gain, shift, bias, time_shift, mine, theirs, weights)


def stale_kernel(near_ref, far_ref, key_ref, value_ref, keys_ref, values_ref):
    rows = near_ref.shape[0]
    for at, ref in ((0, near_ref), (rows, far_ref)):
        keys_ref[at : at + rows] = dot(ref[...], key_ref[...]).astype(BF)
        values_ref[at : at + rows] = dot(ref[...], value_ref[...]).astype(BF)


def stale_pass(near, far, key_weight, value_weight):
    rows, channels = near.shape
    half = key_weight.shape[1]
    whole = pl.BlockSpec(memory_space=pltpu.VMEM)
    return pl.pallas_call(
        stale_kernel,
        in_specs=[whole] * 4,
        out_specs=[whole] * 2,
        out_shape=[jax.ShapeDtypeStruct((2 * rows, half), BF)] * 2,
        compiler_params=params(),
        cost_estimate=pl.CostEstimate(
            flops=8 * rows * channels * half, bytes_accessed=4 * channels * half, transcendentals=0
        ),
    )(near, far, key_weight, value_weight)


def attention_kernel(
    core_ref, mine_ref, theirs_ref, gain_ref, query_ref, key_ref, value_ref, stale_keys_ref, stale_values_ref,
    out_weight_ref, partial_ref, rest_ref, normed_ref, q_ref, k_ref, v_ref, mixed_ref,
):
    rows, half = mine_ref.shape
    cells = rows // 2
    channels = 2 * half
    first = core_ref[0] == 0
    matrix = shuffle_matrix(64)
    for side in range(2):
        own = mine_ref[side * cells : (side + 1) * cells].astype(F32)
        other = theirs_ref[(1 - side) * cells : (2 - side) * cells].astype(F32)
        low = jnp.where(first, own, other)
        high = jnp.where(first, other, own)
        residual = jnp.concatenate([low, high], axis=1)
        if side == 0:
            rest_ref[...] = residual.astype(BF)
        average = jnp.sum(residual, axis=1, keepdims=True) / channels
        centred = residual - average
        deviation = jnp.sum(centred * centred, axis=1, keepdims=True) / channels
        normed = (centred * lax.rsqrt(deviation + 1e-05) * gain_ref[...]).astype(BF)
        for k in range(0, channels, 256):
            normed_ref[side * cells : (side + 1) * cells, k : k + 256] = dot(
                normed[:, k : k + 256], matrix
            ).astype(BF)
    normed = normed_ref[...]
    q_ref[...] = (dot(normed, query_ref[...]).astype(BF) * BF(1.0 / math.sqrt(HEAD_DIM))).astype(BF)
    k_ref[...] = dot(normed, key_ref[...]).astype(BF)
    v_ref[...] = dot(normed, value_ref[...]).astype(BF)

    ones = jnp.ones((cells, LANES), BF)
    stale_ones = jnp.ones((stale_keys_ref.shape[0], LANES), BF)
    lane = iota((cells, LANES), 1)
    for side in range(2):
        at = slice(side * cells, (side + 1) * cells)
        for pair in range(half // LANES):
            lanes = slice(pair * LANES, (pair + 1) * LANES)
            q = q_ref[at, lanes]
            zero = jnp.zeros_like(q)
            stacked = jnp.concatenate(
                [jnp.where(lane < HEAD_DIM, q, zero), jnp.where(lane < HEAD_DIM, zero, q)], axis=0
            )
            fresh = dot_t(stacked, k_ref[at, lanes])
            stale = dot_t(stacked, stale_keys_ref[:, lanes])
            highest = jnp.maximum(
                jnp.max(fresh, axis=1, keepdims=True), jnp.max(stale, axis=1, keepdims=True)
            )
            fresh = jnp.exp(fresh - highest).astype(BF)
            stale = jnp.exp(stale - highest).astype(BF)
            mixed = dot(fresh, jnp.concatenate([v_ref[at, lanes], ones], axis=1))
            mixed += dot(stale, jnp.concatenate([stale_values_ref[:, lanes], stale_ones], axis=1))
            mixed = mixed[:, :LANES] / mixed[:, LANES:]
            mixed_ref[at, lanes] = jnp.where(lane < HEAD_DIM, mixed[:cells], mixed[cells:]).astype(BF)
    mixture = shuffle(mixed_ref[...], 32).astype(BF)
    partial_ref[...] = dot(mixture, out_weight_ref[...]).astype(BF)


def attention_pass(core, mine, theirs, gain, query, key, value, stale_keys, stale_values, out_weight):
    rows, half = mine.shape
    channels = 2 * half
    cells = rows // 2
    whole = pl.BlockSpec(memory_space=pltpu.VMEM)
    small = pl.BlockSpec(memory_space=pltpu.SMEM)
    return pl.pallas_call(
        attention_kernel,
        in_specs=[small] + [whole] * 9,
        out_specs=[whole] * 2,
        out_shape=[
            jax.ShapeDtypeStruct((rows, channels), BF),
            jax.ShapeDtypeStruct((cells, channels), BF),
        ],
        scratch_shapes=[
            pltpu.VMEM((rows, channels), BF),
            pltpu.VMEM((rows, half), BF),
            pltpu.VMEM((rows, half), BF),
            pltpu.VMEM((rows, half), BF),
            pltpu.VMEM((rows, half), BF),
        ],
        compiler_params=params(),
    )(core, mine, theirs, gain, query, key, value, stale_keys, stale_values, out_weight)


def swap(values, axis, step):
    count = lax.axis_size(axis)
    return lax.ppermute(values, axis, [(i, i ^ step) for i in range(count)])


def total_over(values, axis):
    count = lax.axis_size(axis)
    if count & (count - 1):
        return lax.psum(values, axis)
    step = 1
    while step < count:
        values = values + swap(values, axis, step)
        step *= 2
    return values


def on_device(
    image,
    stale_first,
    stale_normed,
    timestep,
    time_weight,
    gain_first,
    shift_first,
    codes_first,
    table_first,
    bias_first,
    attn_gain,
    query_codes,
    query_table,
    key_codes,
    key_table,
    value_codes,
    value_table,
    out_codes,
    out_table,
):
    height, across, channels = image.shape
    cells = height * across
    rows = lax.axis_size("row")
    cols = lax.axis_size("col")
    members = cells * rows * cols * (channels // GROUPS)
    core = (lax.axis_index("col") % 2).astype(jnp.int32)[None]

    sums, edges, pooled, time_shift = first_pass(core, timestep, image, stale_first, stale_normed, time_weight)

    chips = [list(range(k, cols, 2)) for k in range(2)]
    near = lax.all_gather(pooled, "col", axis=0, tiled=True, axis_index_groups=chips)
    near = lax.all_gather(near, "row", axis=0, tiled=True)
    far = swap(near, "col", 1)

    partner_image = swap(image, "col", 1)
    between = [(i, i + 1) for i in range(1, cols - 1, 2)]
    outer = lax.ppermute(edges[0], "col", between + [(j, i) for i, j in between])
    above = lax.ppermute(
        jnp.concatenate([edges[3], outer]), "row", [(i, i + 1) for i in range(rows - 1)]
    )
    below = lax.ppermute(
        jnp.concatenate([edges[2], outer]), "row", [(i + 1, i) for i in range(rows - 1)]
    )
    rim = jnp.concatenate([above, below, outer, edges[1]])
    partner_rim = swap(rim, "col", 1)

    sums = total_over(total_over(sums, "col"), "row")

    weights = decode_taps(core, codes_first, table_first, 0, 9)
    query, key, value = decode_columns(
        core, query_codes, query_table, key_codes, key_table, value_codes, value_table
    )
    out_weight = decode_rows(core, out_codes, out_table)

    residual = convolve(
        core, sums, image, partner_image, rim, partner_rim, gain_first[None], shift_first[None],
        bias_first[None], time_shift, weights, members,
    )
    partner_residual = swap(residual, "col", 1)
    stale_keys, stale_values = stale_pass(near, far, key, value)
    partial, rest = attention_pass(
        core, residual, partner_residual, attn_gain[None], query, key, value, stale_keys, stale_values, out_weight
    )
    arrived = swap(partial[cells:], "col", 1)
    output = rest.astype(F32) + partial[:cells].astype(F32) + arrived.astype(F32)
    return output.astype(BF).reshape(height, across, channels)


def solution(mesh):
    split = P("row", "col", None)
    in_specs = (split,) * 3 + (P(),) * 16
    return jax.shard_map(on_device, mesh=mesh, in_specs=in_specs, out_specs=split, check_vma=False)
```

time: 476 us -> 134 us (0.28); the launches traced: 467 us -> 133 us
  other arithmetic: 232 us -> 2.84 us
  local copies, waits for them, and re-layouts: 117 us -> 7.09 us
  Pallas kernels: 0 us -> 67.9 us
  matrix products: 50.7 us -> 0 us
  between operations: 15.2 us -> 0.87 us
  blocking collectives: 42.2 us -> 29.7 us
  waiting for transfers between devices: 0.03 us -> 9.39 us
  starting transfers between devices: 10.5 us -> 15.5 us
    select_n x9 -> x0, other arithmetic: 213 us -> none  [unpack_weight(): weight = jnp.where(nibbles == code_value, levels[code_value], weight)]
    select_n x13 -> x0, local copies, waits for them, and re-layouts: 81.4 us -> none  [unpack_weight(): weight = jnp.where(nibbles == code_value, levels[code_value], weight)]
    pallas_call x0 -> x7, Pallas kernels: none -> 67.9 us  [the longest x1 18.1 us: convolve(): pl.pallas_call(functools.partial(conv_kernel, members=members, split=0),...]
    dot_general x18 -> x0, matrix products: 50.7 us -> none  [the longest x1 19.6 us: attend(): jnp.einsum('hqk,khd->qhd', weights, value_heads, preferred_element_type=j...]
    psum x1 -> x0, blocking collectives: 42.2 us -> none  [on_device(): sums_first = lax.psum(group_terms(current), ('row', 'col'))]
    all_gather x0 -> x2, blocking collectives: none -> 29.7 us  [the longest x1 15.8 us: on_device(): lax.all_gather(pooled, 'col', axis=0, tiled=True, axis_index_groups=chips)]
    sub x1 -> x0, other arithmetic: 13.4 us -> none  [attend(): exponent = jnp.exp(scores - highest)]
    shift_right_arithmetic x1 -> x0, local copies, waits for them, and re-layouts: 10.5 us -> none  [unpack_weight(): nibbles = jnp.right_shift(packed[..., :, None, :], shifts[:, None]) & 15]
  transfers between devices with their start and end apart: 5 -> 13, of which waited for: 0 -> 5; matrix products, arithmetic and copies ran while one was open for 72% -> 2% of each run, Pallas kernels for 0% -> 37%
where the time goes in v1:
time: 134 us; the launch traced here: 133 us
  Pallas kernels  67.9 us (51%)
  blocking collectives  29.7 us (22%)
  starting transfers between devices  15.5 us (12%)
  waiting for transfers between devices  9.39 us (7%)
  local copies, waits for them, and re-layouts  7.09 us (5%)
  other arithmetic  2.84 us (2%)
    pallas_call x1, Pallas kernels, convolve(): pl.pallas_call(functools.partial(conv_kernel, members=members, split=0),...  18.1 us
    all_gather x1, blocking collectives, on_device(): lax.all_gather(pooled, 'col', axis=0, tiled=True, axis_index_groups=chips)  15.8 us
    pallas_call x1, Pallas kernels, decode_taps(): pl.pallas_call(functools.partial(decode_kernel, count=1, block=64), grid_...  15.6 us
    pallas_call x1, Pallas kernels, attention_pass(): pl.pallas_call(attention_kernel, in_specs=[small] + [whole] * 9, out_spec...  15.2 us
    all_gather x1, blocking collectives, on_device(): near = lax.all_gather(near, 'row', axis=0, tiled=True)  13.8 us
    ppermute x10, starting transfers between devices, swap(): return lax.ppermute(values, axis, [(i, i ^ step) for i in range(count)])  10.1 us
    ppermute x10, waiting for transfers between devices, swap(): return lax.ppermute(values, axis, [(i, i ^ step) for i in range(count)])  9.39 us
    pallas_call x1, Pallas kernels, decode_columns(): pl.pallas_call(functools.partial(decode_kernel, count=count, block=64), g...  6.53 us
  transfers between devices with their start and end apart: 13, of which 5 were waited for; matrix products, arithmetic and copies ran while one was open for 2% of the time, Pallas kernels for 37%

profile of v1, /device:TPU:0, one launch (start us, length us, event | category | flops | bytes accessed | tf_op | source)
XLA Modules:
  0.0 133.2 jit_solution(18121480595655839915)
XLA Ops:
  0.7 3.4 %shard_map.181 = (f32[8,128]{1,0:T(8,128)}, bf16[4,16,1280]{2,1,0:T(8,128)(2,1)}, bf16[16,1280]{1,0:T(8,128)(2,1)}, f32[8,1280]{1,0:T(8,128)}) custom-call(s32[1]{0:T(128)} %bitcast.core_ref, s32[1]{0:T(128)S(6)} %copy.20.step_ref, bf16[16,16,1280]{2,1,0:T(8,128)(2,1)} %half_mine_ref.1, bf16[16,16,1280]{2,1,0:T(8,128)(2,1)} %first_ref.1, ...), custom_call_target="tpu_custom_call" | custom-call | tf_op jit(solution)/shard_map/pallas_call | solution.py:107
  4.2 0.0 copy-start.9
  4.2 0.9 slice_bitcast_fusion.3
  5.1 0.7 collective-permute-start.6
  5.7 4.4 %collective-permute-start.5 = (bf16[16,16,1280]{2,1,0:T(8,128)(2,1)S(1)}, bf16[16,16,1280]{2,1,0:T(8,128)(2,1)S(1)}, u32[]{:S(2)}, u32[]{:S(2)}) collective-permute-start(bf16[16,16,1280]{2,1,0:T(8,128)(2,1)S(1)} %copy-done), channel_id=1, source_target_pairs={{0,1},{1,0},{2,3},{3,2},{4,5},{5,4},{6,7},{7,6},{8,9},{9,8},{10,11... | collective-permute-start | bytes 1966088 | tf_op jit(solution)/shard_map/ppermute | solution.py:460
  10.2 0.0 collective-permute-done.6
  10.2 3.4 %collective-permute-start.7 = (bf16[32,1280]{1,0:T(8,128)(2,1)S(1)}, bf16[32,1280]{1,0:T(8,128)(2,1)S(1)}, u32[]{:S(2)}, u32[]{:S(2)}) collective-permute-start(bf16[32,1280]{1,0:T(8,128)(2,1)S(1)} %get-tuple-element.31), channel_id=1, source_target_pairs={{0,8},{8,16},{16,24},{1,9},{9,17},{17,25},{2,10},{10,18},{18,26},{... | collective-permute-start | bytes 245768 | tf_op jit(solution)/shard_map/ppermute | solution.py:512
  13.6 1.3 collective-permute-start.8
  14.9 15.8 %all_gather.6 = bf16[64,1280]{1,0:T(8,128)(2,1)S(1)} all-gather(bf16[16,1280]{1,0:T(8,128)(2,1)} %get-tuple-element.22), channel_id=1, replica_groups={{0,2,4,6},{1,3,5,7},{8,10,12,14},{9,11,13,15},{16,18,20,22},{17,19,21,2..., dimensions={0}, use_global_device_ids=true | all-gather | bytes 204800 | tf_op jit(solution)/shard_map/all_gather | solution.py:505
  30.8 0.0 collective-permute-done.7
  30.8 0.0 collective-permute-done.8
  30.8 0.1 collective-permute-start.9
  30.9 13.8 %all_gather.7.near_ref = bf16[256,1280]{1,0:T(8,128)(2,1)S(1)} all-gather(bf16[64,1280]{1,0:T(8,128)(2,1)S(1)} %all_gather.6), channel_id=1, replica_groups=mesh['row'=4,'col'=8] {'row'}, dimensions={0}, use_global_device_ids=true | all-gather | bytes 819200 | tf_op jit(solution)/shard_map/all_gather | solution.py:506
  44.7 0.1 collective-permute-start.11
  44.8 0.5 collective-permute-start
  45.3 1.6 %collective-permute-done = f32[8,128]{1,0:T(8,128)S(1)} collective-permute-done((f32[8,128]{1,0:T(8,128)S(1)}, f32[8,128]{1,0:T(8,128)S(1)}, u32[]{:S(2)}, u32[]{:S(2)}) %collective-permute-start) | collective-permute-done | bytes 4128 | tf_op jit(solution)/shard_map/ppermute | solution.py:460
  46.9 1.4 %collective-permute-start.1 = (f32[8,128]{1,0:T(8,128)S(1)}, f32[8,128]{1,0:T(8,128)S(1)}, u32[]{:S(2)}, u32[]{:S(2)}) collective-permute-start(f32[8,128]{1,0:T(8,128)S(1)} %add.26), channel_id=1, source_target_pairs={{0,2},{1,3},{2,0},{3,1},{4,6},{5,7},{6,4},{7,5},{8,10},{9,11},{10,... | collective-permute-start | bytes 12296 | tf_op jit(solution)/shard_map/ppermute | solution.py:460
  48.3 2.2 %collective-permute-done.1 = f32[8,128]{1,0:T(8,128)S(1)} collective-permute-done((f32[8,128]{1,0:T(8,128)S(1)}, f32[8,128]{1,0:T(8,128)S(1)}, u32[]{:S(2)}, u32[]{:S(2)}) %collective-permute-start.1) | collective-permute-done | bytes 4128 | tf_op jit(solution)/shard_map/ppermute | solution.py:460
  50.5 1.8 %collective-permute-start.2 = (f32[8,128]{1,0:T(8,128)S(1)}, f32[8,128]{1,0:T(8,128)S(1)}, u32[]{:S(2)}, u32[]{:S(2)}) collective-permute-start(f32[8,128]{1,0:T(8,128)S(1)} %add.27), channel_id=1, source_target_pairs={{0,4},{1,5},{2,6},{3,7},{4,0},{5,1},{6,2},{7,3},{8,12},{9,13},{10,... | collective-permute-start | bytes 12296 | tf_op jit(solution)/shard_map/ppermute | solution.py:460
  52.3 2.7 %collective-permute-done.2 = f32[8,128]{1,0:T(8,128)S(1)} collective-permute-done((f32[8,128]{1,0:T(8,128)S(1)}, f32[8,128]{1,0:T(8,128)S(1)}, u32[]{:S(2)}, u32[]{:S(2)}) %collective-permute-start.2) | collective-permute-done | bytes 4128 | tf_op jit(solution)/shard_map/ppermute | solution.py:460
  55.0 0.6 collective-permute-start.3
  55.6 0.6 broadcast_in_dim.16.gain_ref
  56.2 0.6 broadcast_in_dim.17.shift_ref
  56.8 0.6 broadcast_in_dim.18.bias_ref
  57.4 1.2 collective-permute-done.3
  58.6 0.6 collective-permute-start.4
  59.2 15.6 %shard_map.182.weight_ref = bf16[9,1280,640]{2,1,0:T(8,128)(2,1)} custom-call(s32[1]{0:T(128)} %bitcast.core_ref, s32[9,320,1280]{2,1,0:T(8,128)} %refs_0_.3, f32[16,1280]{1,0:T(8,128)} %refs_1_.3), custom_call_target="tpu_custom_call" | custom-call | flops 58982400 | bytes 22118400 | tf_op jit(solution)/shard_map/pallas_call | solution.py:167
  74.8 0.0 collective-permute-done.4
  74.8 0.6 add.30.sums_ref
  75.4 0.0 collective-permute-done.9.rim_theirs_ref
  75.4 0.0 collective-permute-done.5.theirs_ref.half_theirs_ref
  75.4 0.0 copy-start.1
  75.4 0.7 copy-done.6
  76.1 0.2 copy-done.1
  76.3 18.1 %shard_map.183.mine_ref = bf16[512,640]{1,0:T(8,128)(2,1)} custom-call(s32[1]{0:T(128)} %bitcast.core_ref, f32[8,128]{1,0:T(8,128)} %add.30.sums_ref, bf16[16,16,1280]{2,1,0:T(8,128)(2,1)} %half_mine_ref.1, bf16[16,16,1280]{2,1,0:T(8,128)(2,1)} %copy-done.1, bf16[96,1280]{1,0:T(8,128)(2,1)} %copy-done.3, bf16[96,1280]{1,0:T(8,128)(2,1)} %copy-done.6, ...), custom_call_target="tpu_custom_call" | custom-call | tf_op jit(solution)/shard_map/pallas_call | solution.py:321
  94.4 0.0 collective-permute-start.10
  94.4 0.6 broadcast_in_dim.19.gain_ref
  95.0 3.6 %shard_map.186.out_weight_ref = bf16[640,1280]{1,0:T(8,128)(2,1)} custom-call(s32[1]{0:T(128)} %bitcast.core_ref, s32[320,1280]{1,0:T(8,128)} %refs_0_.5, f32[16,1280]{1,0:T(8,128)} %refs_1_.5), custom_call_target="tpu_custom_call" | custom-call | flops 6553600 | bytes 2457600 | tf_op jit(solution)/shard_map/pallas_call | solution.py:209
  98.6 6.5 %shard_map.184 = (bf16[1280,640]{1,0:T(8,128)(2,1)}, bf16[1280,640]{1,0:T(8,128)(2,1)}, bf16[1280,640]{1,0:T(8,128)(2,1)}) custom-call(s32[1]{0:T(128)} %bitcast.core_ref, s32[320,1280]{1,0:T(8,128)} %refs_0_.4, f32[16,1280]{1,0:T(8,128)} %refs_1_.4, s32[320,1280]{1,0:T(8,128)} %refs_2_.1, f32[16,1280]{1,0:T(8,128)} %refs_3_.1, s32[320,1280]{1,0:T(8,128)} %refs_4_.1, ...), custom_call_target="tpu_custom_call" | custom-call | flops 19660800 | bytes 7372800 | tf_op jit(solution)/shard_map/pallas_call | solution.py:188
  105.2 0.0 collective-permute-done.11.far_ref
  105.2 0.8 copy-done.12
  106.0 5.4 %shard_map.185 = (bf16[512,640]{1,0:T(8,128)(2,1)}, bf16[512,640]{1,0:T(8,128)(2,1)}) custom-call(bf16[256,1280]{1,0:T(8,128)(2,1)} %copy-done.5, bf16[256,1280]{1,0:T(8,128)(2,1)} %copy-done.12, bf16[1280,640]{1,0:T(8,128)(2,1)} %get-tuple-element.20.key_ref, bf16[1280,640]{1,0:T(8,128)(2,1)} %get-tuple-element.21.value_ref), custom_call_target="tpu_custom_call" | custom-call | flops 1677721600 | bytes 3276800 | tf_op jit(solution)/shard_map/pallas_call | solution.py:364
  111.4 0.8 copy-done.4
  112.3 15.2 %shard_map.187 = (bf16[512,1280]{1,0:T(8,128)(2,1)}, bf16[256,1280]{1,0:T(8,128)(2,1)}) custom-call(s32[1]{0:T(128)} %bitcast.core_ref, bf16[512,640]{1,0:T(8,128)(2,1)} %shard_map.183.mine_ref, bf16[512,640]{1,0:T(8,128)(2,1)} %copy-done.4, f32[1,1280]{1,0:T(1,128)} %broadcast_in_dim.19.gain_ref, bf16[1280,640]{1,0:T(8,128)(2,1)} %get-tuple-element.19.query_ref, ...), custom_call_target="tpu_custom_call" | custom-call | tf_op jit(solution)/shard_map/pallas_call | solution.py:439
  127.5 1.2 slice.23
  128.8 0.6 collective-permute-start.12
  129.3 1.7 %collective-permute-done.12 = bf16[256,1280]{1,0:T(8,128)(2,1)S(1)} collective-permute-done((bf16[256,1280]{1,0:T(8,128)(2,1)S(1)}, bf16[256,1280]{1,0:T(8,128)(2,1)S(1)}, u32[]{:S(2)}, u32[]{:S(2)}) %collective-permute-start.12) | collective-permute-done | bytes 655392 | tf_op jit(solution)/shard_map/ppermute | solution.py:460
  131.1 2.2 %add_convert_fusion = bf16[256,1280]{1,0:T(8,128)(2,1)} fusion(bf16[256,1280]{1,0:T(8,128)(2,1)S(1)} %collective-permute-done.12, bf16[256,1280]{1,0:T(8,128)(2,1)} %get-tuple-element.25, bf16[512,1280]{1,0:T(8,128)(2,1)S(1)} %copy-done.2), kind=kLoop, calls=%fused_computation | loop fusion | flops 1966080 | bytes 2621440 | tf_op jit(solution)/shard_map/convert_element_type | solution.py:540
  (27 shorter events, 0.1 us)
Async XLA Ops:
  0.0 5.7 %copy-start = (bf16[16,16,1280]{2,1,0:T(8,128)(2,1)S(1)}, bf16[16,16,1280]{2,1,0:T(8,128)(2,1)}, u32[]{:S(2)}) copy-start(bf16[16,16,1280]{2,1,0:T(8,128)(2,1)} %half_mine_ref.1) | copy-start | bytes 1966084
  4.2 40.6 %copy-start.11 = (f32[8,128]{1,0:T(8,128)S(1)}, f32[8,128]{1,0:T(8,128)}, u32[]{:S(2)}) copy-start(f32[8,128]{1,0:T(8,128)} %get-tuple-element.16) | copy-start | bytes 12292
  4.2 51.4 %copy-start.7 = (f32[1280]{0:T(1024)S(1)}, f32[1280]{0:T(1024)}, u32[]{:S(2)}) copy-start(f32[1280]{0:T(1024)} %param.24) | copy-start | bytes 15364
  4.2 52.0 %copy-start.8 = (f32[1280]{0:T(1024)S(1)}, f32[1280]{0:T(1024)}, u32[]{:S(2)}) copy-start(f32[1280]{0:T(1024)} %param.25) | copy-start | bytes 15364
  4.2 52.6 %copy-start.9 = (f32[1280]{0:T(1024)S(1)}, f32[1280]{0:T(1024)}, u32[]{:S(2)}) copy-start(f32[1280]{0:T(1024)} %param.28) | copy-start | bytes 15364
  5.1 5.1 %collective-permute-start.6 = (bf16[16,1280]{1,0:T(8,128)(2,1)S(1)}, bf16[16,1280]{1,0:T(8,128)(2,1)S(1)}, u32[]{:S(2)}, u32[]{:S(2)}) collective-permute-start(bf16[16,1280]{1,0:T(8,128)(2,1)S(1)} %get-tuple-element.30), channel_id=1, source_target_pairs={{1,2},{3,4},{5,6},{2,1},{4,3},{6,5},{9,10},{11,12},{13,14},{10,9},... | collective-permute-start | bytes 122888 | tf_op jit(solution)/shard_map/ppermute | solution.py:511
  5.7 69.7 %collective-permute-start.5 = (bf16[16,16,1280]{2,1,0:T(8,128)(2,1)S(1)}, bf16[16,16,1280]{2,1,0:T(8,128)(2,1)S(1)}, u32[]{:S(2)}, u32[]{:S(2)}) collective-permute-start(bf16[16,16,1280]{2,1,0:T(8,128)(2,1)S(1)} %copy-done), channel_id=1, source_target_pairs={{0,1},{1,0},{2,3},{3,2},{4,5},{5,4},{6,7},{7,6},{8,9},{9,8},{10,11... | collective-permute-start | bytes 1966088 | tf_op jit(solution)/shard_map/ppermute | solution.py:460
  10.2 20.6 %collective-permute-start.7 = (bf16[32,1280]{1,0:T(8,128)(2,1)S(1)}, bf16[32,1280]{1,0:T(8,128)(2,1)S(1)}, u32[]{:S(2)}, u32[]{:S(2)}) collective-permute-start(bf16[32,1280]{1,0:T(8,128)(2,1)S(1)} %get-tuple-element.31), channel_id=1, source_target_pairs={{0,8},{8,16},{16,24},{1,9},{9,17},{17,25},{2,10},{10,18},{18,26},{... | collective-permute-start | bytes 245768 | tf_op jit(solution)/shard_map/ppermute | solution.py:512
  13.6 17.1 %collective-permute-start.8 = (bf16[32,1280]{1,0:T(8,128)(2,1)S(1)}, bf16[32,1280]{1,0:T(8,128)(2,1)S(1)}, u32[]{:S(2)}, u32[]{:S(2)}) collective-permute-start(bf16[32,1280]{1,0:T(8,128)(2,1)S(1)} %get-tuple-element.32), channel_id=1, source_target_pairs={{8,0},{16,8},{24,16},{9,1},{17,9},{25,17},{10,2},{18,10},{26,18},{... | collective-permute-start | bytes 245768 | tf_op jit(solution)/shard_map/ppermute | solution.py:515
  30.8 44.0 %copy-start.3 = (bf16[96,1280]{1,0:T(8,128)(2,1)}, bf16[96,1280]{1,0:T(8,128)(2,1)S(1)}, u32[]{:S(2)}) copy-start(bf16[96,1280]{1,0:T(8,128)(2,1)S(1)} %pad_maximum_fusion.rim_mine_ref) | copy-start | bytes 737284
  30.8 44.6 %collective-permute-start.9 = (bf16[96,1280]{1,0:T(8,128)(2,1)S(1)}, bf16[96,1280]{1,0:T(8,128)(2,1)S(1)}, u32[]{:S(2)}, u32[]{:S(2)}) collective-permute-start(bf16[96,1280]{1,0:T(8,128)(2,1)S(1)} %pad_maximum_fusion.rim_mine_ref), channel_id=1, source_target_pairs={{0,1},{1,0},{2,3},{3,2},{4,5},{5,4},{6,7},{7,6},{8,9},{9,8},{10,11... | collective-permute-start | bytes 737288 | tf_op jit(solution)/shard_map/ppermute | solution.py:460
  44.7 30.1 %copy-start.5 = (bf16[256,1280]{1,0:T(8,128)(2,1)}, bf16[256,1280]{1,0:T(8,128)(2,1)S(1)}, u32[]{:S(2)}) copy-start(bf16[256,1280]{1,0:T(8,128)(2,1)S(1)} %all_gather.7.near_ref) | copy-start | bytes 1966084
  44.7 60.5 %collective-permute-start.11 = (bf16[256,1280]{1,0:T(8,128)(2,1)S(1)}, bf16[256,1280]{1,0:T(8,128)(2,1)S(1)}, u32[]{:S(2)}, u32[]{:S(2)}) collective-permute-start(bf16[256,1280]{1,0:T(8,128)(2,1)S(1)} %all_gather.7.near_ref), channel_id=1, source_target_pairs={{0,1},{1,0},{2,3},{3,2},{4,5},{5,4},{6,7},{7,6},{8,9},{9,8},{10,11... | collective-permute-start | bytes 1966088 | tf_op jit(solution)/shard_map/ppermute | solution.py:460
  44.8 2.1 %collective-permute-start = (f32[8,128]{1,0:T(8,128)S(1)}, f32[8,128]{1,0:T(8,128)S(1)}, u32[]{:S(2)}, u32[]{:S(2)}) collective-permute-start(f32[8,128]{1,0:T(8,128)S(1)} %copy-done.11), channel_id=1, source_target_pairs={{0,1},{1,0},{2,3},{3,2},{4,5},{5,4},{6,7},{7,6},{8,9},{9,8},{10,11... | collective-permute-start | bytes 12296 | tf_op jit(solution)/shard_map/ppermute | solution.py:460
  46.9 3.6 %collective-permute-start.1 = (f32[8,128]{1,0:T(8,128)S(1)}, f32[8,128]{1,0:T(8,128)S(1)}, u32[]{:S(2)}, u32[]{:S(2)}) collective-permute-start(f32[8,128]{1,0:T(8,128)S(1)} %add.26), channel_id=1, source_target_pairs={{0,2},{1,3},{2,0},{3,1},{4,6},{5,7},{6,4},{7,5},{8,10},{9,11},{10,... | collective-permute-start | bytes 12296 | tf_op jit(solution)/shard_map/ppermute | solution.py:460
  50.5 4.5 %collective-permute-start.2 = (f32[8,128]{1,0:T(8,128)S(1)}, f32[8,128]{1,0:T(8,128)S(1)}, u32[]{:S(2)}, u32[]{:S(2)}) collective-permute-start(f32[8,128]{1,0:T(8,128)S(1)} %add.27), channel_id=1, source_target_pairs={{0,4},{1,5},{2,6},{3,7},{4,0},{5,1},{6,2},{7,3},{8,12},{9,13},{10,... | collective-permute-start | bytes 12296 | tf_op jit(solution)/shard_map/ppermute | solution.py:460
  55.0 3.6 %collective-permute-start.3 = (f32[8,128]{1,0:T(8,128)S(1)}, f32[8,128]{1,0:T(8,128)S(1)}, u32[]{:S(2)}, u32[]{:S(2)}) collective-permute-start(f32[8,128]{1,0:T(8,128)S(1)} %add.28), channel_id=1, source_target_pairs={{0,8},{8,0},{16,24},{24,16},{1,9},{9,1},{17,25},{25,17},{2,10},{10... | collective-permute-start | bytes 12296 | tf_op jit(solution)/shard_map/ppermute | solution.py:460
  58.6 16.2 %collective-permute-start.4 = (f32[8,128]{1,0:T(8,128)S(1)}, f32[8,128]{1,0:T(8,128)S(1)}, u32[]{:S(2)}, u32[]{:S(2)}) collective-permute-start(f32[8,128]{1,0:T(8,128)S(1)} %add.29), channel_id=1, source_target_pairs={{0,16},{8,24},{16,0},{24,8},{1,17},{9,25},{17,1},{25,9},{2,18},{10... | collective-permute-start | bytes 12296 | tf_op jit(solution)/shard_map/ppermute | solution.py:460
  75.4 0.7 copy-start.6
  75.4 0.9 copy-start.1
  76.3 18.1 %copy-start.10 = (f32[1280]{0:T(1024)S(1)}, f32[1280]{0:T(1024)}, u32[]{:S(2)}) copy-start(f32[1280]{0:T(1024)} %param.29) | copy-start | bytes 15364
  94.4 17.0 %collective-permute-start.10 = (bf16[512,640]{1,0:T(8,128)(2,1)}, bf16[512,640]{1,0:T(8,128)(2,1)S(1)}, u32[]{:S(2)}, u32[]{:S(2)}) collective-permute-start(bf16[512,640]{1,0:T(8,128)(2,1)} %shard_map.183.mine_ref), channel_id=1, source_target_pairs={{0,1},{1,0},{2,3},{3,2},{4,5},{5,4},{6,7},{7,6},{8,9},{9,8},{10,11... | collective-permute-start | bytes 1966088 | tf_op jit(solution)/shard_map/ppermute | solution.py:460
  105.2 0.8 copy-start.12
  111.4 0.8 copy-start.4
  127.5 3.5 %copy-start.2 = (bf16[512,1280]{1,0:T(8,128)(2,1)S(1)}, bf16[512,1280]{1,0:T(8,128)(2,1)}, u32[]{:S(2)}) copy-start(bf16[512,1280]{1,0:T(8,128)(2,1)} %get-tuple-element.26) | copy-start | bytes 3932164
  128.8 2.3 %collective-permute-start.12 = (bf16[256,1280]{1,0:T(8,128)(2,1)S(1)}, bf16[256,1280]{1,0:T(8,128)(2,1)S(1)}, u32[]{:S(2)}, u32[]{:S(2)}) collective-permute-start(bf16[256,1280]{1,0:T(8,128)(2,1)S(1)} %slice.23), channel_id=1, source_target_pairs={{0,1},{1,0},{2,3},{3,2},{4,5},{5,4},{6,7},{7,6},{8,9},{9,8},{10,11... | collective-permute-start | bytes 1966088 | tf_op jit(solution)/shard_map/ppermute | solution.py:460

commit v2 on v1

--- a/solution.py
+++ b/solution.py
@@ -15,11 +15,10 @@
 LANES = 128
 BF = jnp.bfloat16
 F32 = jnp.float32
-VMEM_LIMIT = 56 * 2**20
-
-
-def params(**extra):
-    return pltpu.CompilerParams(vmem_limit_bytes=VMEM_LIMIT, **extra)
+
+
+def params(mebibytes):
+    return pltpu.CompilerParams(vmem_limit_bytes=mebibytes * 2**20)
 
 
 def dot(a, b, **extra):
@@ -114,7 +113,7 @@
             jax.ShapeDtypeStruct((pools, channels), BF),
             jax.ShapeDtypeStruct((8, channels), F32),
         ],
-        compiler_params=params(),
+        compiler_params=params(12),
     )(core, timestep, image, stale_first, stale_normed, time_weight)
 
 
@@ -161,24 +160,27 @@
     return pl.CostEstimate(flops=8 * weights, bytes_accessed=3 * weights, transcendentals=0)
 
 
-def decode_taps(core, codes, table, start, stop):
+def decode_taps(core, codes, table, weights, start, stop):
     words, channels = codes.shape[1:]
     half = channels // 2
-    return pl.pallas_call(
-        functools.partial(decode_kernel, count=1, block=64),
+    into = [] if weights is None else [weights]
+    return pl.pallas_call(
+        lambda core_ref, codes_ref, table_ref, *refs: decode_into(codes_ref, table_ref, refs[-1], 64),
         grid_spec=pltpu.PrefetchScalarGridSpec(
             num_scalar_prefetch=1,
             grid=(stop - start,),
             in_specs=[
                 pl.BlockSpec((1, words, half), lambda t, c: (start + t, 0, c[0])),
                 pl.BlockSpec((16, half), lambda t, c: (0, c[0])),
-            ],
-            out_specs=[pl.BlockSpec((1, 4 * words, half), lambda t, c: (t, 0, 0))],
+            ]
+            + [pl.BlockSpec(memory_space=pl.ANY)] * len(into),
+            out_specs=pl.BlockSpec((1, 4 * words, half), lambda t, c: (start + t, 0, 0)),
         ),
-        out_shape=[jax.ShapeDtypeStruct((stop - start, 4 * words, half), BF)],
-        compiler_params=params(),
+        out_shape=jax.ShapeDtypeStruct((codes.shape[0], 4 * words, half), BF),
+        input_output_aliases={3: 0} if into else {},
+        compiler_params=params(8),
         cost_estimate=decode_cost((stop - start) * 4 * words * half),
-    )(core, codes, table)[0]
+    )(core, codes, table, *into)
 
 
 def decode_columns(core, *pairs):
@@ -198,7 +200,7 @@
             out_specs=[pl.BlockSpec((4 * words, half), lambda t, c: (0, 0))] * count,
         ),
         out_shape=[jax.ShapeDtypeStruct((4 * words, half), BF)] * count,
-        compiler_params=params(),
+        compiler_params=params(14),
         cost_estimate=decode_cost(count * 4 * words * half),
     )(core, *pairs)
 
@@ -218,14 +220,14 @@
             out_specs=[pl.BlockSpec((4 * half, channels), lambda t, c: (0, 0))],
         ),
         out_shape=[jax.ShapeDtypeStruct((4 * half, channels), BF)],
-        compiler_params=params(),
+        compiler_params=params(10),
         cost_estimate=decode_cost(4 * half * channels),
     )(core, codes, table)[0]
 
 
 def conv_kernel(
     core_ref, sums_ref, mine_ref, theirs_ref, rim_mine_ref, rim_theirs_ref, gain_ref, shift_ref, bias_ref, time_ref,
-    half_mine_ref, half_theirs_ref, weight_ref, out_ref, act_ref, rim_ref, padded_ref, total_ref, *, members, split,
+    weight_ref, out_ref, act_ref, rim_ref, padded_ref, total_ref, *, members,
 ):
     tap = pl.program_id(0)
     taps = pl.num_programs(0)
@@ -304,8 +306,9 @@
     @pl.when(tap == taps - 1)
     def _():
         extra = bias_ref[...] + time_ref[0:1]
-        for side, ref in enumerate((half_mine_ref, half_theirs_ref)):
-            image = ref[...].reshape(cells, -1).astype(F32)
+        half = channels // 2
+        for side, ref in enumerate((mine_ref, theirs_ref)):
+            image = jnp.where(core == 0, ref[:, :, :half], ref[:, :, half:]).reshape(cells, half).astype(F32)
             rows = slice(side * cells, (side + 1) * cells)
             conv = total_ref[rows] + part[rows] + extra
             out_ref[rows] = (image + conv).astype(BF)
@@ -319,7 +322,7 @@
     part = lambda *shape: pl.BlockSpec(shape, lambda t, c: (0,) * (len(shape) - 1) + (c[0],))
     rim_rows = rim_mine.shape[0]
     return pl.pallas_call(
-        functools.partial(conv_kernel, members=members, split=0),
+        functools.partial(conv_kernel, members=members),
         grid_spec=pltpu.PrefetchScalarGridSpec(
             num_scalar_prefetch=1,
             grid=(9,),
@@ -333,8 +336,6 @@
                 whole(1, channels),
                 part(1, half),
                 part(8, half),
-                part(height, across, half),
-                part(height, across, half),
                 pl.BlockSpec((1, channels, half), lambda t, c: (t, 0, 0)),
             ],
             out_specs=whole(2 * cells, half),
@@ -346,8 +347,8 @@
             ],
         ),
         out_shape=jax.ShapeDtypeStruct((2 * cells, half), BF),
-        compiler_params=params(),
-    )(core, sums, mine, theirs, rim_mine, rim_theirs, gain, shift, bias, time_shift, mine, theirs, weights)
+        compiler_params=params(24),
+    )(core, sums, mine, theirs, rim_mine, rim_theirs, gain, shift, bias, time_shift, weights)
 
 
 def stale_kernel(near_ref, far_ref, key_ref, value_ref, keys_ref, values_ref):
@@ -366,7 +367,7 @@
         in_specs=[whole] * 4,
         out_specs=[whole] * 2,
         out_shape=[jax.ShapeDtypeStruct((2 * rows, half), BF)] * 2,
-        compiler_params=params(),
+        compiler_params=params(20),
         cost_estimate=pl.CostEstimate(
             flops=8 * rows * channels * half, bytes_accessed=4 * channels * half, transcendentals=0
         ),
@@ -375,7 +376,7 @@
 
 def attention_kernel(
     core_ref, mine_ref, theirs_ref, gain_ref, query_ref, key_ref, value_ref, stale_keys_ref, stale_values_ref,
-    out_weight_ref, partial_ref, rest_ref, normed_ref, q_ref, k_ref, v_ref, mixed_ref,
+    out_weight_ref, send_ref, keep_ref, normed_ref, q_ref, k_ref, v_ref, mixed_ref,
 ):
     rows, half = mine_ref.shape
     cells = rows // 2
@@ -389,7 +390,7 @@
         high = jnp.where(first, other, own)
         residual = jnp.concatenate([low, high], axis=1)
         if side == 0:
-            rest_ref[...] = residual.astype(BF)
+            keep_ref[...] = residual
         average = jnp.sum(residual, axis=1, keepdims=True) / channels
         centred = residual - average
         deviation = jnp.sum(centred * centred, axis=1, keepdims=True) / channels
@@ -427,7 +428,8 @@
             mixed = mixed[:, :LANES] / mixed[:, LANES:]
             mixed_ref[at, lanes] = jnp.where(lane < HEAD_DIM, mixed[:cells], mixed[cells:]).astype(BF)
     mixture = shuffle(mixed_ref[...], 32).astype(BF)
-    partial_ref[...] = dot(mixture, out_weight_ref[...]).astype(BF)
+    send_ref[...] = dot(mixture[cells:], out_weight_ref[...]).astype(BF)
+    keep_ref[...] += dot(mixture[:cells], out_weight_ref[...])
 
 
 def attention_pass(core, mine, theirs, gain, query, key, value, stale_keys, stale_values, out_weight):
@@ -441,8 +443,8 @@
         in_specs=[small] + [whole] * 9,
         out_specs=[whole] * 2,
         out_shape=[
-            jax.ShapeDtypeStruct((rows, channels), BF),
             jax.ShapeDtypeStruct((cells, channels), BF),
+            jax.ShapeDtypeStruct((cells, channels), F32),
         ],
         scratch_shapes=[
             pltpu.VMEM((rows, channels), BF),
@@ -451,7 +453,7 @@
             pltpu.VMEM((rows, half), BF),
             pltpu.VMEM((rows, half), BF),
         ],
-        compiler_params=params(),
+        compiler_params=params(28),
     )(core, mine, theirs, gain, query, key, value, stale_keys, stale_values, out_weight)
 
 
@@ -460,15 +462,17 @@
     return lax.ppermute(values, axis, [(i, i ^ step) for i in range(count)])
 
 
-def total_over(values, axis):
+def steps_over(axis, first):
     count = lax.axis_size(axis)
-    if count & (count - 1):
-        return lax.psum(values, axis)
-    step = 1
-    while step < count:
-        values = values + swap(values, axis, step)
-        step *= 2
-    return values
+    steps = []
+    while first < count:
+        steps.append((axis, first))
+        first *= 2
+    return steps
+
+
+def tie(first, second):
+    return lax.optimization_barrier((first, second))
 
 
 def on_device(
@@ -501,42 +505,54 @@
 
     sums, edges, pooled, time_shift = first_pass(core, timestep, image, stale_first, stale_normed, time_weight)
 
-    chips = [list(range(k, cols, 2)) for k in range(2)]
-    near = lax.all_gather(pooled, "col", axis=0, tiled=True, axis_index_groups=chips)
-    near = lax.all_gather(near, "row", axis=0, tiled=True)
+    between = [(i, i + 1) for i in range(1, cols - 1, 2)]
+    sum_steps = steps_over("col", 1) + steps_over("row", 1)
+    pool_steps = steps_over("col", 2) + steps_over("row", 1)
+    chunks = [(0, 2), (2, 4), (4, 6), (6, 9)]
+    slots = max(len(sum_steps), len(pool_steps), len(chunks))
+    weights = None
+    near = pooled
+    codes = codes_first
+    for slot in range(slots):
+        if weights is not None:
+            (sums, near), weights = tie((sums, near), weights)
+        if slot == 0:
+            outer = lax.ppermute(edges[0], "col", between + [(j, i) for i, j in between])
+        elif slot == 1:
+            above = lax.ppermute(
+                jnp.concatenate([edges[3], outer]), "row", [(i, i + 1) for i in range(rows - 1)]
+            )
+            below = lax.ppermute(
+                jnp.concatenate([edges[2], outer]), "row", [(i + 1, i) for i in range(rows - 1)]
+            )
+        elif slot == 2:
+            rim = jnp.concatenate([above, below, outer, edges[1]])
+            partner_rim = swap(rim, "col", 1)
+        elif slot == 3:
+            partner_image = swap(image, "col", 1)
+        next_sums = sums + swap(sums, *sum_steps[slot]) if slot < len(sum_steps) else sums
+        next_near = jnp.concatenate([near, swap(near, *pool_steps[slot])]) if slot < len(pool_steps) else near
+        if slot < len(chunks):
+            _, codes = tie((sums, near), codes)
+            weights = decode_taps(core, codes, table_first, weights, *chunks[slot])
+        sums = next_sums
+        near = next_near
     far = swap(near, "col", 1)
-
-    partner_image = swap(image, "col", 1)
-    between = [(i, i + 1) for i in range(1, cols - 1, 2)]
-    outer = lax.ppermute(edges[0], "col", between + [(j, i) for i, j in between])
-    above = lax.ppermute(
-        jnp.concatenate([edges[3], outer]), "row", [(i, i + 1) for i in range(rows - 1)]
-    )
-    below = lax.ppermute(
-        jnp.concatenate([edges[2], outer]), "row", [(i + 1, i) for i in range(rows - 1)]
-    )
-    rim = jnp.concatenate([above, below, outer, edges[1]])
-    partner_rim = swap(rim, "col", 1)
-
-    sums = total_over(total_over(sums, "col"), "row")
-
-    weights = decode_taps(core, codes_first, table_first, 0, 9)
     query, key, value = decode_columns(
         core, query_codes, query_table, key_codes, key_table, value_codes, value_table
     )
-    out_weight = decode_rows(core, out_codes, out_table)
-
     residual = convolve(
         core, sums, image, partner_image, rim, partner_rim, gain_first[None], shift_first[None],
         bias_first[None], time_shift, weights, members,
     )
     partner_residual = swap(residual, "col", 1)
+    (residual, out_codes), _ = tie((residual, out_codes), residual)
+    out_weight = decode_rows(core, out_codes, out_table)
     stale_keys, stale_values = stale_pass(near, far, key, value)
-    partial, rest = attention_pass(
+    send, keep = attention_pass(
         core, residual, partner_residual, attn_gain[None], query, key, value, stale_keys, stale_values, out_weight
     )
-    arrived = swap(partial[cells:], "col", 1)
-    output = rest.astype(F32) + partial[:cells].astype(F32) + arrived.astype(F32)
+    output = keep + swap(send, "col", 1).astype(F32)
     return output.astype(BF).reshape(height, across, channels)
 
 

time: 134 us -> 87.9 us (0.66)
  blocking collectives: 29.7 us -> 0 us
  Pallas kernels: 67.9 us -> 45.7 us
  starting transfers between devices: 15.5 us -> 22.6 us
  local copies, waits for them, and re-layouts: 7.09 us -> 9.71 us
  waiting for transfers between devices: 9.39 us -> 7.16 us
  other arithmetic: 2.84 us -> 1.1 us
    all_gather x2 -> x0, blocking collectives: 29.7 us -> none  [the longest x1 15.8 us: on_device(): lax.all_gather(pooled, 'col', axis=0, tiled=True, axis_index_groups=chips)]
    unnamed x26 -> x40, local copies, waits for them, and re-layouts: 2.61 us -> 9.68 us
    ppermute x10 -> x14, starting transfers between devices: 10.1 us -> 17.1 us  [swap(): return lax.ppermute(values, axis, [(i, i ^ step) for i in range(count)])]
    pallas_call x2 -> x5, Pallas kernels: 33.7 us -> 26.9 us  [the longest x1 14.8 us: convolve(): pl.pallas_call(functools.partial(conv_kernel, members=members), grid_spec...]
    pallas_call x1, Pallas kernels: 15.2 us -> 10.5 us  [attention_pass(): pl.pallas_call(attention_kernel, in_specs=[small] + [whole] * 9, out_spec...]
    pallas_call x1, Pallas kernels: 5.43 us -> 2.23 us  [stale_pass(): pl.pallas_call(stale_kernel, in_specs=[whole] * 4, out_specs=[whole] * 2,...]
    ppermute x10 -> x14, waiting for transfers between devices: 9.39 us -> 6.45 us  [swap(): return lax.ppermute(values, axis, [(i, i ^ step) for i in range(count)])]
    pallas_call x1, Pallas kernels: 6.53 us -> 3.72 us  [decode_columns(): pl.pallas_call(functools.partial(decode_kernel, count=count, block=64), g...]
  transfers between devices with their start and end apart: 13 -> 17, of which waited for: 5 -> 5; matrix products, arithmetic and copies ran while one was open for 2% -> 0% of each run, Pallas kernels for 37% -> 39%
where the time goes in v2:
time: 87.9 us; the launch traced here: 87.3 us
  Pallas kernels  45.7 us (52%)
  starting transfers between devices  22.6 us (26%)
  local copies, waits for them, and re-layouts  9.71 us (11%)
  waiting for transfers between devices  7.16 us (8%)
  between operations  1.11 us (1%)
  other arithmetic  1.1 us (1%)
    ppermute x14, starting transfers between devices, swap(): return lax.ppermute(values, axis, [(i, i ^ step) for i in range(count)])  17.1 us
    pallas_call x1, Pallas kernels, convolve(): pl.pallas_call(functools.partial(conv_kernel, members=members), grid_spec...  14.8 us
    pallas_call x4, Pallas kernels, decode_taps(): pl.pallas_call(lambda core_ref, codes_ref, table_ref, *refs: decode_into(...  12 us
    pallas_call x1, Pallas kernels, attention_pass(): pl.pallas_call(attention_kernel, in_specs=[small] + [whole] * 9, out_spec...  10.5 us
    unnamed x40, local copies, waits for them, and re-layouts  9.68 us
    ppermute x14, waiting for transfers between devices, swap(): return lax.ppermute(values, axis, [(i, i ^ step) for i in range(count)])  6.45 us
    pallas_call x1, Pallas kernels, decode_columns(): pl.pallas_call(functools.partial(decode_kernel, count=count, block=64), g...  3.72 us
    ppermute x1, starting transfers between devices, on_device(): lax.ppermute(jnp.concatenate([edges[3], outer]), 'row', [(i, i + 1) for i...  3.4 us
  transfers between devices with their start and end apart: 17, of which 5 were waited for; matrix products, arithmetic and copies ran while one was open for 0% of the time, Pallas kernels for 39%

profile of v2, /device:TPU:0, one launch (start us, length us, event | category | flops | bytes accessed | tf_op | source)
XLA Modules:
  0.0 87.3 jit_solution(9624352264120708916)
XLA Ops:
  0.7 0.0 copy-start.2
  0.7 1.1 %copy-done.2 = bf16[16,16,1280]{2,1,0:T(8,128)(2,1)S(1)} copy-done((bf16[16,16,1280]{2,1,0:T(8,128)(2,1)S(1)}, bf16[16,16,1280]{2,1,0:T(8,128)(2,1)}, u32[]{:S(2)}) %copy-start.2) | copy-done | bytes 655384
  1.7 1.1 %copy-done.9 = bf16[320,1280]{1,0:T(8,128)(2,1)S(1)} copy-done((bf16[320,1280]{1,0:T(8,128)(2,1)S(1)}, bf16[320,1280]{1,0:T(8,128)(2,1)}, u32[]{:S(2)}) %copy-start.9) | copy-done | bytes 819224
  2.9 1.1 %copy-done.10 = bf16[16,16,1280]{2,1,0:T(8,128)(2,1)S(1)} copy-done((bf16[16,16,1280]{2,1,0:T(8,128)(2,1)S(1)}, bf16[16,16,1280]{2,1,0:T(8,128)(2,1)}, u32[]{:S(2)}) %copy-start.10) | copy-done | bytes 655384
  4.0 1.1 %copy-done.11 = bf16[16,16,1280]{2,1,0:T(8,128)(2,1)S(1)} copy-done((bf16[16,16,1280]{2,1,0:T(8,128)(2,1)S(1)}, bf16[16,16,1280]{2,1,0:T(8,128)(2,1)}, u32[]{:S(2)}) %copy-start.11) | copy-done | bytes 655384
  5.1 1.0 %shard_map.181 = (f32[8,128]{1,0:T(8,128)S(1)}, bf16[4,16,1280]{2,1,0:T(8,128)(2,1)S(1)}, bf16[16,1280]{1,0:T(8,128)(2,1)S(1)}, f32[8,1280]{1,0:T(8,128)S(1)}) custom-call(s32[1]{0:T(128)} %bitcast.core_ref, s32[1]{0:T(128)S(6)} %copy.26.step_ref, bf16[16,16,1280]{2,1,0:T(8,128)(2,1)S(1)} %copy-done.2, bf16[16,16,1280]{2,1,0:T(8,128)(2,1)S(1)} %copy-done.10, ...), custom_call_target="tpu_custom_call" | custom-call | tf_op jit(solution)/shard_map/pallas_call | solution.py:106
  6.1 3.1 %collective-permute-start.1 = (bf16[16,1280]{1,0:T(8,128)(2,1)S(1)}, bf16[16,1280]{1,0:T(8,128)(2,1)S(1)}, u32[]{:S(2)}, u32[]{:S(2)}) collective-permute-start(bf16[16,1280]{1,0:T(8,128)(2,1)S(1)} %get-tuple-element.35), channel_id=1, source_target_pairs={{0,2},{1,3},{2,0},{3,1},{4,6},{5,7},{6,4},{7,5},{8,10},{9,11},{10,... | collective-permute-start | bytes 122888 | tf_op jit(solution)/shard_map/ppermute | solution.py:462
  9.2 5.2 %copy-done = s32[9,320,1280]{2,1,0:T(8,128)S(1)} copy-done((s32[9,320,1280]{2,1,0:T(8,128)S(1)}, s32[9,320,1280]{2,1,0:T(8,128)}, u32[]{:S(2)}) %copy-start) | copy-done | bytes 14745624
  14.4 2.7 %shard_map.182.refs_0_ = bf16[9,1280,640]{2,1,0:T(8,128)(2,1)S(1)} custom-call(s32[1]{0:T(128)} %bitcast.core_ref, s32[9,320,1280]{2,1,0:T(8,128)S(1)} %copy-done, f32[16,1280]{1,0:T(8,128)S(1)} %copy-done.8), custom_call_target="tpu_custom_call" | custom-call | flops 13107200 | bytes 4915200 | tf_op jit(solution)/shard_map/pallas_call | solution.py:167
  17.1 2.7 %collective-permute-start.3 = (bf16[32,1280]{1,0:T(8,128)(2,1)S(1)}, bf16[32,1280]{1,0:T(8,128)(2,1)S(1)}, u32[]{:S(2)}, u32[]{:S(2)}) collective-permute-start(bf16[32,1280]{1,0:T(8,128)(2,1)S(1)} %pad_maximum_fusion.6), channel_id=1, source_target_pairs={{0,4},{1,5},{2,6},{3,7},{4,0},{5,1},{6,2},{7,3},{8,12},{9,13},{10,... | collective-permute-start | bytes 245768 | tf_op jit(solution)/shard_map/ppermute | solution.py:462
  19.8 0.4 collective-permute-start.2
  20.2 2.7 %shard_map.183.refs_0_ = bf16[9,1280,640]{2,1,0:T(8,128)(2,1)S(1)} custom-call(s32[1]{0:T(128)} %bitcast.core_ref, s32[9,320,1280]{2,1,0:T(8,128)S(1)} %copy-done.1, f32[16,1280]{1,0:T(8,128)S(1)} %copy-done.8, bf16[9,1280,640]{2,1,0:T(8,128)(2,1)S(1)} %shard_map.182.refs_0_), custom_call_target="tpu_custom_call", output_to_operand_aliasing={{}: (3, {})} | custom-call | flops 13107200 | bytes 4915200 | tf_op jit(solution)/shard_map/pallas_call | solution.py:167
  22.9 0.9 %collective-permute-done.2 = f32[8,128]{1,0:T(8,128)S(1)} collective-permute-done((f32[8,128]{1,0:T(8,128)S(1)}, f32[8,128]{1,0:T(8,128)S(1)}, u32[]{:S(2)}, u32[]{:S(2)}) %collective-permute-start.2) | collective-permute-done | bytes 4128 | tf_op jit(solution)/shard_map/ppermute | solution.py:462
  23.8 0.8 collective-permute-done.3
  24.6 1.6 %collective-permute-start.5 = (bf16[64,1280]{1,0:T(8,128)(2,1)S(1)}, bf16[64,1280]{1,0:T(8,128)(2,1)S(1)}, u32[]{:S(2)}, u32[]{:S(2)}) collective-permute-start(bf16[64,1280]{1,0:T(8,128)(2,1)S(1)} %pad_maximum_fusion.3), channel_id=1, source_target_pairs={{0,8},{8,0},{16,24},{24,16},{1,9},{9,1},{17,25},{25,17},{2,10},{10... | collective-permute-start | bytes 491528 | tf_op jit(solution)/shard_map/ppermute | solution.py:462
  26.2 1.0 %collective-permute-start.4 = (f32[8,128]{1,0:T(8,128)S(1)}, f32[8,128]{1,0:T(8,128)S(1)}, u32[]{:S(2)}, u32[]{:S(2)}) collective-permute-start(f32[8,128]{1,0:T(8,128)S(1)} %add.24), channel_id=1, source_target_pairs={{0,4},{1,5},{2,6},{3,7},{4,0},{5,1},{6,2},{7,3},{8,12},{9,13},{10,... | collective-permute-start | bytes 12296 | tf_op jit(solution)/shard_map/ppermute | solution.py:462
  27.2 0.0 copy-start.3
  27.2 0.8 collective-permute-start.10
  28.0 2.7 %shard_map.184.refs_0_ = bf16[9,1280,640]{2,1,0:T(8,128)(2,1)S(1)} custom-call(s32[1]{0:T(128)} %bitcast.core_ref, s32[9,320,1280]{2,1,0:T(8,128)S(1)} %copy-done.1, f32[16,1280]{1,0:T(8,128)S(1)} %copy-done.8, bf16[9,1280,640]{2,1,0:T(8,128)(2,1)S(1)} %shard_map.183.refs_0_), custom_call_target="tpu_custom_call", output_to_operand_aliasing={{}: (3, {})} | custom-call | flops 13107200 | bytes 4915200 | tf_op jit(solution)/shard_map/pallas_call | solution.py:167
  30.8 0.0 collective-permute-done.5
  30.8 1.6 %collective-permute-start.7 = (bf16[128,1280]{1,0:T(8,128)(2,1)S(1)}, bf16[128,1280]{1,0:T(8,128)(2,1)S(1)}, u32[]{:S(2)}, u32[]{:S(2)}) collective-permute-start(bf16[128,1280]{1,0:T(8,128)(2,1)S(1)} %pad_maximum_fusion.1), channel_id=1, source_target_pairs={{0,16},{8,24},{16,0},{24,8},{1,17},{9,25},{17,1},{25,9},{2,18},{10... | collective-permute-start | bytes 983048 | tf_op jit(solution)/shard_map/ppermute | solution.py:462
  32.5 3.4 %collective-permute-start.11 = (bf16[32,1280]{1,0:T(8,128)(2,1)S(1)}, bf16[32,1280]{1,0:T(8,128)(2,1)S(1)}, u32[]{:S(2)}, u32[]{:S(2)}) collective-permute-start(bf16[32,1280]{1,0:T(8,128)(2,1)S(1)} %get-tuple-element.67), channel_id=1, source_target_pairs={{0,8},{8,16},{16,24},{1,9},{9,17},{17,25},{2,10},{10,18},{18,26},{... | collective-permute-start | bytes 245768 | tf_op jit(solution)/shard_map/ppermute | solution.py:522
  35.9 1.3 %collective-permute-start.12 = (bf16[32,1280]{1,0:T(8,128)(2,1)S(1)}, bf16[32,1280]{1,0:T(8,128)(2,1)S(1)}, u32[]{:S(2)}, u32[]{:S(2)}) collective-permute-start(bf16[32,1280]{1,0:T(8,128)(2,1)S(1)} %get-tuple-element.68), channel_id=1, source_target_pairs={{8,0},{16,8},{24,16},{9,1},{17,9},{25,17},{10,2},{18,10},{26,18},{... | collective-permute-start | bytes 245768 | tf_op jit(solution)/shard_map/ppermute | solution.py:525
  37.2 2.0 %collective-permute-start.9 = (bf16[16,16,1280]{2,1,0:T(8,128)(2,1)S(1)}, bf16[16,16,1280]{2,1,0:T(8,128)(2,1)S(1)}, u32[]{:S(2)}, u32[]{:S(2)}) collective-permute-start(bf16[16,16,1280]{2,1,0:T(8,128)(2,1)S(1)} %copy-done.3), channel_id=1, source_target_pairs={{0,1},{1,0},{2,3},{3,2},{4,5},{5,4},{6,7},{7,6},{8,9},{9,8},{10,11... | collective-permute-start | bytes 1966088 | tf_op jit(solution)/shard_map/ppermute | solution.py:462
  39.2 2.4 %collective-permute-start.6 = (f32[8,128]{1,0:T(8,128)S(1)}, f32[8,128]{1,0:T(8,128)S(1)}, u32[]{:S(2)}, u32[]{:S(2)}) collective-permute-start(f32[8,128]{1,0:T(8,128)S(1)} %add.25), channel_id=1, source_target_pairs={{0,8},{8,0},{16,24},{24,16},{1,9},{9,1},{17,25},{25,17},{2,10},{10... | collective-permute-start | bytes 12296 | tf_op jit(solution)/shard_map/ppermute | solution.py:462
  41.5 0.7 collective-permute-done.12
  42.2 0.0 copy-start.16
  42.3 0.0 copy-start.17
  42.3 0.0 copy-start.18
  42.3 1.1 %collective-permute-start.13 = (bf16[96,1280]{1,0:T(8,128)(2,1)S(1)}, bf16[96,1280]{1,0:T(8,128)(2,1)S(1)}, u32[]{:S(2)}, u32[]{:S(2)}) collective-permute-start(bf16[96,1280]{1,0:T(8,128)(2,1)S(1)} %pad_maximum_fusion.2.rim_mine_ref), channel_id=1, source_target_pairs={{0,1},{1,0},{2,3},{3,2},{4,5},{5,4},{6,7},{7,6},{8,9},{9,8},{10,11... | collective-permute-start | bytes 737288 | tf_op jit(solution)/shard_map/ppermute | solution.py:462
  43.3 4.0 %shard_map.185.weight_ref = bf16[9,1280,640]{2,1,0:T(8,128)(2,1)S(1)} custom-call(s32[1]{0:T(128)} %bitcast.core_ref, s32[9,320,1280]{2,1,0:T(8,128)S(1)} %copy-done.1, f32[16,1280]{1,0:T(8,128)S(1)} %copy-done.8, bf16[9,1280,640]{2,1,0:T(8,128)(2,1)S(1)} %shard_map.184.refs_0_), custom_call_target="tpu_custom_call", output_to_operand_aliasing={{}: (3, {})} | custom-call | flops 19660800 | bytes 7372800 | tf_op jit(solution)/shard_map/pallas_call | solution.py:167
  47.4 0.1 collective-permute-start.15
  47.5 0.6 collective-permute-start.8
  48.2 3.0 %collective-permute-done.8 = f32[8,128]{1,0:T(8,128)S(1)} collective-permute-done((f32[8,128]{1,0:T(8,128)S(1)}, f32[8,128]{1,0:T(8,128)S(1)}, u32[]{:S(2)}, u32[]{:S(2)}) %collective-permute-start.8) | collective-permute-done | bytes 4128 | tf_op jit(solution)/shard_map/ppermute | solution.py:462
  51.2 0.0 copy-start.19
  51.2 0.0 copy-start.4
  51.2 0.0 copy-start.6
  51.2 0.0 copy-start.13
  51.3 0.0 copy-start.15
  51.3 14.8 %shard_map.186.mine_ref = bf16[512,640]{1,0:T(8,128)(2,1)S(1)} custom-call(s32[1]{0:T(128)} %bitcast.core_ref, f32[8,128]{1,0:T(8,128)S(1)} %add.27.sums_ref, bf16[16,16,1280]{2,1,0:T(8,128)(2,1)S(1)} %copy-done.3, bf16[16,16,1280]{2,1,0:T(8,128)(2,1)S(1)} %collective-permute-done.9.theirs_ref, bf16[96,1280]{1,0:T(8,128)(2,1)S(1)} %pad_maximum_fusion.2.rim_mine_ref, ...), custom_call_target="tpu_custom_call" | custom-call | tf_op jit(solution)/shard_map/pallas_call | solution.py:324
  66.1 0.1 collective-permute-start.14
  66.3 3.7 %shard_map.187 = (bf16[1280,640]{1,0:T(8,128)(2,1)S(1)}, bf16[1280,640]{1,0:T(8,128)(2,1)S(1)}, bf16[1280,640]{1,0:T(8,128)(2,1)S(1)}) custom-call(s32[1]{0:T(128)} %bitcast.core_ref, s32[320,1280]{1,0:T(8,128)S(1)} %copy-done.4, f32[16,1280]{1,0:T(8,128)S(1)} %copy-done.13, s32[320,1280]{1,0:T(8,128)S(1)} %copy-done.5, f32[16,1280]{1,0:T(8,128)S(1)} %copy-done.14, ...), custom_call_target="tpu_custom_call" | custom-call | flops 19660800 | bytes 7372800 | tf_op jit(solution)/shard_map/pallas_call | solution.py:190
  70.1 1.2 %shard_map.189.out_weight_ref = bf16[640,1280]{1,0:T(8,128)(2,1)S(1)} custom-call(s32[1]{0:T(128)} %bitcast.core_ref, s32[320,1280]{1,0:T(8,128)S(1)} %copy-done.7, f32[16,1280]{1,0:T(8,128)S(1)} %copy-done.12), custom_call_target="tpu_custom_call" | custom-call | flops 6553600 | bytes 2457600 | tf_op jit(solution)/shard_map/pallas_call | solution.py:211
  71.3 2.2 %shard_map.188 = (bf16[512,640]{1,0:T(8,128)(2,1)S(1)}, bf16[512,640]{1,0:T(8,128)(2,1)S(1)}) custom-call(bf16[256,1280]{1,0:T(8,128)(2,1)S(1)} %pad_maximum_fusion.near_ref, bf16[256,1280]{1,0:T(8,128)(2,1)S(1)} %collective-permute-done.15.far_ref, bf16[1280,640]{1,0:T(8,128)(2,1)S(1)} %get-tuple-element.55.key_ref, ...), custom_call_target="tpu_custom_call" | custom-call | flops 1677721600 | bytes 3276800 | tf_op jit(solution)/shard_map/pallas_call | solution.py:365
  73.6 10.5 %shard_map.190 = (bf16[256,1280]{1,0:T(8,128)(2,1)S(1)}, f32[256,1280]{1,0:T(8,128)S(1)}) custom-call(s32[1]{0:T(128)} %bitcast.core_ref, bf16[512,640]{1,0:T(8,128)(2,1)S(1)} %shard_map.186.mine_ref, bf16[512,640]{1,0:T(8,128)(2,1)S(1)} %collective-permute-done.14.theirs_ref, f32[1,1280]{1,0:T(1,128)S(1)} %broadcast_in_dim.19.gain_ref, ...), custom_call_target="tpu_custom_call" | custom-call | tf_op jit(solution)/shard_map/pallas_call | solution.py:441
  84.1 0.5 collective-permute-start.16
  84.7 1.7 %collective-permute-done.16 = bf16[256,1280]{1,0:T(8,128)(2,1)S(1)} collective-permute-done((bf16[256,1280]{1,0:T(8,128)(2,1)S(1)}, bf16[256,1280]{1,0:T(8,128)(2,1)S(1)}, u32[]{:S(2)}, u32[]{:S(2)}) %collective-permute-start.16) | collective-permute-done | bytes 655392 | tf_op jit(solution)/shard_map/ppermute | solution.py:462
  86.4 1.0 %add_convert_fusion = bf16[256,1280]{1,0:T(8,128)(2,1)} fusion(f32[256,1280]{1,0:T(8,128)S(1)} %get-tuple-element.61, bf16[256,1280]{1,0:T(8,128)(2,1)S(1)} %collective-permute-done.16), kind=kLoop, calls=%fused_computation | loop fusion | flops 983040 | bytes 2621440 | tf_op jit(solution)/shard_map/convert_element_type | solution.py:556
  (53 shorter events, 0.3 us)
Async XLA Ops:
  0.7 1.1 %copy-start.2 = (bf16[16,16,1280]{2,1,0:T(8,128)(2,1)S(1)}, bf16[16,16,1280]{2,1,0:T(8,128)(2,1)}, u32[]{:S(2)}) copy-start(bf16[16,16,1280]{2,1,0:T(8,128)(2,1)} %mine_ref.1) | copy-start | bytes 1966084
  1.7 1.1 %copy-start.9 = (bf16[320,1280]{1,0:T(8,128)(2,1)S(1)}, bf16[320,1280]{1,0:T(8,128)(2,1)}, u32[]{:S(2)}) copy-start(bf16[320,1280]{1,0:T(8,128)(2,1)} %time_ref.1) | copy-start | bytes 2457604
  2.9 1.1 %copy-start.10 = (bf16[16,16,1280]{2,1,0:T(8,128)(2,1)S(1)}, bf16[16,16,1280]{2,1,0:T(8,128)(2,1)}, u32[]{:S(2)}) copy-start(bf16[16,16,1280]{2,1,0:T(8,128)(2,1)} %first_ref.1) | copy-start | bytes 1966084
  4.0 1.1 %copy-start.11 = (bf16[16,16,1280]{2,1,0:T(8,128)(2,1)S(1)}, bf16[16,16,1280]{2,1,0:T(8,128)(2,1)}, u32[]{:S(2)}) copy-start(bf16[16,16,1280]{2,1,0:T(8,128)(2,1)} %normed_ref.1) | copy-start | bytes 1966084
  5.1 4.1 %copy-start.8 = (f32[16,1280]{1,0:T(8,128)S(1)}, f32[16,1280]{1,0:T(8,128)}, u32[]{:S(2)}) copy-start(f32[16,1280]{1,0:T(8,128)} %table_ref.7) | copy-start | bytes 245764
  6.1 11.0 %collective-permute-start.1 = (bf16[16,1280]{1,0:T(8,128)(2,1)S(1)}, bf16[16,1280]{1,0:T(8,128)(2,1)S(1)}, u32[]{:S(2)}, u32[]{:S(2)}) collective-permute-start(bf16[16,1280]{1,0:T(8,128)(2,1)S(1)} %get-tuple-element.35), channel_id=1, source_target_pairs={{0,2},{1,3},{2,0},{3,1},{4,6},{5,7},{6,4},{7,5},{8,10},{9,11},{10,... | collective-permute-start | bytes 122888 | tf_op jit(solution)/shard_map/ppermute | solution.py:462
  9.2 7.9 %collective-permute-start = (f32[8,128]{1,0:T(8,128)S(1)}, f32[8,128]{1,0:T(8,128)S(1)}, u32[]{:S(2)}, u32[]{:S(2)}) collective-permute-start(f32[8,128]{1,0:T(8,128)S(1)} %get-tuple-element.34), channel_id=1, source_target_pairs={{0,1},{1,0},{2,3},{3,2},{4,5},{5,4},{6,7},{7,6},{8,9},{9,8},{10,11... | collective-permute-start | bytes 12296 | tf_op jit(solution)/shard_map/ppermute | solution.py:462
  9.2 5.2 %copy-start = (s32[9,320,1280]{2,1,0:T(8,128)S(1)}, s32[9,320,1280]{2,1,0:T(8,128)}, u32[]{:S(2)}) copy-start(s32[9,320,1280]{2,1,0:T(8,128)} %codes_ref.3) | copy-start | bytes 44236804
  14.4 5.8 %copy-start.1 = (s32[9,320,1280]{2,1,0:T(8,128)S(1)}, s32[9,320,1280]{2,1,0:T(8,128)}, u32[]{:S(2)}) copy-start(s32[9,320,1280]{2,1,0:T(8,128)} %codes_ref.3) | copy-start | bytes 44236804
  17.1 7.5 %collective-permute-start.3 = (bf16[32,1280]{1,0:T(8,128)(2,1)S(1)}, bf16[32,1280]{1,0:T(8,128)(2,1)S(1)}, u32[]{:S(2)}, u32[]{:S(2)}) collective-permute-start(bf16[32,1280]{1,0:T(8,128)(2,1)S(1)} %pad_maximum_fusion.6), channel_id=1, source_target_pairs={{0,4},{1,5},{2,6},{3,7},{4,0},{5,1},{6,2},{7,3},{8,12},{9,13},{10,... | collective-permute-start | bytes 245768 | tf_op jit(solution)/shard_map/ppermute | solution.py:462
  19.8 4.0 %collective-permute-start.2 = (f32[8,128]{1,0:T(8,128)S(1)}, f32[8,128]{1,0:T(8,128)S(1)}, u32[]{:S(2)}, u32[]{:S(2)}) collective-permute-start(f32[8,128]{1,0:T(8,128)S(1)} %add.23), channel_id=1, source_target_pairs={{0,2},{1,3},{2,0},{3,1},{4,6},{5,7},{6,4},{7,5},{8,10},{9,11},{10,... | collective-permute-start | bytes 12296 | tf_op jit(solution)/shard_map/ppermute | solution.py:462
  24.6 6.2 %collective-permute-start.5 = (bf16[64,1280]{1,0:T(8,128)(2,1)S(1)}, bf16[64,1280]{1,0:T(8,128)(2,1)S(1)}, u32[]{:S(2)}, u32[]{:S(2)}) collective-permute-start(bf16[64,1280]{1,0:T(8,128)(2,1)S(1)} %pad_maximum_fusion.3), channel_id=1, source_target_pairs={{0,8},{8,0},{16,24},{24,16},{1,9},{9,1},{17,25},{25,17},{2,10},{10... | collective-permute-start | bytes 491528 | tf_op jit(solution)/shard_map/ppermute | solution.py:462
  26.2 4.5 %collective-permute-start.4 = (f32[8,128]{1,0:T(8,128)S(1)}, f32[8,128]{1,0:T(8,128)S(1)}, u32[]{:S(2)}, u32[]{:S(2)}) collective-permute-start(f32[8,128]{1,0:T(8,128)S(1)} %add.24), channel_id=1, source_target_pairs={{0,4},{1,5},{2,6},{3,7},{4,0},{5,1},{6,2},{7,3},{8,12},{9,13},{10,... | collective-permute-start | bytes 12296 | tf_op jit(solution)/shard_map/ppermute | solution.py:462
  27.2 10.0 %copy-start.3 = (bf16[16,16,1280]{2,1,0:T(8,128)(2,1)S(1)}, bf16[16,16,1280]{2,1,0:T(8,128)(2,1)}, u32[]{:S(2)}) copy-start(bf16[16,16,1280]{2,1,0:T(8,128)(2,1)} %mine_ref.1) | copy-start | bytes 1966084
  27.2 5.2 %collective-permute-start.10 = (bf16[16,1280]{1,0:T(8,128)(2,1)S(1)}, bf16[16,1280]{1,0:T(8,128)(2,1)S(1)}, u32[]{:S(2)}, u32[]{:S(2)}) collective-permute-start(bf16[16,1280]{1,0:T(8,128)(2,1)S(1)} %get-tuple-element.66), channel_id=1, source_target_pairs={{1,2},{3,4},{5,6},{2,1},{4,3},{6,5},{9,10},{11,12},{13,14},{10,9},... | collective-permute-start | bytes 122888 | tf_op jit(solution)/shard_map/ppermute | solution.py:520
  30.8 16.5 %collective-permute-start.7 = (bf16[128,1280]{1,0:T(8,128)(2,1)S(1)}, bf16[128,1280]{1,0:T(8,128)(2,1)S(1)}, u32[]{:S(2)}, u32[]{:S(2)}) collective-permute-start(bf16[128,1280]{1,0:T(8,128)(2,1)S(1)} %pad_maximum_fusion.1), channel_id=1, source_target_pairs={{0,16},{8,24},{16,0},{24,8},{1,17},{9,25},{17,1},{25,9},{2,18},{10... | collective-permute-start | bytes 983048 | tf_op jit(solution)/shard_map/ppermute | solution.py:462
  32.5 9.0 %collective-permute-start.11 = (bf16[32,1280]{1,0:T(8,128)(2,1)S(1)}, bf16[32,1280]{1,0:T(8,128)(2,1)S(1)}, u32[]{:S(2)}, u32[]{:S(2)}) collective-permute-start(bf16[32,1280]{1,0:T(8,128)(2,1)S(1)} %get-tuple-element.67), channel_id=1, source_target_pairs={{0,8},{8,16},{16,24},{1,9},{9,17},{17,25},{2,10},{10,18},{18,26},{... | collective-permute-start | bytes 245768 | tf_op jit(solution)/shard_map/ppermute | solution.py:522
  35.9 6.3 %collective-permute-start.12 = (bf16[32,1280]{1,0:T(8,128)(2,1)S(1)}, bf16[32,1280]{1,0:T(8,128)(2,1)S(1)}, u32[]{:S(2)}, u32[]{:S(2)}) collective-permute-start(bf16[32,1280]{1,0:T(8,128)(2,1)S(1)} %get-tuple-element.68), channel_id=1, source_target_pairs={{8,0},{16,8},{24,16},{9,1},{17,9},{25,17},{10,2},{18,10},{26,18},{... | collective-permute-start | bytes 245768 | tf_op jit(solution)/shard_map/ppermute | solution.py:525
  37.2 14.0 %collective-permute-start.9 = (bf16[16,16,1280]{2,1,0:T(8,128)(2,1)S(1)}, bf16[16,16,1280]{2,1,0:T(8,128)(2,1)S(1)}, u32[]{:S(2)}, u32[]{:S(2)}) collective-permute-start(bf16[16,16,1280]{2,1,0:T(8,128)(2,1)S(1)} %copy-done.3), channel_id=1, source_target_pairs={{0,1},{1,0},{2,3},{3,2},{4,5},{5,4},{6,7},{7,6},{8,9},{9,8},{10,11... | collective-permute-start | bytes 1966088 | tf_op jit(solution)/shard_map/ppermute | solution.py:462
  39.2 8.2 %collective-permute-start.6 = (f32[8,128]{1,0:T(8,128)S(1)}, f32[8,128]{1,0:T(8,128)S(1)}, u32[]{:S(2)}, u32[]{:S(2)}) collective-permute-start(f32[8,128]{1,0:T(8,128)S(1)} %add.25), channel_id=1, source_target_pairs={{0,8},{8,0},{16,24},{24,16},{1,9},{9,1},{17,25},{25,17},{2,10},{10... | collective-permute-start | bytes 12296 | tf_op jit(solution)/shard_map/ppermute | solution.py:462
  42.2 5.9 %copy-start.16 = (f32[1280]{0:T(1024)S(1)}, f32[1280]{0:T(1024)}, u32[]{:S(2)}) copy-start(f32[1280]{0:T(1024)} %param.24) | copy-start | bytes 15364
  42.3 5.9 %copy-start.17 = (f32[1280]{0:T(1024)S(1)}, f32[1280]{0:T(1024)}, u32[]{:S(2)}) copy-start(f32[1280]{0:T(1024)} %param.25) | copy-start | bytes 15364
  42.3 5.9 %copy-start.18 = (f32[1280]{0:T(1024)S(1)}, f32[1280]{0:T(1024)}, u32[]{:S(2)}) copy-start(f32[1280]{0:T(1024)} %param.28) | copy-start | bytes 15364
  42.3 8.9 %collective-permute-start.13 = (bf16[96,1280]{1,0:T(8,128)(2,1)S(1)}, bf16[96,1280]{1,0:T(8,128)(2,1)S(1)}, u32[]{:S(2)}, u32[]{:S(2)}) collective-permute-start(bf16[96,1280]{1,0:T(8,128)(2,1)S(1)} %pad_maximum_fusion.2.rim_mine_ref), channel_id=1, source_target_pairs={{0,1},{1,0},{2,3},{3,2},{4,5},{5,4},{6,7},{7,6},{8,9},{9,8},{10,11... | collective-permute-start | bytes 737288 | tf_op jit(solution)/shard_map/ppermute | solution.py:462
  47.4 23.9 %collective-permute-start.15 = (bf16[256,1280]{1,0:T(8,128)(2,1)S(1)}, bf16[256,1280]{1,0:T(8,128)(2,1)S(1)}, u32[]{:S(2)}, u32[]{:S(2)}) collective-permute-start(bf16[256,1280]{1,0:T(8,128)(2,1)S(1)} %pad_maximum_fusion.near_ref), channel_id=1, source_target_pairs={{0,1},{1,0},{2,3},{3,2},{4,5},{5,4},{6,7},{7,6},{8,9},{9,8},{10,11... | collective-permute-start | bytes 1966088 | tf_op jit(solution)/shard_map/ppermute | solution.py:462
  47.5 3.6 %collective-permute-start.8 = (f32[8,128]{1,0:T(8,128)S(1)}, f32[8,128]{1,0:T(8,128)S(1)}, u32[]{:S(2)}, u32[]{:S(2)}) collective-permute-start(f32[8,128]{1,0:T(8,128)S(1)} %add.26), channel_id=1, source_target_pairs={{0,16},{8,24},{16,0},{24,8},{1,17},{9,25},{17,1},{25,9},{2,18},{10... | collective-permute-start | bytes 12296 | tf_op jit(solution)/shard_map/ppermute | solution.py:462
  51.2 15.0 %copy-start.19 = (f32[1280]{0:T(1024)S(1)}, f32[1280]{0:T(1024)}, u32[]{:S(2)}) copy-start(f32[1280]{0:T(1024)} %param.29) | copy-start | bytes 15364
  51.2 15.0 %copy-start.4 = (s32[320,1280]{1,0:T(8,128)S(1)}, s32[320,1280]{1,0:T(8,128)}, u32[]{:S(2)}) copy-start(s32[320,1280]{1,0:T(8,128)} %refs_0_.1) | copy-start | bytes 4915204
  51.2 15.0 %copy-start.5 = (s32[320,1280]{1,0:T(8,128)S(1)}, s32[320,1280]{1,0:T(8,128)}, u32[]{:S(2)}) copy-start(s32[320,1280]{1,0:T(8,128)} %refs_2_.1) | copy-start | bytes 4915204
  51.2 15.0 %copy-start.6 = (s32[320,1280]{1,0:T(8,128)S(1)}, s32[320,1280]{1,0:T(8,128)}, u32[]{:S(2)}) copy-start(s32[320,1280]{1,0:T(8,128)} %refs_4_.1) | copy-start | bytes 4915204
  51.2 15.0 %copy-start.13 = (f32[16,1280]{1,0:T(8,128)S(1)}, f32[16,1280]{1,0:T(8,128)}, u32[]{:S(2)}) copy-start(f32[16,1280]{1,0:T(8,128)} %refs_1_.2) | copy-start | bytes 245764
  51.3 15.0 %copy-start.14 = (f32[16,1280]{1,0:T(8,128)S(1)}, f32[16,1280]{1,0:T(8,128)}, u32[]{:S(2)}) copy-start(f32[16,1280]{1,0:T(8,128)} %refs_3_.1) | copy-start | bytes 245764
  51.3 15.0 %copy-start.15 = (f32[16,1280]{1,0:T(8,128)S(1)}, f32[16,1280]{1,0:T(8,128)}, u32[]{:S(2)}) copy-start(f32[16,1280]{1,0:T(8,128)} %refs_5_.1) | copy-start | bytes 245764
  66.1 7.4 %collective-permute-start.14 = (bf16[512,640]{1,0:T(8,128)(2,1)S(1)}, bf16[512,640]{1,0:T(8,128)(2,1)S(1)}, u32[]{:S(2)}, u32[]{:S(2)}) collective-permute-start(bf16[512,640]{1,0:T(8,128)(2,1)S(1)} %shard_map.186.mine_ref), channel_id=1, source_target_pairs={{0,1},{1,0},{2,3},{3,2},{4,5},{5,4},{6,7},{7,6},{8,9},{9,8},{10,11... | collective-permute-start | bytes 1966088 | tf_op jit(solution)/shard_map/ppermute | solution.py:462
  66.3 3.8 %copy-start.7 = (s32[320,1280]{1,0:T(8,128)S(1)}, s32[320,1280]{1,0:T(8,128)}, u32[]{:S(2)}) copy-start(s32[320,1280]{1,0:T(8,128)} %refs_0_.2) | copy-start | bytes 4915204
  66.3 3.8 %copy-start.12 = (f32[16,1280]{1,0:T(8,128)S(1)}, f32[16,1280]{1,0:T(8,128)}, u32[]{:S(2)}) copy-start(f32[16,1280]{1,0:T(8,128)} %refs_1_.3) | copy-start | bytes 245764
  84.1 2.3 %collective-permute-start.16 = (bf16[256,1280]{1,0:T(8,128)(2,1)S(1)}, bf16[256,1280]{1,0:T(8,128)(2,1)S(1)}, u32[]{:S(2)}, u32[]{:S(2)}) collective-permute-start(bf16[256,1280]{1,0:T(8,128)(2,1)S(1)} %get-tuple-element.62), channel_id=1, source_target_pairs={{0,1},{1,0},{2,3},{3,2},{4,5},{5,4},{6,7},{7,6},{8,9},{9,8},{10,11... | collective-permute-start | bytes 1966088 | tf_op jit(solution)/shard_map/ppermute | solution.py:462

commit v3 on v2

--- a/solution.py
+++ b/solution.py
@@ -66,7 +66,7 @@
     squares = jnp.sum(image * image, axis=0, keepdims=True)
     row8 = iota((8, channels), 0)
     both = jnp.where(row8 == 0, sums, jnp.where(row8 == 1, squares, 0.0))
-    sums_ref[...] = dot(both, group_matrix(channels, False), precision=lax.Precision.HIGHEST)
+    sums_ref[...] = dot(both, group_matrix(channels, False), precision=lax.Precision.HIGHEST)[0:2]
 
     cells_first = first_ref[...].reshape(cells, channels)
     row = iota((height, cells), 0)
@@ -108,7 +108,7 @@
         in_specs=[small, small] + [whole] * 4,
         out_specs=[whole] * 4,
         out_shape=[
-            jax.ShapeDtypeStruct((8, LANES), F32),
+            jax.ShapeDtypeStruct((2, LANES), F32),
             jax.ShapeDtypeStruct((4, height, channels), BF),
             jax.ShapeDtypeStruct((pools, channels), BF),
             jax.ShapeDtypeStruct((8, channels), F32),
@@ -178,7 +178,7 @@
         ),
         out_shape=jax.ShapeDtypeStruct((codes.shape[0], 4 * words, half), BF),
         input_output_aliases={3: 0} if into else {},
-        compiler_params=params(8),
+        compiler_params=params(34),
         cost_estimate=decode_cost((stop - start) * 4 * words * half),
     )(core, codes, table, *into)
 
@@ -238,7 +238,10 @@
 
     @pl.when(tap == 0)
     def _():
-        spread = dot(sums_ref[...], group_matrix(channels, True), precision=lax.Precision.HIGHEST)
+        parts = rim_theirs_ref[0:16, channels:].astype(F32)
+        sums = sums_ref[...] + parts[0:2] + parts[2:4] + parts[4:6]
+        sums = jnp.concatenate([sums, jnp.zeros((6, LANES), F32)], axis=0)
+        spread = dot(sums, group_matrix(channels, True), precision=lax.Precision.HIGHEST)
         average = spread[0:1] / members
         mean_square = spread[1:2] / members
         scale = lax.rsqrt(mean_square - average * average + 1e-05) * gain_ref[...]
@@ -327,11 +330,11 @@
             num_scalar_prefetch=1,
             grid=(9,),
             in_specs=[
-                whole(8, LANES),
+                whole(2, LANES),
                 whole(height, across, channels),
                 whole(height, across, channels),
                 whole(rim_rows, channels),
-                whole(rim_rows, channels),
+                whole(rim_rows, channels + LANES),
                 whole(1, channels),
                 whole(1, channels),
                 part(1, half),
@@ -351,32 +354,30 @@
     )(core, sums, mine, theirs, rim_mine, rim_theirs, gain, shift, bias, time_shift, weights)
 
 
-def stale_kernel(near_ref, far_ref, key_ref, value_ref, keys_ref, values_ref):
-    rows = near_ref.shape[0]
-    for at, ref in ((0, near_ref), (rows, far_ref)):
-        keys_ref[at : at + rows] = dot(ref[...], key_ref[...]).astype(BF)
-        values_ref[at : at + rows] = dot(ref[...], value_ref[...]).astype(BF)
-
-
-def stale_pass(near, far, key_weight, value_weight):
+def stale_kernel(near_ref, key_ref, value_ref, keys_ref, values_ref):
+    keys_ref[...] = dot(near_ref[...], key_ref[...]).astype(BF)
+    values_ref[...] = dot(near_ref[...], value_ref[...]).astype(BF)
+
+
+def stale_pass(near, key_weight, value_weight):
     rows, channels = near.shape
     half = key_weight.shape[1]
     whole = pl.BlockSpec(memory_space=pltpu.VMEM)
     return pl.pallas_call(
         stale_kernel,
-        in_specs=[whole] * 4,
+        in_specs=[whole] * 3,
         out_specs=[whole] * 2,
-        out_shape=[jax.ShapeDtypeStruct((2 * rows, half), BF)] * 2,
-        compiler_params=params(20),
+        out_shape=[jax.ShapeDtypeStruct((rows, half), BF)] * 2,
+        compiler_params=params(16),
         cost_estimate=pl.CostEstimate(
-            flops=8 * rows * channels * half, bytes_accessed=4 * channels * half, transcendentals=0
+            flops=4 * rows * channels * half, bytes_accessed=4 * channels * half, transcendentals=0
         ),
-    )(near, far, key_weight, value_weight)
+    )(near, key_weight, value_weight)
 
 
 def attention_kernel(
-    core_ref, mine_ref, theirs_ref, gain_ref, query_ref, key_ref, value_ref, stale_keys_ref, stale_values_ref,
-    out_weight_ref, send_ref, keep_ref, normed_ref, q_ref, k_ref, v_ref, mixed_ref,
+    core_ref, mine_ref, theirs_ref, gain_ref, query_ref, key_ref, value_ref, near_keys_ref, near_values_ref,
+    far_ref, out_weight_ref, send_ref, keep_ref, normed_ref, q_ref, k_ref, v_ref, mixed_ref, stale_keys_ref, stale_values_ref,
 ):
     rows, half = mine_ref.shape
     cells = rows // 2
@@ -399,6 +400,11 @@
             normed_ref[side * cells : (side + 1) * cells, k : k + 256] = dot(
                 normed[:, k : k + 256], matrix
             ).astype(BF)
+    near_rows = near_keys_ref.shape[0]
+    stale_keys_ref[:near_rows] = near_keys_ref[...]
+    stale_values_ref[:near_rows] = near_values_ref[...]
+    stale_keys_ref[near_rows:] = dot(far_ref[...], key_ref[...]).astype(BF)
+    stale_values_ref[near_rows:] = dot(far_ref[...], value_ref[...]).astype(BF)
     normed = normed_ref[...]
     q_ref[...] = (dot(normed, query_ref[...]).astype(BF) * BF(1.0 / math.sqrt(HEAD_DIM))).astype(BF)
     k_ref[...] = dot(normed, key_ref[...]).astype(BF)
@@ -432,7 +438,7 @@
     keep_ref[...] += dot(mixture[:cells], out_weight_ref[...])
 
 
-def attention_pass(core, mine, theirs, gain, query, key, value, stale_keys, stale_values, out_weight):
+def attention_pass(core, mine, theirs, gain, query, key, value, near_keys, near_values, far, out_weight):
     rows, half = mine.shape
     channels = 2 * half
     cells = rows // 2
@@ -440,7 +446,7 @@
     small = pl.BlockSpec(memory_space=pltpu.SMEM)
     return pl.pallas_call(
         attention_kernel,
-        in_specs=[small] + [whole] * 9,
+        in_specs=[small] + [whole] * 10,
         out_specs=[whole] * 2,
         out_shape=[
             jax.ShapeDtypeStruct((cells, channels), BF),
@@ -452,9 +458,11 @@
             pltpu.VMEM((rows, half), BF),
             pltpu.VMEM((rows, half), BF),
             pltpu.VMEM((rows, half), BF),
+            pltpu.VMEM((2 * far.shape[0], half), BF),
+            pltpu.VMEM((2 * far.shape[0], half), BF),
         ],
         compiler_params=params(28),
-    )(core, mine, theirs, gain, query, key, value, stale_keys, stale_values, out_weight)
+    )(core, mine, theirs, gain, query, key, value, near_keys, near_values, far, out_weight)
 
 
 def swap(values, axis, step):
@@ -464,11 +472,21 @@
 
 def steps_over(axis, first):
     count = lax.axis_size(axis)
-    steps = []
-    while first < count:
-        steps.append((axis, first))
-        first *= 2
-    return steps
+    return [(axis, 2 * m - 1) for m in (1 << k for k in range(count.bit_length() - 1)) if m >= first]
+
+
+def split_sums(sums):
+    high = lax.reduce_precision(sums, 8, 7)
+    rest = sums - high
+    middle = lax.reduce_precision(rest, 8, 7)
+    low = rest - middle
+    parts = jnp.concatenate([high, middle, low, jnp.zeros((10, LANES), F32)])
+    return parts.astype(BF)
+
+
+def join_sums(parts):
+    parts = parts.astype(F32)
+    return parts[0:2] + parts[2:4] + parts[4:6]
 
 
 def tie(first, second):
@@ -505,52 +523,73 @@
 
     sums, edges, pooled, time_shift = first_pass(core, timestep, image, stale_first, stale_normed, time_weight)
 
-    between = [(i, i + 1) for i in range(1, cols - 1, 2)]
-    sum_steps = steps_over("col", 1) + steps_over("row", 1)
-    pool_steps = steps_over("col", 2) + steps_over("row", 1)
-    chunks = [(0, 2), (2, 4), (4, 6), (6, 9)]
-    slots = max(len(sum_steps), len(pool_steps), len(chunks))
+    row_at = lax.axis_index("row")
+    col_at = lax.axis_index("col")
+    beside = jnp.where(core[0] == 0, col_at - 1, col_at + 1)
+    hops = steps_over("col", 2) + steps_over("row", 1)
+    chunks = [(0, 2), (2, 6), (6, 9)]
+    outer = jnp.zeros_like(edges[0])
+    above = below = jnp.zeros((height + across, channels), BF)
+    near = pooled
     weights = None
-    near = pooled
     codes = codes_first
-    for slot in range(slots):
+    for at, (axis, step) in enumerate(hops):
+        last = at == len(hops) - 1
         if weights is not None:
             (sums, near), weights = tie((sums, near), weights)
-        if slot == 0:
-            outer = lax.ppermute(edges[0], "col", between + [(j, i) for i, j in between])
-        elif slot == 1:
-            above = lax.ppermute(
-                jnp.concatenate([edges[3], outer]), "row", [(i, i + 1) for i in range(rows - 1)]
+        if axis == "col":
+            border = edges[0]
+        else:
+            partner = row_at ^ step
+            border = jnp.concatenate([jnp.where(partner > row_at, edges[3], edges[2]), outer])
+        parts = jnp.pad(split_sums(sums), ((0, border.shape[0] - across), (0, 0)))
+        border = jnp.concatenate([border, parts], axis=1)
+        if last:
+            got_border = swap(border, axis, step)
+            final = (near, axis, step)
+        else:
+            payload = jnp.concatenate([border, jnp.pad(near, ((0, 0), (0, LANES)))])
+            got = swap(payload, axis, step)
+            got_border = got[: border.shape[0]]
+        if at == 1:
+            partner_image = swap(image, "col", 1)
+        if at < len(chunks):
+            _, codes = tie((sums, near), codes)
+            weights = decode_taps(core, codes, table_first, weights, *chunks[at])
+        elif at == len(chunks):
+            _, (query_codes, key_codes, value_codes) = tie(
+                (sums, near), (query_codes, key_codes, value_codes)
             )
-            below = lax.ppermute(
-                jnp.concatenate([edges[2], outer]), "row", [(i + 1, i) for i in range(rows - 1)]
+            query, key, value = decode_columns(
+                core, query_codes, query_table, key_codes, key_table, value_codes, value_table
             )
-        elif slot == 2:
-            rim = jnp.concatenate([above, below, outer, edges[1]])
-            partner_rim = swap(rim, "col", 1)
-        elif slot == 3:
-            partner_image = swap(image, "col", 1)
-        next_sums = sums + swap(sums, *sum_steps[slot]) if slot < len(sum_steps) else sums
-        next_near = jnp.concatenate([near, swap(near, *pool_steps[slot])]) if slot < len(pool_steps) else near
-        if slot < len(chunks):
-            _, codes = tie((sums, near), codes)
-            weights = decode_taps(core, codes, table_first, weights, *chunks[slot])
-        sums = next_sums
-        near = next_near
-    far = swap(near, "col", 1)
-    query, key, value = decode_columns(
-        core, query_codes, query_table, key_codes, key_table, value_codes, value_table
-    )
+            weights, key = tie(weights, key)
+        sums = sums + join_sums(got_border[:across, channels:])
+        cells_got = got_border[:, :channels]
+        if axis == "col":
+            outer = jnp.where((col_at ^ step) == beside, cells_got, outer)
+        else:
+            above = jnp.where(partner == row_at - 1, cells_got, above)
+            below = jnp.where(partner == row_at + 1, cells_got, below)
+        if not last:
+            near = jnp.concatenate([near, got[border.shape[0] :, :channels]])
+    (above, below, sums), weights = tie((above, below, sums), weights)
+    rim = jnp.concatenate([above, below, outer, edges[1]])
+    parts = jnp.pad(split_sums(sums), ((0, rim.shape[0] - across), (0, 0)))
+    partner_rim = swap(jnp.concatenate([rim, parts], axis=1), "col", 1)
+    near = jnp.concatenate([near, swap(*final)])
+
     residual = convolve(
         core, sums, image, partner_image, rim, partner_rim, gain_first[None], shift_first[None],
         bias_first[None], time_shift, weights, members,
     )
+    (residual, near, out_codes), _ = tie((residual, near, out_codes), residual)
     partner_residual = swap(residual, "col", 1)
-    (residual, out_codes), _ = tie((residual, out_codes), residual)
+    far = swap(near, "col", 1)
     out_weight = decode_rows(core, out_codes, out_table)
-    stale_keys, stale_values = stale_pass(near, far, key, value)
+    near_keys, near_values = stale_pass(near, key, value)
     send, keep = attention_pass(
-        core, residual, partner_residual, attn_gain[None], query, key, value, stale_keys, stale_values, out_weight
+        core, residual, partner_residual, attn_gain[None], query, key, value, near_keys, near_values, far, out_weight
     )
     output = keep + swap(send, "col", 1).astype(F32)
     return output.astype(BF).reshape(height, across, channels)

time: 87.9 us -> 95.7 us (1.089)
  local copies, waits for them, and re-layouts: 9.71 us -> 28.2 us
  starting transfers between devices: 22.6 us -> 11 us
  waiting for transfers between devices: 7.16 us -> 3.89 us
  Pallas kernels: 45.7 us -> 47.9 us
  other arithmetic: 1.1 us -> 3.03 us
    unnamed x40 -> x48, local copies, waits for them, and re-layouts: 9.68 us -> 28.2 us
    ppermute x14 -> x10, starting transfers between devices: 17.1 us -> 11 us  [swap(): return lax.ppermute(values, axis, [(i, i ^ step) for i in range(count)])]
    ppermute x3 -> x0, starting transfers between devices: 5.49 us -> none  [the longest x1 3.4 us: on_device(): lax.ppermute(jnp.concatenate([edges[3], outer]), 'row', [(i, i + 1) for i...]
    pallas_call x4 -> x3, Pallas kernels: 12 us -> 14.8 us  [decode_taps(): pl.pallas_call(lambda core_ref, codes_ref, table_ref, *refs: decode_into(...]
    ppermute x14 -> x10, waiting for transfers between devices: 6.45 us -> 3.89 us  [swap(): return lax.ppermute(values, axis, [(i, i ^ step) for i in range(count)])]
  transfers between devices with their start and end apart: 17 -> 10, of which waited for: 5 -> 2; matrix products, arithmetic and copies ran while one was open for 0% -> 1% of each run, Pallas kernels for 39% -> 22%
where the time goes in v3:
time: 95.7 us; the launch traced here: 95.2 us
  Pallas kernels  47.9 us (50%)
  local copies, waits for them, and re-layouts  28.2 us (29%)
  starting transfers between devices  11 us (11%)
  waiting for transfers between devices  3.89 us (4%)
  other arithmetic  3.03 us (3%)
  between operations  1.11 us (1%)
    unnamed x48, local copies, waits for them, and re-layouts  28.2 us
    pallas_call x3, Pallas kernels, decode_taps(): pl.pallas_call(lambda core_ref, codes_ref, table_ref, *refs: decode_into(...  14.8 us
    pallas_call x1, Pallas kernels, convolve(): pl.pallas_call(functools.partial(conv_kernel, members=members), grid_spec...  14.8 us
    pallas_call x1, Pallas kernels, attention_pass(): pl.pallas_call(attention_kernel, in_specs=[small] + [whole] * 10, out_spe...  11.1 us
    ppermute x10, starting transfers between devices, swap(): return lax.ppermute(values, axis, [(i, i ^ step) for i in range(count)])  11 us
    ppermute x10, waiting for transfers between devices, swap(): return lax.ppermute(values, axis, [(i, i ^ step) for i in range(count)])  3.89 us
    pallas_call x1, Pallas kernels, decode_columns(): pl.pallas_call(functools.partial(decode_kernel, count=count, block=64), g...  3.72 us
  transfers between devices with their start and end apart: 10, of which 2 were waited for; matrix products, arithmetic and copies ran while one was open for 1% of the time, Pallas kernels for 22%

profile of v3, /device:TPU:0, one launch (start us, length us, event | category | flops | bytes accessed | tf_op | source)
XLA Modules:
  0.0 95.2 jit_solution(6484559916048570605)
XLA Ops:
  0.7 0.0 copy-start.4
  0.7 1.1 %copy-done.4 = bf16[16,16,1280]{2,1,0:T(8,128)(2,1)S(1)} copy-done((bf16[16,16,1280]{2,1,0:T(8,128)(2,1)S(1)}, bf16[16,16,1280]{2,1,0:T(8,128)(2,1)}, u32[]{:S(2)}) %copy-start.4) | copy-done | bytes 655384
  1.8 1.1 %copy-done.10 = bf16[320,1280]{1,0:T(8,128)(2,1)S(1)} copy-done((bf16[320,1280]{1,0:T(8,128)(2,1)S(1)}, bf16[320,1280]{1,0:T(8,128)(2,1)}, u32[]{:S(2)}) %copy-start.10) | copy-done | bytes 819224
  2.9 1.1 %copy-done.12 = bf16[16,16,1280]{2,1,0:T(8,128)(2,1)S(1)} copy-done((bf16[16,16,1280]{2,1,0:T(8,128)(2,1)S(1)}, bf16[16,16,1280]{2,1,0:T(8,128)(2,1)}, u32[]{:S(2)}) %copy-start.12) | copy-done | bytes 655384
  4.0 1.1 %copy-done.13 = bf16[16,16,1280]{2,1,0:T(8,128)(2,1)S(1)} copy-done((bf16[16,16,1280]{2,1,0:T(8,128)(2,1)S(1)}, bf16[16,16,1280]{2,1,0:T(8,128)(2,1)}, u32[]{:S(2)}) %copy-start.13) | copy-done | bytes 655384
  5.1 1.0 %shard_map.181 = (f32[2,128]{1,0:T(2,128)S(1)}, bf16[4,16,1280]{2,1,0:T(8,128)(2,1)S(1)}, bf16[16,1280]{1,0:T(8,128)(2,1)S(1)}, f32[8,1280]{1,0:T(8,128)S(1)}) custom-call(s32[1]{0:T(128)} %bitcast.core_ref, s32[1]{0:T(128)S(6)} %copy.24.step_ref, bf16[16,16,1280]{2,1,0:T(8,128)(2,1)S(1)} %copy-done.4, bf16[16,16,1280]{2,1,0:T(8,128)(2,1)S(1)} %copy-done.12, ...), custom_call_target="tpu_custom_call" | custom-call | tf_op jit(solution)/shard_map/pallas_call | solution.py:106
  6.2 2.5 %collective-permute-start = (bf16[32,1408]{1,0:T(8,128)(2,1)S(1)}, bf16[32,1408]{1,0:T(8,128)(2,1)S(1)}, u32[]{:S(2)}, u32[]{:S(2)}) collective-permute-start(bf16[32,1408]{1,0:T(8,128)(2,1)S(1)} %fusion.13), channel_id=1, source_target_pairs={{0,3},{1,2},{2,1},{3,0},{4,7},{5,6},{6,5},{7,4},{8,11},{9,10},{10,... | collective-permute-start | bytes 270344 | tf_op jit(solution)/shard_map/ppermute | solution.py:470
  8.7 3.7 %shard_map.182.refs_0_ = bf16[9,1280,640]{2,1,0:T(8,128)(2,1)S(1)} custom-call(s32[1]{0:T(128)} %bitcast.core_ref, s32[9,320,1280]{2,1,0:T(8,128)} %codes_ref.2, f32[16,1280]{1,0:T(8,128)S(1)} %copy-done.11), custom_call_target="tpu_custom_call" | custom-call | flops 13107200 | bytes 4915200 | tf_op jit(solution)/shard_map/pallas_call | solution.py:167
  12.4 5.2 %copy-done = bf16[9,1280,640]{2,1,0:T(8,128)(2,1)} copy-done((bf16[9,1280,640]{2,1,0:T(8,128)(2,1)}, bf16[9,1280,640]{2,1,0:T(8,128)(2,1)S(1)}, u32[]{:S(2)}) %copy-start) | copy-done | bytes 14745624
  17.6 0.0 collective-permute-done
  17.7 2.8 %collective-permute-start.1 = (bf16[48,1408]{1,0:T(8,128)(2,1)S(1)}, bf16[48,1408]{1,0:T(8,128)(2,1)S(1)}, u32[]{:S(2)}, u32[]{:S(2)}) collective-permute-start(bf16[48,1408]{1,0:T(8,128)(2,1)S(1)} %fusion.11), channel_id=1, source_target_pairs={{0,7},{1,6},{2,5},{3,4},{4,3},{5,2},{6,1},{7,0},{8,15},{9,14},{10,... | collective-permute-start | bytes 405512 | tf_op jit(solution)/shard_map/ppermute | solution.py:470
  20.5 5.2 %copy-done.1 = bf16[9,1280,640]{2,1,0:T(8,128)(2,1)S(1)} copy-done((bf16[9,1280,640]{2,1,0:T(8,128)(2,1)S(1)}, bf16[9,1280,640]{2,1,0:T(8,128)(2,1)}, u32[]{:S(2)}) %copy-start.1) | copy-done | bytes 14745624
  25.7 6.2 %shard_map.183.refs_0_ = bf16[9,1280,640]{2,1,0:T(8,128)(2,1)S(1)} custom-call(s32[1]{0:T(128)} %bitcast.core_ref, s32[9,320,1280]{2,1,0:T(8,128)} %codes_ref.2, f32[16,1280]{1,0:T(8,128)S(1)} %copy-done.11, bf16[9,1280,640]{2,1,0:T(8,128)(2,1)S(1)} %copy-done.1), custom_call_target="tpu_custom_call", output_to_operand_aliasing={{}: (3, {})} | custom-call | flops 26214400 | bytes 9830400 | tf_op jit(solution)/shard_map/pallas_call | solution.py:167
  32.0 0.0 copy-start.5
  32.1 0.0 copy-start.20
  32.1 0.0 copy-start.21
  32.1 0.0 copy-start.22
  32.1 0.0 copy-start.15
  32.1 0.0 copy-start.16
  32.1 0.0 copy-start.17
  32.1 1.6 %collective-permute-start.2 = (bf16[96,1408]{1,0:T(8,128)(2,1)S(1)}, bf16[96,1408]{1,0:T(8,128)(2,1)S(1)}, u32[]{:S(2)}, u32[]{:S(2)}) collective-permute-start(bf16[96,1408]{1,0:T(8,128)(2,1)S(1)} %fusion.5), channel_id=1, source_target_pairs={{0,8},{8,0},{16,24},{24,16},{1,9},{9,1},{17,25},{25,17},{2,10},{10... | collective-permute-start | bytes 811016 | tf_op jit(solution)/shard_map/ppermute | solution.py:470
  33.7 5.0 %shard_map.184.weight_ref = bf16[9,1280,640]{2,1,0:T(8,128)(2,1)S(1)} custom-call(s32[1]{0:T(128)} %bitcast.core_ref, s32[9,320,1280]{2,1,0:T(8,128)} %codes_ref.2, f32[16,1280]{1,0:T(8,128)S(1)} %copy-done.11, bf16[9,1280,640]{2,1,0:T(8,128)(2,1)S(1)} %shard_map.183.refs_0_), custom_call_target="tpu_custom_call", output_to_operand_aliasing={{}: (3, {})} | custom-call | flops 19660800 | bytes 7372800 | tf_op jit(solution)/shard_map/pallas_call | solution.py:167
  38.7 5.2 %copy-done.2 = bf16[9,1280,640]{2,1,0:T(8,128)(2,1)} copy-done((bf16[9,1280,640]{2,1,0:T(8,128)(2,1)}, bf16[9,1280,640]{2,1,0:T(8,128)(2,1)S(1)}, u32[]{:S(2)}) %copy-start.2) | copy-done | bytes 14745624
  44.0 0.0 collective-permute-done.2
  44.0 0.8 pad_maximum_fusion.1
  44.8 1.6 %collective-permute-start.3 = (bf16[32,1408]{1,0:T(8,128)(2,1)S(1)}, bf16[32,1408]{1,0:T(8,128)(2,1)S(1)}, u32[]{:S(2)}, u32[]{:S(2)}) collective-permute-start(bf16[32,1408]{1,0:T(8,128)(2,1)S(1)} %fusion.12), channel_id=1, source_target_pairs={{0,24},{8,16},{16,8},{24,0},{1,25},{9,17},{17,9},{25,1},{2,26},{10... | collective-permute-start | bytes 270344 | tf_op jit(solution)/shard_map/ppermute | solution.py:470
  46.5 1.5 %collective-permute-start.6 = (bf16[128,1280]{1,0:T(8,128)(2,1)}, bf16[128,1280]{1,0:T(8,128)(2,1)S(1)}, u32[]{:S(2)}, u32[]{:S(2)}) collective-permute-start(bf16[128,1280]{1,0:T(8,128)(2,1)} %pad_maximum_fusion.1), channel_id=1, source_target_pairs={{0,24},{8,16},{16,8},{24,0},{1,25},{9,17},{17,9},{25,1},{2,26},{10... | collective-permute-start | bytes 983048 | tf_op jit(solution)/shard_map/ppermute | solution.py:470
  48.0 0.0 copy-start.7
  48.0 1.4 %copy-done.7 = s32[320,1280]{1,0:T(8,128)S(1)} copy-done((s32[320,1280]{1,0:T(8,128)S(1)}, s32[320,1280]{1,0:T(8,128)}, u32[]{:S(2)}) %copy-start.7) | copy-done | bytes 1638424
  49.4 1.4 %copy-done.8 = s32[320,1280]{1,0:T(8,128)S(1)} copy-done((s32[320,1280]{1,0:T(8,128)S(1)}, s32[320,1280]{1,0:T(8,128)}, u32[]{:S(2)}) %copy-start.8) | copy-done | bytes 1638424
  50.9 3.7 %shard_map.185 = (bf16[1280,640]{1,0:T(8,128)(2,1)S(1)}, bf16[1280,640]{1,0:T(8,128)(2,1)S(1)}, bf16[1280,640]{1,0:T(8,128)(2,1)S(1)}) custom-call(s32[1]{0:T(128)} %bitcast.core_ref, s32[320,1280]{1,0:T(8,128)S(1)} %copy-done.6, f32[16,1280]{1,0:T(8,128)S(1)} %copy-done.15, s32[320,1280]{1,0:T(8,128)S(1)} %copy-done.7, f32[16,1280]{1,0:T(8,128)S(1)} %copy-done.16, ...), custom_call_target="tpu_custom_call" | custom-call | flops 19660800 | bytes 7372800 | tf_op jit(solution)/shard_map/pallas_call | solution.py:190
  54.6 0.9 select_select_fusion
  55.6 0.3 collective-permute-start.5
  55.9 1.9 %collective-permute-done.6 = bf16[128,1280]{1,0:T(8,128)(2,1)S(1)} collective-permute-done((bf16[128,1280]{1,0:T(8,128)(2,1)}, bf16[128,1280]{1,0:T(8,128)(2,1)S(1)}, u32[]{:S(2)}, u32[]{:S(2)}) %collective-permute-start.6) | collective-permute-done | bytes 327712 | tf_op jit(solution)/shard_map/ppermute | solution.py:470
  57.8 0.0 collective-permute-done.4.theirs_ref
  57.8 0.0 collective-permute-done.5.rim_theirs_ref
  57.8 5.2 %copy-done.3 = bf16[9,1280,640]{2,1,0:T(8,128)(2,1)S(1)} copy-done((bf16[9,1280,640]{2,1,0:T(8,128)(2,1)S(1)}, bf16[9,1280,640]{2,1,0:T(8,128)(2,1)}, u32[]{:S(2)}) %copy-start.3) | copy-done | bytes 14745624
  63.0 14.8 %shard_map.186.mine_ref = bf16[512,640]{1,0:T(8,128)(2,1)S(1)} custom-call(s32[1]{0:T(128)} %bitcast.core_ref, f32[2,128]{1,0:T(2,128)S(1)} %fusion.20.sums_ref, bf16[16,16,1280]{2,1,0:T(8,128)(2,1)S(1)} %copy-done.5, bf16[16,16,1280]{2,1,0:T(8,128)(2,1)S(1)} %collective-permute-done.4.theirs_ref, bf16[96,1280]{1,0:T(8,128)(2,1)S(1)} %pad_maximum_fusion.2.rim_mine_ref, ...), custom_call_target="tpu_custom_call" | custom-call | tf_op jit(solution)/shard_map/pallas_call | solution.py:327
  77.8 0.1 collective-permute-start.7
  77.9 0.5 collective-permute-start.8
  78.4 1.2 %shard_map.188.out_weight_ref = bf16[640,1280]{1,0:T(8,128)(2,1)S(1)} custom-call(s32[1]{0:T(128)} %bitcast.core_ref, s32[320,1280]{1,0:T(8,128)S(1)} %copy-done.9, f32[16,1280]{1,0:T(8,128)S(1)} %copy-done.14), custom_call_target="tpu_custom_call" | custom-call | flops 6553600 | bytes 2457600 | tf_op jit(solution)/shard_map/pallas_call | solution.py:211
  79.6 1.2 %shard_map.187 = (bf16[256,640]{1,0:T(8,128)(2,1)S(1)}, bf16[256,640]{1,0:T(8,128)(2,1)S(1)}) custom-call(bf16[256,1280]{1,0:T(8,128)(2,1)S(1)} %pad_maximum_fusion.near_ref, bf16[1280,640]{1,0:T(8,128)(2,1)S(1)} %get-tuple-element.67.key_ref, bf16[1280,640]{1,0:T(8,128)(2,1)S(1)} %get-tuple-element.68.value_ref), custom_call_target="tpu_custom_call" | custom-call | flops 838860800 | bytes 3276800 | tf_op jit(solution)/shard_map/pallas_call | solution.py:366
  80.8 0.0 collective-permute-done.7.theirs_ref
  80.9 0.0 collective-permute-done.8.far_ref
  80.9 11.1 %shard_map.189 = (bf16[256,1280]{1,0:T(8,128)(2,1)S(1)}, f32[256,1280]{1,0:T(8,128)S(1)}) custom-call(s32[1]{0:T(128)} %bitcast.core_ref, bf16[512,640]{1,0:T(8,128)(2,1)S(1)} %shard_map.186.mine_ref, bf16[512,640]{1,0:T(8,128)(2,1)S(1)} %collective-permute-done.7.theirs_ref, f32[1,1280]{1,0:T(1,128)S(1)} %broadcast_in_dim.27.gain_ref, ...), custom_call_target="tpu_custom_call" | custom-call | tf_op jit(solution)/shard_map/pallas_call | solution.py:447
  92.0 0.2 collective-permute-start.9
  92.2 2.0 %collective-permute-done.9 = bf16[256,1280]{1,0:T(8,128)(2,1)S(1)} collective-permute-done((bf16[256,1280]{1,0:T(8,128)(2,1)S(1)}, bf16[256,1280]{1,0:T(8,128)(2,1)S(1)}, u32[]{:S(2)}, u32[]{:S(2)}) %collective-permute-start.9) | collective-permute-done | bytes 655392 | tf_op jit(solution)/shard_map/ppermute | solution.py:470
  94.2 1.0 %add_convert_fusion = bf16[256,1280]{1,0:T(8,128)(2,1)} fusion(f32[256,1280]{1,0:T(8,128)S(1)} %get-tuple-element.73, bf16[256,1280]{1,0:T(8,128)(2,1)S(1)} %collective-permute-done.9), kind=kLoop, calls=%fused_computation | loop fusion | flops 983040 | bytes 2621440 | tf_op jit(solution)/shard_map/convert_element_type | solution.py:595
  (67 shorter events, 0.4 us)
Async XLA Ops:
  0.7 1.1 %copy-start.4 = (bf16[16,16,1280]{2,1,0:T(8,128)(2,1)S(1)}, bf16[16,16,1280]{2,1,0:T(8,128)(2,1)}, u32[]{:S(2)}) copy-start(bf16[16,16,1280]{2,1,0:T(8,128)(2,1)} %mine_ref.1) | copy-start | bytes 1966084
  1.8 1.1 %copy-start.10 = (bf16[320,1280]{1,0:T(8,128)(2,1)S(1)}, bf16[320,1280]{1,0:T(8,128)(2,1)}, u32[]{:S(2)}) copy-start(bf16[320,1280]{1,0:T(8,128)(2,1)} %time_ref.1) | copy-start | bytes 2457604
  2.9 1.1 %copy-start.12 = (bf16[16,16,1280]{2,1,0:T(8,128)(2,1)S(1)}, bf16[16,16,1280]{2,1,0:T(8,128)(2,1)}, u32[]{:S(2)}) copy-start(bf16[16,16,1280]{2,1,0:T(8,128)(2,1)} %first_ref.1) | copy-start | bytes 1966084
  4.0 1.1 %copy-start.13 = (bf16[16,16,1280]{2,1,0:T(8,128)(2,1)S(1)}, bf16[16,16,1280]{2,1,0:T(8,128)(2,1)}, u32[]{:S(2)}) copy-start(bf16[16,16,1280]{2,1,0:T(8,128)(2,1)} %normed_ref.1) | copy-start | bytes 1966084
  5.1 3.7 %copy-start.11 = (f32[16,1280]{1,0:T(8,128)S(1)}, f32[16,1280]{1,0:T(8,128)}, u32[]{:S(2)}) copy-start(f32[16,1280]{1,0:T(8,128)} %table_ref.5) | copy-start | bytes 245764
  6.2 11.4 %collective-permute-start = (bf16[32,1408]{1,0:T(8,128)(2,1)S(1)}, bf16[32,1408]{1,0:T(8,128)(2,1)S(1)}, u32[]{:S(2)}, u32[]{:S(2)}) collective-permute-start(bf16[32,1408]{1,0:T(8,128)(2,1)S(1)} %fusion.13), channel_id=1, source_target_pairs={{0,3},{1,2},{2,1},{3,0},{4,7},{5,6},{6,5},{7,4},{8,11},{9,10},{10,... | collective-permute-start | bytes 270344 | tf_op jit(solution)/shard_map/ppermute | solution.py:470
  12.4 5.2 %copy-start = (bf16[9,1280,640]{2,1,0:T(8,128)(2,1)}, bf16[9,1280,640]{2,1,0:T(8,128)(2,1)S(1)}, u32[]{:S(2)}) copy-start(bf16[9,1280,640]{2,1,0:T(8,128)(2,1)S(1)} %shard_map.182.refs_0_) | copy-start | bytes 44236804
  17.7 14.2 %collective-permute-start.1 = (bf16[48,1408]{1,0:T(8,128)(2,1)S(1)}, bf16[48,1408]{1,0:T(8,128)(2,1)S(1)}, u32[]{:S(2)}, u32[]{:S(2)}) collective-permute-start(bf16[48,1408]{1,0:T(8,128)(2,1)S(1)} %fusion.11), channel_id=1, source_target_pairs={{0,7},{1,6},{2,5},{3,4},{4,3},{5,2},{6,1},{7,0},{8,15},{9,14},{10,... | collective-permute-start | bytes 405512 | tf_op jit(solution)/shard_map/ppermute | solution.py:470
  20.5 5.2 %copy-start.1 = (bf16[9,1280,640]{2,1,0:T(8,128)(2,1)S(1)}, bf16[9,1280,640]{2,1,0:T(8,128)(2,1)}, u32[]{:S(2)}) copy-start(bf16[9,1280,640]{2,1,0:T(8,128)(2,1)} %copy-done) | copy-start | bytes 44236804
  32.0 14.4 %copy-start.5 = (bf16[16,16,1280]{2,1,0:T(8,128)(2,1)S(1)}, bf16[16,16,1280]{2,1,0:T(8,128)(2,1)}, u32[]{:S(2)}) copy-start(bf16[16,16,1280]{2,1,0:T(8,128)(2,1)} %mine_ref.1) | copy-start | bytes 1966084
  32.1 14.3 %copy-start.20 = (f32[1280]{0:T(1024)S(1)}, f32[1280]{0:T(1024)}, u32[]{:S(2)}) copy-start(f32[1280]{0:T(1024)} %param.24) | copy-start | bytes 15364
  32.1 14.4 %copy-start.21 = (f32[1280]{0:T(1024)S(1)}, f32[1280]{0:T(1024)}, u32[]{:S(2)}) copy-start(f32[1280]{0:T(1024)} %param.25) | copy-start | bytes 15364
  32.1 14.4 %copy-start.22 = (f32[1280]{0:T(1024)S(1)}, f32[1280]{0:T(1024)}, u32[]{:S(2)}) copy-start(f32[1280]{0:T(1024)} %param.28) | copy-start | bytes 15364
  32.1 15.9 %copy-start.15 = (f32[16,1280]{1,0:T(8,128)S(1)}, f32[16,1280]{1,0:T(8,128)}, u32[]{:S(2)}) copy-start(f32[16,1280]{1,0:T(8,128)} %refs_1_.2) | copy-start | bytes 245764
  32.1 15.9 %copy-start.16 = (f32[16,1280]{1,0:T(8,128)S(1)}, f32[16,1280]{1,0:T(8,128)}, u32[]{:S(2)}) copy-start(f32[16,1280]{1,0:T(8,128)} %refs_3_.1) | copy-start | bytes 245764
  32.1 15.9 %copy-start.17 = (f32[16,1280]{1,0:T(8,128)S(1)}, f32[16,1280]{1,0:T(8,128)}, u32[]{:S(2)}) copy-start(f32[16,1280]{1,0:T(8,128)} %refs_5_.1) | copy-start | bytes 245764
  32.1 11.8 %collective-permute-start.2 = (bf16[96,1408]{1,0:T(8,128)(2,1)S(1)}, bf16[96,1408]{1,0:T(8,128)(2,1)S(1)}, u32[]{:S(2)}, u32[]{:S(2)}) collective-permute-start(bf16[96,1408]{1,0:T(8,128)(2,1)S(1)} %fusion.5), channel_id=1, source_target_pairs={{0,8},{8,0},{16,24},{24,16},{1,9},{9,1},{17,25},{25,17},{2,10},{10... | collective-permute-start | bytes 811016 | tf_op jit(solution)/shard_map/ppermute | solution.py:470
  33.7 14.3 %copy-start.6 = (s32[320,1280]{1,0:T(8,128)S(1)}, s32[320,1280]{1,0:T(8,128)}, u32[]{:S(2)}) copy-start(s32[320,1280]{1,0:T(8,128)} %refs_0_) | copy-start | bytes 4915204
  38.7 5.2 %copy-start.2 = (bf16[9,1280,640]{2,1,0:T(8,128)(2,1)}, bf16[9,1280,640]{2,1,0:T(8,128)(2,1)S(1)}, u32[]{:S(2)}) copy-start(bf16[9,1280,640]{2,1,0:T(8,128)(2,1)S(1)} %shard_map.184.weight_ref) | copy-start | bytes 44236804
  44.0 0.9 copy-start.19
  44.8 9.7 %collective-permute-start.3 = (bf16[32,1408]{1,0:T(8,128)(2,1)S(1)}, bf16[32,1408]{1,0:T(8,128)(2,1)S(1)}, u32[]{:S(2)}, u32[]{:S(2)}) collective-permute-start(bf16[32,1408]{1,0:T(8,128)(2,1)S(1)} %fusion.12), channel_id=1, source_target_pairs={{0,24},{8,16},{16,8},{24,0},{1,25},{9,17},{17,9},{25,1},{2,26},{10... | collective-permute-start | bytes 270344 | tf_op jit(solution)/shard_map/ppermute | solution.py:470
  46.4 11.4 %collective-permute-start.4 = (bf16[16,16,1280]{2,1,0:T(8,128)(2,1)S(1)}, bf16[16,16,1280]{2,1,0:T(8,128)(2,1)S(1)}, u32[]{:S(2)}, u32[]{:S(2)}) collective-permute-start(bf16[16,16,1280]{2,1,0:T(8,128)(2,1)S(1)} %copy-done.5), channel_id=1, source_target_pairs={{0,1},{1,0},{2,3},{3,2},{4,5},{5,4},{6,7},{7,6},{8,9},{9,8},{10,11... | collective-permute-start | bytes 1966088 | tf_op jit(solution)/shard_map/ppermute | solution.py:470
  46.5 11.3 %collective-permute-start.6 = (bf16[128,1280]{1,0:T(8,128)(2,1)}, bf16[128,1280]{1,0:T(8,128)(2,1)S(1)}, u32[]{:S(2)}, u32[]{:S(2)}) collective-permute-start(bf16[128,1280]{1,0:T(8,128)(2,1)} %pad_maximum_fusion.1), channel_id=1, source_target_pairs={{0,24},{8,16},{16,8},{24,0},{1,25},{9,17},{17,9},{25,1},{2,26},{10... | collective-permute-start | bytes 983048 | tf_op jit(solution)/shard_map/ppermute | solution.py:470
  48.0 1.4 %copy-start.7 = (s32[320,1280]{1,0:T(8,128)S(1)}, s32[320,1280]{1,0:T(8,128)}, u32[]{:S(2)}) copy-start(s32[320,1280]{1,0:T(8,128)} %refs_2_) | copy-start | bytes 4915204
  49.4 1.4 %copy-start.8 = (s32[320,1280]{1,0:T(8,128)S(1)}, s32[320,1280]{1,0:T(8,128)}, u32[]{:S(2)}) copy-start(s32[320,1280]{1,0:T(8,128)} %refs_4_) | copy-start | bytes 4915204
  50.8 6.9 %copy-start.18 = (bf16[128,1280]{1,0:T(8,128)(2,1)S(1)}, bf16[128,1280]{1,0:T(8,128)(2,1)}, u32[]{:S(2)}) copy-start(bf16[128,1280]{1,0:T(8,128)(2,1)} %pad_maximum_fusion.1) | copy-start | bytes 983044
  55.6 2.2 %collective-permute-start.5 = (bf16[96,1408]{1,0:T(8,128)(2,1)S(1)}, bf16[96,1408]{1,0:T(8,128)(2,1)S(1)}, u32[]{:S(2)}, u32[]{:S(2)}) collective-permute-start(bf16[96,1408]{1,0:T(8,128)(2,1)S(1)} %fusion.7), channel_id=1, source_target_pairs={{0,1},{1,0},{2,3},{3,2},{4,5},{5,4},{6,7},{7,6},{8,9},{9,8},{10,11... | collective-permute-start | bytes 811016 | tf_op jit(solution)/shard_map/ppermute | solution.py:470
  57.8 5.2 %copy-start.3 = (bf16[9,1280,640]{2,1,0:T(8,128)(2,1)S(1)}, bf16[9,1280,640]{2,1,0:T(8,128)(2,1)}, u32[]{:S(2)}) copy-start(bf16[9,1280,640]{2,1,0:T(8,128)(2,1)} %copy-done.2) | copy-start | bytes 44236804
  63.0 15.4 %copy-start.23 = (f32[1280]{0:T(1024)S(1)}, f32[1280]{0:T(1024)}, u32[]{:S(2)}) copy-start(f32[1280]{0:T(1024)} %param.29) | copy-start | bytes 15364
  63.0 15.4 %copy-start.9 = (s32[320,1280]{1,0:T(8,128)S(1)}, s32[320,1280]{1,0:T(8,128)}, u32[]{:S(2)}) copy-start(s32[320,1280]{1,0:T(8,128)} %refs_0_.1) | copy-start | bytes 4915204
  63.0 15.4 %copy-start.14 = (f32[16,1280]{1,0:T(8,128)S(1)}, f32[16,1280]{1,0:T(8,128)}, u32[]{:S(2)}) copy-start(f32[16,1280]{1,0:T(8,128)} %refs_1_.3) | copy-start | bytes 245764
  77.8 3.1 %collective-permute-start.7 = (bf16[512,640]{1,0:T(8,128)(2,1)S(1)}, bf16[512,640]{1,0:T(8,128)(2,1)S(1)}, u32[]{:S(2)}, u32[]{:S(2)}) collective-permute-start(bf16[512,640]{1,0:T(8,128)(2,1)S(1)} %shard_map.186.mine_ref), channel_id=1, source_target_pairs={{0,1},{1,0},{2,3},{3,2},{4,5},{5,4},{6,7},{7,6},{8,9},{9,8},{10,11... | collective-permute-start | bytes 1966088 | tf_op jit(solution)/shard_map/ppermute | solution.py:470
  77.9 3.0 %collective-permute-start.8 = (bf16[256,1280]{1,0:T(8,128)(2,1)S(1)}, bf16[256,1280]{1,0:T(8,128)(2,1)S(1)}, u32[]{:S(2)}, u32[]{:S(2)}) collective-permute-start(bf16[256,1280]{1,0:T(8,128)(2,1)S(1)} %pad_maximum_fusion.near_ref), channel_id=1, source_target_pairs={{0,1},{1,0},{2,3},{3,2},{4,5},{5,4},{6,7},{7,6},{8,9},{9,8},{10,11... | collective-permute-start | bytes 1966088 | tf_op jit(solution)/shard_map/ppermute | solution.py:470
  92.0 2.2 %collective-permute-start.9 = (bf16[256,1280]{1,0:T(8,128)(2,1)S(1)}, bf16[256,1280]{1,0:T(8,128)(2,1)S(1)}, u32[]{:S(2)}, u32[]{:S(2)}) collective-permute-start(bf16[256,1280]{1,0:T(8,128)(2,1)S(1)} %get-tuple-element.74), channel_id=1, source_target_pairs={{0,1},{1,0},{2,3},{3,2},{4,5},{5,4},{6,7},{7,6},{8,9},{9,8},{10,11... | collective-permute-start | bytes 1966088 | tf_op jit(solution)/shard_map/ppermute | solution.py:470

commit v4 on v3

--- a/solution.py
+++ b/solution.py
@@ -27,6 +27,14 @@
 
 def dot_t(a, b):
     return lax.dot_general(a, b, (((1,), (1,)), ((), ())), preferred_element_type=F32)
+
+
+def from_hbm(values):
+    return pltpu.with_memory_space_constraint(values, pltpu.HBM)
+
+
+def whole_block(shape):
+    return pl.BlockSpec(shape, lambda *at: (0,) * len(shape))
 
 
 def iota(shape, dim):
@@ -101,20 +109,17 @@
 def first_pass(core, timestep, image, stale_first, stale_normed, time_weight):
     height, across, channels = image.shape
     pools = (height // POOL) * (across // POOL)
-    whole = pl.BlockSpec(memory_space=pltpu.VMEM)
     small = pl.BlockSpec(memory_space=pltpu.SMEM)
+    big = [from_hbm(x) for x in (image, stale_first, stale_normed, time_weight)]
+    shapes = [(2, LANES), (4, height, channels), (pools, channels), (8, channels)]
     return pl.pallas_call(
         first_kernel,
-        in_specs=[small, small] + [whole] * 4,
-        out_specs=[whole] * 4,
-        out_shape=[
-            jax.ShapeDtypeStruct((2, LANES), F32),
-            jax.ShapeDtypeStruct((4, height, channels), BF),
-            jax.ShapeDtypeStruct((pools, channels), BF),
-            jax.ShapeDtypeStruct((8, channels), F32),
-        ],
-        compiler_params=params(12),
-    )(core, timestep, image, stale_first, stale_normed, time_weight)
+        grid=(1,),
+        in_specs=[small, small] + [whole_block(x.shape) for x in (image, stale_first, stale_normed, time_weight)],
+        out_specs=[whole_block(shape) for shape in shapes],
+        out_shape=[jax.ShapeDtypeStruct(shape, kind) for shape, kind in zip(shapes, (F32, BF, BF, F32))],
+        compiler_params=params(16),
+    )(core, timestep, *big)
 
 
 def decode_tile(words, words16, low, high, place):
@@ -134,224 +139,288 @@
     )
 
 
-def decode_kernel(core_ref, *refs, count, block):
-    for k in range(count):
-        codes_ref, table_ref, weight_ref = refs[2 * k], refs[2 * k + 1], refs[2 * count + k]
-        decode_into(codes_ref, table_ref, weight_ref, block)
-
-
-def decode_into(codes_ref, table_ref, weight_ref, block):
-    words_all, columns = codes_ref.shape[-2:]
-    lead = (0,) * (len(codes_ref.shape) - 2)
-    for c in range(columns // LANES):
-        lanes = pl.ds(c * LANES, LANES)
-        low = table_ref[0:8, lanes]
-        high = table_ref[8:16, lanes]
-        for g in range(words_all // block):
-            words = codes_ref[lead + (pl.ds(g * block, block), lanes)]
-            words16 = words.astype(jnp.int16)
-            for place in range(4):
-                weight_ref[lead + (pl.ds((4 * g + place) * block, block), lanes)] = decode_tile(
-                    words, words16, low, high, place
-                )
+def decode_lanes(codes_ref, low, high, weight_ref, block):
+    for g in range(codes_ref.shape[0] // block):
+        words = codes_ref[g * block : (g + 1) * block]
+        words16 = words.astype(jnp.int16)
+        for place in range(4):
+            at = (4 * g + place) * block
+            weight_ref[at : at + block] = decode_tile(words, words16, low, high, place)
+
+
+def lanes_at(index):
+    return pl.ds(index * LANES, LANES)
 
 
 def decode_cost(weights):
     return pl.CostEstimate(flops=8 * weights, bytes_accessed=3 * weights, transcendentals=0)
 
 
-def decode_taps(core, codes, table, weights, start, stop):
+def taps_kernel(core_ref, token_ref, table_ref, codes_ref, *refs, start, count):
+    weight_ref, token_out_ref, words_ref, held_ref, came, went = refs[-6:]
+    slots = words_ref.shape[0]
+    blocks = words_ref.shape[2] // LANES
+    first = core_ref[0] * blocks
+    token_out_ref[...] = token_ref[...]
+
+    def far_lanes(block):
+        return pl.ds(pl.multiple_of((first + block) * LANES, LANES), LANES)
+
+    def fetch(tap, block):
+        slot = tap % slots
+        return pltpu.make_async_copy(
+            codes_ref.at[start + tap, :, far_lanes(block)],
+            words_ref.at[slot, :, lanes_at(block)],
+            came.at[slot, block],
+        )
+
+    def store(tap, block):
+        slot = tap % 2
+        return pltpu.make_async_copy(
+            held_ref.at[slot, :, lanes_at(block)],
+            weight_ref.at[start + tap, :, lanes_at(block)],
+            went.at[slot, block],
+        )
+
+    for tap in range(min(slots, count)):
+        for block in range(blocks):
+            fetch(tap, block).start()
+
+    @pl.loop(0, count)
+    def _(tap):
+        for block in range(blocks):
+            fetch(tap, block).wait()
+
+            @pl.when(tap >= 2)
+            def _():
+                store(tap - 2, block).wait()
+
+            decode_lanes(
+                words_ref.at[tap % slots, :, lanes_at(block)],
+                table_ref[0:8, far_lanes(block)],
+                table_ref[8:16, far_lanes(block)],
+                held_ref.at[tap % 2, :, lanes_at(block)],
+                64,
+            )
+            store(tap, block).start()
+
+            @pl.when(tap + slots < count)
+            def _():
+                fetch(tap + slots, block).start()
+
+    for tap in range(max(count - 2, 0), count):
+        for block in range(blocks):
+            store(tap, block).wait()
+
+
+def decode_taps(core, token, codes, table, weights, start, stop):
     words, channels = codes.shape[1:]
     half = channels // 2
-    into = [] if weights is None else [weights]
+    count = stop - start
+    into = [] if weights is None else [from_hbm(weights)]
+    whole = pl.BlockSpec(memory_space=pltpu.VMEM)
+    far = pl.BlockSpec(memory_space=pl.ANY)
     return pl.pallas_call(
-        lambda core_ref, codes_ref, table_ref, *refs: decode_into(codes_ref, table_ref, refs[-1], 64),
-        grid_spec=pltpu.PrefetchScalarGridSpec(
-            num_scalar_prefetch=1,
-            grid=(stop - start,),
-            in_specs=[
-                pl.BlockSpec((1, words, half), lambda t, c: (start + t, 0, c[0])),
-                pl.BlockSpec((16, half), lambda t, c: (0, c[0])),
-            ]
-            + [pl.BlockSpec(memory_space=pl.ANY)] * len(into),
-            out_specs=pl.BlockSpec((1, 4 * words, half), lambda t, c: (start + t, 0, 0)),
-        ),
-        out_shape=jax.ShapeDtypeStruct((codes.shape[0], 4 * words, half), BF),
-        input_output_aliases={3: 0} if into else {},
-        compiler_params=params(34),
-        cost_estimate=decode_cost((stop - start) * 4 * words * half),
-    )(core, codes, table, *into)
-
-
-def decode_columns(core, *pairs):
-    count = len(pairs) // 2
-    words, channels = pairs[0].shape
-    half = channels // 2
+        functools.partial(taps_kernel, start=start, count=count),
+        in_specs=[pl.BlockSpec(memory_space=pltpu.SMEM), whole, whole, far] + [far] * len(into),
+        out_specs=[far, whole],
+        out_shape=[
+            pltpu.HBM((codes.shape[0], 4 * words, half), BF),
+            jax.ShapeDtypeStruct(token.shape, token.dtype),
+        ],
+        scratch_shapes=[
+            pltpu.VMEM((3, words, half), jnp.int32),
+            pltpu.VMEM((2, 4 * words, half), BF),
+            pltpu.SemaphoreType.DMA((3, half // LANES)),
+            pltpu.SemaphoreType.DMA((2, half // LANES)),
+        ],
+        input_output_aliases={4: 0} if into else {},
+        compiler_params=params(10),
+        cost_estimate=decode_cost(count * 4 * words * half),
+    )(core, token, table, from_hbm(codes), *into)
+
+
+def matrices_kernel(core_ref, token_ref, *refs, count, by_rows, block):
+    tables = refs[:count]
+    codes = refs[count : 2 * count]
+    weights = refs[2 * count : 3 * count]
+    token_out_ref, words_ref, came = refs[3 * count :]
+    token_out_ref[...] = token_ref[...]
+    rows = words_ref.shape[1]
+    blocks = words_ref.shape[2] // LANES
+    core = core_ref[0]
+    first = 0 if by_rows else core * blocks
+    row = pl.multiple_of(core * rows, 8) if by_rows else 0
+
+    def far_lanes(at):
+        return lanes_at(at) if by_rows else pl.ds(pl.multiple_of((first + at) * LANES, LANES), LANES)
+
+    def fetch(k, at):
+        return pltpu.make_async_copy(
+            codes[k].at[pl.ds(row, rows), far_lanes(at)], words_ref.at[k, :, lanes_at(at)], came.at[k, at]
+        )
+
+    for k in range(count):
+        for at in range(blocks):
+            fetch(k, at).start()
+    for k in range(count):
+        for at in range(blocks):
+            fetch(k, at).wait()
+            decode_lanes(
+                words_ref.at[k, :, lanes_at(at)],
+                tables[k][0:8, far_lanes(at)],
+                tables[k][8:16, far_lanes(at)],
+                weights[k].at[:, lanes_at(at)],
+                block,
+            )
+
+
+def decode_matrices(core, token, codes, tables, by_rows):
+    count = len(codes)
+    words, channels = codes[0].shape
+    rows, columns = (words // 2, channels) if by_rows else (words, channels // 2)
+    whole = pl.BlockSpec(memory_space=pltpu.VMEM)
     return pl.pallas_call(
-        functools.partial(decode_kernel, count=count, block=64),
-        grid_spec=pltpu.PrefetchScalarGridSpec(
-            num_scalar_prefetch=1,
-            grid=(1,),
-            in_specs=[
-                pl.BlockSpec((words, half), lambda t, c: (0, c[0])),
-                pl.BlockSpec((16, half), lambda t, c: (0, c[0])),
-            ]
-            * count,
-            out_specs=[pl.BlockSpec((4 * words, half), lambda t, c: (0, 0))] * count,
-        ),
-        out_shape=[jax.ShapeDtypeStruct((4 * words, half), BF)] * count,
-        compiler_params=params(14),
-        cost_estimate=decode_cost(count * 4 * words * half),
-    )(core, *pairs)
-
-
-def decode_rows(core, codes, table):
-    words, channels = codes.shape
-    half = words // 2
-    return pl.pallas_call(
-        functools.partial(decode_kernel, count=1, block=32),
-        grid_spec=pltpu.PrefetchScalarGridSpec(
-            num_scalar_prefetch=1,
-            grid=(1,),
-            in_specs=[
-                pl.BlockSpec((half, channels), lambda t, c: (c[0], 0)),
-                pl.BlockSpec((16, channels), lambda t, c: (0, 0)),
-            ],
-            out_specs=[pl.BlockSpec((4 * half, channels), lambda t, c: (0, 0))],
-        ),
-        out_shape=[jax.ShapeDtypeStruct((4 * half, channels), BF)],
+        functools.partial(matrices_kernel, count=count, by_rows=by_rows, block=32 if by_rows else 64),
+        in_specs=[pl.BlockSpec(memory_space=pltpu.SMEM)]
+        + [whole] * (1 + count)
+        + [pl.BlockSpec(memory_space=pl.ANY)] * count,
+        out_specs=[whole] * (count + 1),
+        out_shape=[jax.ShapeDtypeStruct((4 * rows, columns), BF)] * count
+        + [jax.ShapeDtypeStruct(token.shape, token.dtype)],
+        scratch_shapes=[
+            pltpu.VMEM((count, rows, columns), jnp.int32),
+            pltpu.SemaphoreType.DMA((count, columns // LANES)),
+        ],
         compiler_params=params(10),
-        cost_estimate=decode_cost(4 * half * channels),
-    )(core, codes, table)[0]
+        cost_estimate=decode_cost(count * 4 * rows * columns),
+    )(core, token, *tables, *[from_hbm(x) for x in codes])
 
 
 def conv_kernel(
     core_ref, sums_ref, mine_ref, theirs_ref, rim_mine_ref, rim_theirs_ref, gain_ref, shift_ref, bias_ref, time_ref,
-    weight_ref, out_ref, act_ref, rim_ref, padded_ref, total_ref, *, members,
+    weight_ref, out_ref, act_ref, rim_ref, padded_ref, total_ref, held_ref, arrived, *, members,
 ):
-    tap = pl.program_id(0)
-    taps = pl.num_programs(0)
+    taps = weight_ref.shape[0]
+    slots = held_ref.shape[0]
+
+    def fetch(tap):
+        slot = tap % slots
+        return pltpu.make_async_copy(weight_ref.at[tap], held_ref.at[slot], arrived.at[slot])
+
+    for tap in range(slots):
+        fetch(tap).start()
     channels = gain_ref.shape[-1]
     height, across = mine_ref.shape[:2]
     cells = height * across
     core = core_ref[0]
 
-    @pl.when(tap == 0)
-    def _():
-        parts = rim_theirs_ref[0:16, channels:].astype(F32)
-        sums = sums_ref[...] + parts[0:2] + parts[2:4] + parts[4:6]
-        sums = jnp.concatenate([sums, jnp.zeros((6, LANES), F32)], axis=0)
-        spread = dot(sums, group_matrix(channels, True), precision=lax.Precision.HIGHEST)
-        average = spread[0:1] / members
-        mean_square = spread[1:2] / members
-        scale = lax.rsqrt(mean_square - average * average + 1e-05) * gain_ref[...]
-        offset = shift_ref[...] - average * scale
-        size = 256
-        matrix = shuffle_matrix(64)
-        for side, ref in enumerate((mine_ref, theirs_ref)):
-            for k in range(0, channels, size):
-                lanes = slice(k, k + size)
-                value = ref[:, :, lanes].reshape(cells, size).astype(F32)
-                value = value * scale[:, lanes] + offset[:, lanes]
-                value = (0.5 * value) * (1.0 + jnp.tanh(0.5 * value))
-                act_ref[side, :, lanes] = dot(value.astype(BF), matrix)
-        for side, ref in enumerate((rim_mine_ref, rim_theirs_ref)):
-            for k in range(0, channels, size):
-                lanes = slice(k, k + size)
-                rim_ref[side, :, lanes] = dot(ref[:, lanes], matrix)
-
-        column = iota((across, channels), 0)
-
-        def spread_row(side, line, value, left, right):
-            padded_ref[side, 0, line] = jnp.where(column == 0, left, pltpu.roll(value, 1, 0)).astype(BF)
-            padded_ref[side, 1, line] = value.astype(BF)
-            padded_ref[side, 2, line] = jnp.where(
-                column == across - 1, right, pltpu.roll(value, across - 1, 0)
-            ).astype(BF)
-
-        for side in range(2):
-            other = 1 - side
-            is_left = core == side
-            for line, base in ((0, 0), (height + 1, 2 * across)):
-                corner = across + (height - 1 if line == 0 else 0)
-                far = rim_ref[side, base + corner : base + corner + 1]
-                next_last = rim_ref[other, base + across - 1 : base + across]
-                next_first = rim_ref[other, base : base + 1]
-                value = rim_ref[side, base : base + across]
-                spread_row(
-                    side, line, value, jnp.where(is_left, far, next_last), jnp.where(is_left, next_first, far)
-                )
-            outer_at = 4 * across
-            inner_at = 4 * across + height
-
-            @pl.loop(0, height)
-            def _(r):
-                outer = rim_ref[side, pl.ds(outer_at + r, 1)]
-                inner = rim_ref[other, pl.ds(inner_at + r, 1)]
-                value = act_ref[side, pl.ds(pl.multiple_of(r * across, across), across)]
-                spread_row(
-                    side, r + 1, value, jnp.where(is_left, outer, inner), jnp.where(is_left, inner, outer)
-                )
-
-    row_start = tap // 3
-    col_start = tap % 3
-    source = padded_ref[:, col_start, pl.ds(row_start, height)].reshape(2 * cells, channels)
-    part = dot(source, weight_ref[0])
-
-    @pl.when(tap == 0)
-    def _():
-        total_ref[...] = part
-
-    @pl.when((tap > 0) & (tap < taps - 1))
-    def _():
-        total_ref[...] += part
-
-    @pl.when(tap == taps - 1)
-    def _():
-        extra = bias_ref[...] + time_ref[0:1]
-        half = channels // 2
-        for side, ref in enumerate((mine_ref, theirs_ref)):
-            image = jnp.where(core == 0, ref[:, :, :half], ref[:, :, half:]).reshape(cells, half).astype(F32)
-            rows = slice(side * cells, (side + 1) * cells)
-            conv = total_ref[rows] + part[rows] + extra
-            out_ref[rows] = (image + conv).astype(BF)
+    parts = rim_theirs_ref[0:16, channels:].astype(F32)
+    sums = sums_ref[...] + parts[0:2] + parts[2:4] + parts[4:6]
+    sums = jnp.concatenate([sums, jnp.zeros((6, LANES), F32)], axis=0)
+    spread = dot(sums, group_matrix(channels, True), precision=lax.Precision.HIGHEST)
+    average = spread[0:1] / members
+    mean_square = spread[1:2] / members
+    scale = lax.rsqrt(mean_square - average * average + 1e-05) * gain_ref[...]
+    offset = shift_ref[...] - average * scale
+    size = 256
+    matrix = shuffle_matrix(64)
+    for side, ref in enumerate((mine_ref, theirs_ref)):
+        for k in range(0, channels, size):
+            lanes = slice(k, k + size)
+            value = ref[:, :, lanes].reshape(cells, size).astype(F32)
+            value = value * scale[:, lanes] + offset[:, lanes]
+            value = (0.5 * value) * (1.0 + jnp.tanh(0.5 * value))
+            act_ref[side, :, lanes] = dot(value.astype(BF), matrix)
+    for side, ref in enumerate((rim_mine_ref, rim_theirs_ref)):
+        for k in range(0, channels, size):
+            lanes = slice(k, k + size)
+            rim_ref[side, :, lanes] = dot(ref[:, lanes], matrix)
+
+    column = iota((across, channels), 0)
+
+    def spread_row(side, line, value, left, right):
+        padded_ref[side, 0, line] = jnp.where(column == 0, left, pltpu.roll(value, 1, 0)).astype(BF)
+        padded_ref[side, 1, line] = value.astype(BF)
+        padded_ref[side, 2, line] = jnp.where(
+            column == across - 1, right, pltpu.roll(value, across - 1, 0)
+        ).astype(BF)
+
+    for side in range(2):
+        other = 1 - side
+        is_left = core == side
+        for line, base in ((0, 0), (height + 1, 2 * across)):
+            corner = across + (height - 1 if line == 0 else 0)
+            far = rim_ref[side, base + corner : base + corner + 1]
+            next_last = rim_ref[other, base + across - 1 : base + across]
+            next_first = rim_ref[other, base : base + 1]
+            value = rim_ref[side, base : base + across]
+            spread_row(
+                side, line, value, jnp.where(is_left, far, next_last), jnp.where(is_left, next_first, far)
+            )
+        outer_at = 4 * across
+        inner_at = 4 * across + height
+
+        @pl.loop(0, height, unroll=4)
+        def _(r):
+            outer = rim_ref[side, pl.ds(outer_at + r, 1)]
+            inner = rim_ref[other, pl.ds(inner_at + r, 1)]
+            value = act_ref[side, pl.ds(pl.multiple_of(r * across, across), across)]
+            spread_row(
+                side, r + 1, value, jnp.where(is_left, outer, inner), jnp.where(is_left, inner, outer)
+            )
+
+    half = channels // 2
+
+    def tap_product(tap):
+        fetch(tap).wait()
+        source = padded_ref[:, tap % 3, pl.ds(tap // 3, height)].reshape(2 * cells, channels)
+        return dot(source, held_ref[tap % slots])
+
+    total_ref[...] = tap_product(0)
+    fetch(slots).start()
+
+    @pl.loop(1, taps - slots)
+    def _(tap):
+        total_ref[...] += tap_product(tap)
+        fetch(tap + slots).start()
+
+    for tap in range(taps - slots, taps - 1):
+        total_ref[...] += tap_product(tap)
+    last = tap_product(taps - 1)
+    extra = bias_ref[...] + time_ref[0:1]
+    extra = jnp.where(core == 0, extra[:, :half], extra[:, half:])
+    for side, ref in enumerate((mine_ref, theirs_ref)):
+        image = jnp.where(core == 0, ref[:, :, :half], ref[:, :, half:]).reshape(cells, half).astype(F32)
+        rows = slice(side * cells, (side + 1) * cells)
+        out_ref[rows] = (image + (total_ref[rows] + last[rows] + extra)).astype(BF)
 
 
 def convolve(core, sums, mine, theirs, rim_mine, rim_theirs, gain, shift, bias, time_shift, weights, members):
     height, across, channels = mine.shape
     cells = height * across
     half = channels // 2
-    whole = lambda *shape: pl.BlockSpec(shape, lambda t, c: (0,) * len(shape))
-    part = lambda *shape: pl.BlockSpec(shape, lambda t, c: (0,) * (len(shape) - 1) + (c[0],))
+    whole = pl.BlockSpec(memory_space=pltpu.VMEM)
+    small = pl.BlockSpec(memory_space=pltpu.SMEM)
     rim_rows = rim_mine.shape[0]
     return pl.pallas_call(
         functools.partial(conv_kernel, members=members),
-        grid_spec=pltpu.PrefetchScalarGridSpec(
-            num_scalar_prefetch=1,
-            grid=(9,),
-            in_specs=[
-                whole(2, LANES),
-                whole(height, across, channels),
-                whole(height, across, channels),
-                whole(rim_rows, channels),
-                whole(rim_rows, channels + LANES),
-                whole(1, channels),
-                whole(1, channels),
-                part(1, half),
-                part(8, half),
-                pl.BlockSpec((1, channels, half), lambda t, c: (t, 0, 0)),
-            ],
-            out_specs=whole(2 * cells, half),
-            scratch_shapes=[
-                pltpu.VMEM((2, cells, channels), F32),
-                pltpu.VMEM((2, rim_rows, channels), F32),
-                pltpu.VMEM((2, 3, height + 2, across, channels), BF),
-                pltpu.VMEM((2 * cells, half), F32),
-            ],
+        in_specs=[small] + [whole] * 9 + [pl.BlockSpec(memory_space=pl.ANY)],
+        out_specs=whole,
+        out_shape=jax.ShapeDtypeStruct((2 * cells, half), BF),
+        scratch_shapes=[
+            pltpu.VMEM((2, cells, channels), F32),
+            pltpu.VMEM((2, rim_rows, channels), F32),
+            pltpu.VMEM((2, 3, height + 2, across, channels), BF),
+            pltpu.VMEM((2 * cells, half), F32),
+            pltpu.VMEM((3, channels, half), BF),
+            pltpu.SemaphoreType.DMA((3,)),
+        ],
+        compiler_params=params(26),
+        cost_estimate=pl.CostEstimate(
+            flops=36 * cells * channels * half, bytes_accessed=18 * channels * half, transcendentals=2 * cells * channels
         ),
-        out_shape=jax.ShapeDtypeStruct((2 * cells, half), BF),
-        compiler_params=params(24),
-    )(core, sums, mine, theirs, rim_mine, rim_theirs, gain, shift, bias, time_shift, weights)
+    )(core, sums, mine, theirs, rim_mine, rim_theirs, gain, shift, bias, time_shift, from_hbm(weights))
 
 
 def stale_kernel(near_ref, key_ref, value_ref, keys_ref, values_ref):
@@ -532,11 +601,10 @@
     above = below = jnp.zeros((height + across, channels), BF)
     near = pooled
     weights = None
-    codes = codes_first
+    token = sums
     for at, (axis, step) in enumerate(hops):
         last = at == len(hops) - 1
-        if weights is not None:
-            (sums, near), weights = tie((sums, near), weights)
+        (sums, near), token = tie((sums, near), token)
         if axis == "col":
             border = edges[0]
         else:
@@ -554,16 +622,11 @@
         if at == 1:
             partner_image = swap(image, "col", 1)
         if at < len(chunks):
-            _, codes = tie((sums, near), codes)
-            weights = decode_taps(core, codes, table_first, weights, *chunks[at])
+            weights, token = decode_taps(core, token, codes_first, table_first, weights, *chunks[at])
         elif at == len(chunks):
-            _, (query_codes, key_codes, value_codes) = tie(
-                (sums, near), (query_codes, key_codes, value_codes)
+            query, key, value, token = decode_matrices(
+                core, token, (query_codes, key_codes, value_codes), (query_table, key_table, value_table), False
             )
-            query, key, value = decode_columns(
-                core, query_codes, query_table, key_codes, key_table, value_codes, value_table
-            )
-            weights, key = tie(weights, key)
         sums = sums + join_sums(got_border[:across, channels:])
         cells_got = got_border[:, :channels]
         if axis == "col":
@@ -573,20 +636,21 @@
             below = jnp.where(partner == row_at + 1, cells_got, below)
         if not last:
             near = jnp.concatenate([near, got[border.shape[0] :, :channels]])
-    (above, below, sums), weights = tie((above, below, sums), weights)
+    (above, below, sums), token = tie((above, below, sums), token)
     rim = jnp.concatenate([above, below, outer, edges[1]])
     parts = jnp.pad(split_sums(sums), ((0, rim.shape[0] - across), (0, 0)))
     partner_rim = swap(jnp.concatenate([rim, parts], axis=1), "col", 1)
-    near = jnp.concatenate([near, swap(*final)])
+    beyond = swap(*final)
 
     residual = convolve(
         core, sums, image, partner_image, rim, partner_rim, gain_first[None], shift_first[None],
         bias_first[None], time_shift, weights, members,
     )
-    (residual, near, out_codes), _ = tie((residual, near, out_codes), residual)
+    (residual, beyond), token = tie((residual, beyond), token)
+    near = jnp.concatenate([near, beyond])
     partner_residual = swap(residual, "col", 1)
     far = swap(near, "col", 1)
-    out_weight = decode_rows(core, out_codes, out_table)
+    out_weight, _ = decode_matrices(core, token, (out_codes,), (out_table,), True)
     near_keys, near_values = stale_pass(near, key, value)
     send, keep = attention_pass(
         core, residual, partner_residual, attn_gain[None], query, key, value, near_keys, near_values, far, out_weight

time: 95.7 us -> 74.1 us (0.77)
  local copies, waits for them, and re-layouts: 28.2 us -> 0.14 us
  Pallas kernels: 47.9 us -> 55.6 us
  other arithmetic: 3.03 us -> 1.33 us
    unnamed x48 -> x21, local copies, waits for them, and re-layouts: 28.2 us -> 0.07 us
    pallas_call x7, Pallas kernels: 35.6 us -> 43 us  [the longest x3 17.3 us: decode_taps(): pl.pallas_call(functools.partial(taps_kernel, start=start, count=count),...]
  transfers between devices with their start and end apart: 10 -> 10, of which waited for: 2 -> 3; matrix products, arithmetic and copies ran while one was open for 1% -> 0% of each run, Pallas kernels for 22% -> 56%
where the time goes in v4:
time: 74.1 us; the launch traced here: 73.9 us
  Pallas kernels  55.6 us (75%)
  starting transfers between devices  11.1 us (15%)
  waiting for transfers between devices  4.57 us (6%)
  other arithmetic  1.33 us (2%)
  between operations  1.1 us (1%)
    pallas_call x3, Pallas kernels, decode_taps(): pl.pallas_call(functools.partial(taps_kernel, start=start, count=count),...  17.3 us
    pallas_call x1, Pallas kernels, convolve(): pl.pallas_call(functools.partial(conv_kernel, members=members), in_specs=...  15.4 us
    pallas_call x1, Pallas kernels, attention_pass(): pl.pallas_call(attention_kernel, in_specs=[small] + [whole] * 10, out_spe...  11.4 us
    ppermute x10, starting transfers between devices, swap(): return lax.ppermute(values, axis, [(i, i ^ step) for i in range(count)])  11.1 us
    pallas_call x2, Pallas kernels, decode_matrices(): pl.pallas_call(functools.partial(matrices_kernel, count=count, by_rows=by...  7.55 us
    ppermute x10, waiting for transfers between devices, swap(): return lax.ppermute(values, axis, [(i, i ^ step) for i in range(count)])  4.57 us
    pallas_call x1, Pallas kernels, first_pass(): pl.pallas_call(first_kernel, grid=(1,), in_specs=[small, small] + [whole_...  2.81 us
  transfers between devices with their start and end apart: 10, of which 3 were waited for; matrix products, arithmetic and copies ran while one was open for 0% of the time, Pallas kernels for 56%

profile of v4, /device:TPU:0, one launch (start us, length us, event | category | flops | bytes accessed | tf_op | source)
XLA Modules:
  0.0 73.9 jit_solution(7365317016369814815)
XLA Ops:
  0.7 0.0 copy-start
  0.7 2.8 %shard_map.181 = (f32[2,128]{1,0:T(2,128)S(1)}, bf16[4,16,1280]{2,1,0:T(8,128)(2,1)S(1)}, bf16[16,1280]{1,0:T(8,128)(2,1)S(1)}, f32[8,1280]{1,0:T(8,128)S(1)}) custom-call(s32[1]{0:T(128)} %bitcast.core_ref, s32[1]{0:T(128)S(6)} %copy.25.step_ref, bf16[16,16,1280]{2,1,0:T(8,128)(2,1)} %mine_ref.1, bf16[16,16,1280]{2,1,0:T(8,128)(2,1)} %first_ref.1, ...), custom_call_target="tpu_custom_call" | custom-call | tf_op jit(solution)/shard_map/pallas_call | solution.py:115
  3.6 2.5 %collective-permute-start = (bf16[32,1408]{1,0:T(8,128)(2,1)S(1)}, bf16[32,1408]{1,0:T(8,128)(2,1)S(1)}, u32[]{:S(2)}, u32[]{:S(2)}) collective-permute-start(bf16[32,1408]{1,0:T(8,128)(2,1)S(1)} %fusion.13), channel_id=1, source_target_pairs={{0,3},{1,2},{2,1},{3,0},{4,7},{5,6},{6,5},{7,4},{8,11},{9,10},{10,... | collective-permute-start | bytes 270344 | tf_op jit(solution)/shard_map/ppermute | solution.py:539
  6.1 0.0 copy-done
  6.1 4.4 %shard_map.182 = (bf16[9,1280,640]{2,1,0:T(8,128)(2,1)}, f32[2,128]{1,0:T(2,128)S(1)}) custom-call(s32[1]{0:T(128)} %bitcast.core_ref, f32[2,128]{1,0:T(2,128)S(1)} %get-tuple-element.48.token_ref, f32[16,1280]{1,0:T(8,128)S(1)} %copy-done, s32[9,320,1280]{2,1,0:T(8,128)} %codes_ref.5), custom_call_target="tpu_custom_call" | custom-call | flops 13107200 | bytes 4915200 | tf_op jit(solution)/shard_map/pallas_call | solution.py:223
  10.6 0.0 collective-permute-done
  10.7 2.8 %collective-permute-start.1 = (bf16[48,1408]{1,0:T(8,128)(2,1)S(1)}, bf16[48,1408]{1,0:T(8,128)(2,1)S(1)}, u32[]{:S(2)}, u32[]{:S(2)}) collective-permute-start(bf16[48,1408]{1,0:T(8,128)(2,1)S(1)} %fusion.11), channel_id=1, source_target_pairs={{0,7},{1,6},{2,5},{3,4},{4,3},{5,2},{6,1},{7,0},{8,15},{9,14},{10,... | collective-permute-start | bytes 405512 | tf_op jit(solution)/shard_map/ppermute | solution.py:539
  13.5 7.0 %shard_map.183 = (bf16[9,1280,640]{2,1,0:T(8,128)(2,1)}, f32[2,128]{1,0:T(2,128)S(1)}) custom-call(s32[1]{0:T(128)} %bitcast.core_ref, f32[2,128]{1,0:T(2,128)S(1)} %get-tuple-element.52.token_ref, f32[16,1280]{1,0:T(8,128)S(1)} %copy-done, s32[9,320,1280]{2,1,0:T(8,128)} %codes_ref.5, ...), custom_call_target="tpu_custom_call", output_to_operand_aliasing={{0}: (4, {})} | custom-call | flops 26214400 | bytes 9830400 | tf_op jit(solution)/shard_map/pallas_call | solution.py:223
  20.5 0.0 collective-permute-done.1
  20.7 1.6 %collective-permute-start.2 = (bf16[96,1408]{1,0:T(8,128)(2,1)S(1)}, bf16[96,1408]{1,0:T(8,128)(2,1)S(1)}, u32[]{:S(2)}, u32[]{:S(2)}) collective-permute-start(bf16[96,1408]{1,0:T(8,128)(2,1)S(1)} %fusion.5), channel_id=1, source_target_pairs={{0,8},{8,0},{16,24},{24,16},{1,9},{9,1},{17,25},{25,17},{2,10},{10... | collective-permute-start | bytes 811016 | tf_op jit(solution)/shard_map/ppermute | solution.py:539
  22.2 0.0 copy-start.1
  22.2 0.0 copy-start.6
  22.2 0.0 copy-start.7
  22.2 0.0 copy-start.8
  22.2 0.0 copy-start.3
  22.2 0.0 copy-start.4
  22.3 0.0 copy-start.5
  22.3 5.8 %shard_map.184 = (bf16[9,1280,640]{2,1,0:T(8,128)(2,1)}, f32[2,128]{1,0:T(2,128)S(1)}) custom-call(s32[1]{0:T(128)} %bitcast.core_ref, f32[2,128]{1,0:T(2,128)S(1)} %get-tuple-element.57.token_ref, f32[16,1280]{1,0:T(8,128)S(1)} %copy-done, s32[9,320,1280]{2,1,0:T(8,128)} %codes_ref.5, ...), custom_call_target="tpu_custom_call", output_to_operand_aliasing={{0}: (4, {})} | custom-call | flops 19660800 | bytes 7372800 | tf_op jit(solution)/shard_map/pallas_call | solution.py:223
  28.1 1.4 %collective-permute-done.2 = bf16[96,1408]{1,0:T(8,128)(2,1)S(1)} collective-permute-done((bf16[96,1408]{1,0:T(8,128)(2,1)S(1)}, bf16[96,1408]{1,0:T(8,128)(2,1)S(1)}, u32[]{:S(2)}, u32[]{:S(2)}) %collective-permute-start.2) | collective-permute-done | bytes 270368 | tf_op jit(solution)/shard_map/ppermute | solution.py:539
  29.6 2.5 %collective-permute-start.3 = (bf16[32,1408]{1,0:T(8,128)(2,1)S(1)}, bf16[32,1408]{1,0:T(8,128)(2,1)S(1)}, u32[]{:S(2)}, u32[]{:S(2)}) collective-permute-start(bf16[32,1408]{1,0:T(8,128)(2,1)S(1)} %fusion.12), channel_id=1, source_target_pairs={{0,24},{8,16},{16,8},{24,0},{1,25},{9,17},{17,9},{25,1},{2,26},{10... | collective-permute-start | bytes 270344 | tf_op jit(solution)/shard_map/ppermute | solution.py:539
  32.1 0.0 copy-done.1
  32.1 0.0 collective-permute-start.4
  32.1 0.0 copy-done.6
  32.1 0.0 copy-done.7
  32.2 0.0 copy-done.8
  32.2 0.5 collective-permute-start.6
  32.7 0.0 copy-done.3
  32.7 0.0 copy-done.4
  32.7 0.0 copy-done.5
  32.7 4.8 %shard_map.185 = (bf16[1280,640]{1,0:T(8,128)(2,1)S(1)}, bf16[1280,640]{1,0:T(8,128)(2,1)S(1)}, bf16[1280,640]{1,0:T(8,128)(2,1)S(1)}, f32[2,128]{1,0:T(2,128)S(1)}) custom-call(s32[1]{0:T(128)} %bitcast.core_ref, f32[2,128]{1,0:T(2,128)S(1)} %get-tuple-element.61.token_ref, f32[16,1280]{1,0:T(8,128)S(1)} %copy-done.3, f32[16,1280]{1,0:T(8,128)S(1)} %copy-done.4, ...), custom_call_target="tpu_custom_call" | custom-call | flops 19660800 | bytes 7372800 | tf_op jit(solution)/shard_map/pallas_call | solution.py:283
  37.6 0.0 collective-permute-done.3
  37.7 0.3 collective-permute-start.5
  38.0 0.0 collective-permute-done.4.theirs_ref
  38.1 1.3 %collective-permute-done.5.rim_theirs_ref = bf16[96,1408]{1,0:T(8,128)(2,1)S(1)} collective-permute-done((bf16[96,1408]{1,0:T(8,128)(2,1)S(1)}, bf16[96,1408]{1,0:T(8,128)(2,1)S(1)}, u32[]{:S(2)}, u32[]{:S(2)}) %collective-permute-start.5) | collective-permute-done | bytes 270368 | tf_op jit(solution)/shard_map/ppermute | solution.py:539
  39.3 15.4 %shard_map.186.mine_ref = bf16[512,640]{1,0:T(8,128)(2,1)S(1)} custom-call(s32[1]{0:T(128)} %bitcast.core_ref, f32[2,128]{1,0:T(2,128)S(1)} %fusion.20.sums_ref, bf16[16,16,1280]{2,1,0:T(8,128)(2,1)S(1)} %copy-done.1, bf16[16,16,1280]{2,1,0:T(8,128)(2,1)S(1)} %collective-permute-done.4.theirs_ref, bf16[96,1280]{1,0:T(8,128)(2,1)S(1)} %pad_maximum_fusion.1.rim_mine_ref, ...), custom_call_target="tpu_custom_call" | custom-call | flops 7549747200 | bytes 14745600 | tf_op jit(solution)/shard_map/pallas_call | solution.py:406
  54.7 0.0 collective-permute-done.6
  54.8 0.3 collective-permute-start.8
  55.1 0.3 collective-permute-start.7
  55.4 0.0 copy-done.9
  55.4 0.0 copy-done.2
  55.4 2.7 %shard_map.188 = (bf16[640,1280]{1,0:T(8,128)(2,1)S(1)}, f32[2,128]{1,0:T(2,128)}) custom-call(s32[1]{0:T(128)} %bitcast.core_ref, f32[2,128]{1,0:T(2,128)S(1)} %get-tuple-element.77.token_ref, f32[16,1280]{1,0:T(8,128)S(1)} %copy-done.2, s32[320,1280]{1,0:T(8,128)} %refs_1_.3), custom_call_target="tpu_custom_call" | custom-call | flops 6553600 | bytes 2457600 | tf_op jit(solution)/shard_map/pallas_call | solution.py:283
  58.1 1.2 %shard_map.187 = (bf16[256,640]{1,0:T(8,128)(2,1)S(1)}, bf16[256,640]{1,0:T(8,128)(2,1)S(1)}) custom-call(bf16[256,1280]{1,0:T(8,128)(2,1)S(1)} %constant_dynamic-update-slice_fusion.near_ref, bf16[1280,640]{1,0:T(8,128)(2,1)S(1)} %get-tuple-element.72.key_ref, bf16[1280,640]{1,0:T(8,128)(2,1)S(1)} %get-tuple-element.73.value_ref), custom_call_target="tpu_custom_call" | custom-call | flops 838860800 | bytes 3276800 | tf_op jit(solution)/shard_map/pallas_call | solution.py:435
  59.3 0.0 collective-permute-done.8.far_ref
  59.3 0.0 collective-permute-done.7.theirs_ref
  59.3 11.4 %shard_map.189 = (bf16[256,1280]{1,0:T(8,128)(2,1)S(1)}, f32[256,1280]{1,0:T(8,128)S(1)}) custom-call(s32[1]{0:T(128)} %bitcast.core_ref, bf16[512,640]{1,0:T(8,128)(2,1)S(1)} %shard_map.186.mine_ref, bf16[512,640]{1,0:T(8,128)(2,1)S(1)} %collective-permute-done.7.theirs_ref, f32[1,1280]{1,0:T(1,128)S(1)} %broadcast_in_dim.27.gain_ref, ...), custom_call_target="tpu_custom_call" | custom-call | tf_op jit(solution)/shard_map/pallas_call | solution.py:516
  70.7 0.3 collective-permute-start.9
  71.0 1.9 %collective-permute-done.9 = bf16[256,1280]{1,0:T(8,128)(2,1)S(1)} collective-permute-done((bf16[256,1280]{1,0:T(8,128)(2,1)S(1)}, bf16[256,1280]{1,0:T(8,128)(2,1)S(1)}, u32[]{:S(2)}, u32[]{:S(2)}) %collective-permute-start.9) | collective-permute-done | bytes 655392 | tf_op jit(solution)/shard_map/ppermute | solution.py:539
  72.9 1.0 %add_convert_fusion = bf16[256,1280]{1,0:T(8,128)(2,1)} fusion(f32[256,1280]{1,0:T(8,128)S(1)} %get-tuple-element.79, bf16[256,1280]{1,0:T(8,128)(2,1)S(1)} %collective-permute-done.9), kind=kLoop, calls=%fused_computation | loop fusion | flops 983040 | bytes 2621440 | tf_op jit(solution)/shard_map/convert_element_type | solution.py:659
  (40 shorter events, 0.4 us)
Async XLA Ops:
  0.7 5.4 %copy-start = (f32[16,1280]{1,0:T(8,128)S(1)}, f32[16,1280]{1,0:T(8,128)}, u32[]{:S(2)}) copy-start(f32[16,1280]{1,0:T(8,128)} %table_ref.5) | copy-start | bytes 245764
  3.6 7.0 %collective-permute-start = (bf16[32,1408]{1,0:T(8,128)(2,1)S(1)}, bf16[32,1408]{1,0:T(8,128)(2,1)S(1)}, u32[]{:S(2)}, u32[]{:S(2)}) collective-permute-start(bf16[32,1408]{1,0:T(8,128)(2,1)S(1)} %fusion.13), channel_id=1, source_target_pairs={{0,3},{1,2},{2,1},{3,0},{4,7},{5,6},{6,5},{7,4},{8,11},{9,10},{10,... | collective-permute-start | bytes 270344 | tf_op jit(solution)/shard_map/ppermute | solution.py:539
  10.7 9.8 %collective-permute-start.1 = (bf16[48,1408]{1,0:T(8,128)(2,1)S(1)}, bf16[48,1408]{1,0:T(8,128)(2,1)S(1)}, u32[]{:S(2)}, u32[]{:S(2)}) collective-permute-start(bf16[48,1408]{1,0:T(8,128)(2,1)S(1)} %fusion.11), channel_id=1, source_target_pairs={{0,7},{1,6},{2,5},{3,4},{4,3},{5,2},{6,1},{7,0},{8,15},{9,14},{10,... | collective-permute-start | bytes 405512 | tf_op jit(solution)/shard_map/ppermute | solution.py:539
  20.7 8.8 %collective-permute-start.2 = (bf16[96,1408]{1,0:T(8,128)(2,1)S(1)}, bf16[96,1408]{1,0:T(8,128)(2,1)S(1)}, u32[]{:S(2)}, u32[]{:S(2)}) collective-permute-start(bf16[96,1408]{1,0:T(8,128)(2,1)S(1)} %fusion.5), channel_id=1, source_target_pairs={{0,8},{8,0},{16,24},{24,16},{1,9},{9,1},{17,25},{25,17},{2,10},{10... | collective-permute-start | bytes 811016 | tf_op jit(solution)/shard_map/ppermute | solution.py:539
  22.2 9.9 %copy-start.1 = (bf16[16,16,1280]{2,1,0:T(8,128)(2,1)S(1)}, bf16[16,16,1280]{2,1,0:T(8,128)(2,1)}, u32[]{:S(2)}) copy-start(bf16[16,16,1280]{2,1,0:T(8,128)(2,1)} %mine_ref.1) | copy-start | bytes 1966084
  22.2 9.9 %copy-start.6 = (f32[1280]{0:T(1024)S(1)}, f32[1280]{0:T(1024)}, u32[]{:S(2)}) copy-start(f32[1280]{0:T(1024)} %param.24) | copy-start | bytes 15364
  22.2 9.9 %copy-start.7 = (f32[1280]{0:T(1024)S(1)}, f32[1280]{0:T(1024)}, u32[]{:S(2)}) copy-start(f32[1280]{0:T(1024)} %param.25) | copy-start | bytes 15364
  22.2 9.9 %copy-start.8 = (f32[1280]{0:T(1024)S(1)}, f32[1280]{0:T(1024)}, u32[]{:S(2)}) copy-start(f32[1280]{0:T(1024)} %param.28) | copy-start | bytes 15364
  22.2 10.5 %copy-start.3 = (f32[16,1280]{1,0:T(8,128)S(1)}, f32[16,1280]{1,0:T(8,128)}, u32[]{:S(2)}) copy-start(f32[16,1280]{1,0:T(8,128)} %refs_0_.2) | copy-start | bytes 245764
  22.2 10.5 %copy-start.4 = (f32[16,1280]{1,0:T(8,128)S(1)}, f32[16,1280]{1,0:T(8,128)}, u32[]{:S(2)}) copy-start(f32[16,1280]{1,0:T(8,128)} %refs_1_.2) | copy-start | bytes 245764
  22.3 10.5 %copy-start.5 = (f32[16,1280]{1,0:T(8,128)S(1)}, f32[16,1280]{1,0:T(8,128)}, u32[]{:S(2)}) copy-start(f32[16,1280]{1,0:T(8,128)} %refs_2_.1) | copy-start | bytes 245764
  29.6 8.0 %collective-permute-start.3 = (bf16[32,1408]{1,0:T(8,128)(2,1)S(1)}, bf16[32,1408]{1,0:T(8,128)(2,1)S(1)}, u32[]{:S(2)}, u32[]{:S(2)}) collective-permute-start(bf16[32,1408]{1,0:T(8,128)(2,1)S(1)} %fusion.12), channel_id=1, source_target_pairs={{0,24},{8,16},{16,8},{24,0},{1,25},{9,17},{17,9},{25,1},{2,26},{10... | collective-permute-start | bytes 270344 | tf_op jit(solution)/shard_map/ppermute | solution.py:539
  32.1 5.9 %collective-permute-start.4 = (bf16[16,16,1280]{2,1,0:T(8,128)(2,1)S(1)}, bf16[16,16,1280]{2,1,0:T(8,128)(2,1)S(1)}, u32[]{:S(2)}, u32[]{:S(2)}) collective-permute-start(bf16[16,16,1280]{2,1,0:T(8,128)(2,1)S(1)} %copy-done.1), channel_id=1, source_target_pairs={{0,1},{1,0},{2,3},{3,2},{4,5},{5,4},{6,7},{7,6},{8,9},{9,8},{10,11... | collective-permute-start | bytes 1966088 | tf_op jit(solution)/shard_map/ppermute | solution.py:539
  32.2 22.6 %collective-permute-start.6 = (bf16[128,1280]{1,0:T(8,128)(2,1)S(1)}, bf16[128,1280]{1,0:T(8,128)(2,1)S(1)}, u32[]{:S(2)}, u32[]{:S(2)}) collective-permute-start(bf16[128,1280]{1,0:T(8,128)(2,1)S(1)} %pad_maximum_fusion), channel_id=1, source_target_pairs={{0,24},{8,16},{16,8},{24,0},{1,25},{9,17},{17,9},{25,1},{2,26},{10... | collective-permute-start | bytes 983048 | tf_op jit(solution)/shard_map/ppermute | solution.py:539
  37.7 1.6 %collective-permute-start.5 = (bf16[96,1408]{1,0:T(8,128)(2,1)S(1)}, bf16[96,1408]{1,0:T(8,128)(2,1)S(1)}, u32[]{:S(2)}, u32[]{:S(2)}) collective-permute-start(bf16[96,1408]{1,0:T(8,128)(2,1)S(1)} %fusion.7), channel_id=1, source_target_pairs={{0,1},{1,0},{2,3},{3,2},{4,5},{5,4},{6,7},{7,6},{8,9},{9,8},{10,11... | collective-permute-start | bytes 811016 | tf_op jit(solution)/shard_map/ppermute | solution.py:539
  39.3 16.0 %copy-start.9 = (f32[1280]{0:T(1024)S(1)}, f32[1280]{0:T(1024)}, u32[]{:S(2)}) copy-start(f32[1280]{0:T(1024)} %param.29) | copy-start | bytes 15364
  39.3 16.0 %copy-start.2 = (f32[16,1280]{1,0:T(8,128)S(1)}, f32[16,1280]{1,0:T(8,128)}, u32[]{:S(2)}) copy-start(f32[16,1280]{1,0:T(8,128)} %refs_0_.3) | copy-start | bytes 245764
  54.8 4.5 %collective-permute-start.8 = (bf16[256,1280]{1,0:T(8,128)(2,1)S(1)}, bf16[256,1280]{1,0:T(8,128)(2,1)S(1)}, u32[]{:S(2)}, u32[]{:S(2)}) collective-permute-start(bf16[256,1280]{1,0:T(8,128)(2,1)S(1)} %constant_dynamic-update-slice_fusion.near_ref), channel_id=1, source_target_pairs={{0,1},{1,0},{2,3},{3,2},{4,5},{5,4},{6,7},{7,6},{8,9},{9,8},{10,11... | collective-permute-start | bytes 1966088 | tf_op jit(solution)/shard_map/ppermute | solution.py:539
  55.1 4.2 %collective-permute-start.7 = (bf16[512,640]{1,0:T(8,128)(2,1)S(1)}, bf16[512,640]{1,0:T(8,128)(2,1)S(1)}, u32[]{:S(2)}, u32[]{:S(2)}) collective-permute-start(bf16[512,640]{1,0:T(8,128)(2,1)S(1)} %shard_map.186.mine_ref), channel_id=1, source_target_pairs={{0,1},{1,0},{2,3},{3,2},{4,5},{5,4},{6,7},{7,6},{8,9},{9,8},{10,11... | collective-permute-start | bytes 1966088 | tf_op jit(solution)/shard_map/ppermute | solution.py:539
  70.7 2.2 %collective-permute-start.9 = (bf16[256,1280]{1,0:T(8,128)(2,1)S(1)}, bf16[256,1280]{1,0:T(8,128)(2,1)S(1)}, u32[]{:S(2)}, u32[]{:S(2)}) collective-permute-start(bf16[256,1280]{1,0:T(8,128)(2,1)S(1)} %get-tuple-element.80), channel_id=1, source_target_pairs={{0,1},{1,0},{2,3},{3,2},{4,5},{5,4},{6,7},{7,6},{8,9},{9,8},{10,11... | collective-permute-start | bytes 1966088 | tf_op jit(solution)/shard_map/ppermute | solution.py:539

commit v5 on v4

--- a/solution.py
+++ b/solution.py
@@ -301,15 +301,16 @@
     core_ref, sums_ref, mine_ref, theirs_ref, rim_mine_ref, rim_theirs_ref, gain_ref, shift_ref, bias_ref, time_ref,
     weight_ref, out_ref, act_ref, rim_ref, padded_ref, total_ref, held_ref, arrived, *, members,
 ):
-    taps = weight_ref.shape[0]
     slots = held_ref.shape[0]
 
-    def fetch(tap):
-        slot = tap % slots
-        return pltpu.make_async_copy(weight_ref.at[tap], held_ref.at[slot], arrived.at[slot])
-
-    for tap in range(slots):
-        fetch(tap).start()
+    def fetch(tap_row):
+        slot = tap_row % slots
+        return pltpu.make_async_copy(
+            weight_ref.at[3 * tap_row : 3 * tap_row + 3], held_ref.at[slot], arrived.at[slot]
+        )
+
+    for tap_row in range(slots):
+        fetch(tap_row).start()
     channels = gain_ref.shape[-1]
     height, across = mine_ref.shape[:2]
     cells = height * across
@@ -340,11 +341,10 @@
     column = iota((across, channels), 0)
 
     def spread_row(side, line, value, left, right):
-        padded_ref[side, 0, line] = jnp.where(column == 0, left, pltpu.roll(value, 1, 0)).astype(BF)
-        padded_ref[side, 1, line] = value.astype(BF)
-        padded_ref[side, 2, line] = jnp.where(
-            column == across - 1, right, pltpu.roll(value, across - 1, 0)
-        ).astype(BF)
+        before = jnp.where(column == 0, left, pltpu.roll(value, 1, 0))
+        after = jnp.where(column == across - 1, right, pltpu.roll(value, across - 1, 0))
+        for at, shifted in enumerate((before, value, after)):
+            padded_ref[side, line, :, at * channels : (at + 1) * channels] = shifted.astype(BF)
 
     for side in range(2):
         other = 1 - side
@@ -372,22 +372,15 @@
 
     half = channels // 2
 
-    def tap_product(tap):
-        fetch(tap).wait()
-        source = padded_ref[:, tap % 3, pl.ds(tap // 3, height)].reshape(2 * cells, channels)
-        return dot(source, held_ref[tap % slots])
-
-    total_ref[...] = tap_product(0)
-    fetch(slots).start()
-
-    @pl.loop(1, taps - slots)
-    def _(tap):
-        total_ref[...] += tap_product(tap)
-        fetch(tap + slots).start()
-
-    for tap in range(taps - slots, taps - 1):
-        total_ref[...] += tap_product(tap)
-    last = tap_product(taps - 1)
+    def row_product(tap_row):
+        fetch(tap_row).wait()
+        source = padded_ref[:, tap_row : tap_row + height].reshape(2 * cells, 3 * channels)
+        return dot(source, held_ref[tap_row % slots].reshape(3 * channels, half))
+
+    total_ref[...] = row_product(0)
+    fetch(2).start()
+    total_ref[...] += row_product(1)
+    last = row_product(2)
     extra = bias_ref[...] + time_ref[0:1]
     extra = jnp.where(core == 0, extra[:, :half], extra[:, half:])
     for side, ref in enumerate((mine_ref, theirs_ref)):
@@ -411,42 +404,43 @@
         scratch_shapes=[
             pltpu.VMEM((2, cells, channels), F32),
             pltpu.VMEM((2, rim_rows, channels), F32),
-            pltpu.VMEM((2, 3, height + 2, across, channels), BF),
+            pltpu.VMEM((2, height + 2, across, 3 * channels), BF),
             pltpu.VMEM((2 * cells, half), F32),
-            pltpu.VMEM((3, channels, half), BF),
-            pltpu.SemaphoreType.DMA((3,)),
+            pltpu.VMEM((2, 3, channels, half), BF),
+            pltpu.SemaphoreType.DMA((2,)),
         ],
-        compiler_params=params(26),
+        compiler_params=params(32),
         cost_estimate=pl.CostEstimate(
             flops=36 * cells * channels * half, bytes_accessed=18 * channels * half, transcendentals=2 * cells * channels
         ),
     )(core, sums, mine, theirs, rim_mine, rim_theirs, gain, shift, bias, time_shift, from_hbm(weights))
 
 
-def stale_kernel(near_ref, key_ref, value_ref, keys_ref, values_ref):
-    keys_ref[...] = dot(near_ref[...], key_ref[...]).astype(BF)
-    values_ref[...] = dot(near_ref[...], value_ref[...]).astype(BF)
-
-
-def stale_pass(near, key_weight, value_weight):
+def stale_kernel(near_ref, far_ref, key_ref, value_ref, keys_ref, values_ref):
+    pooled = jnp.concatenate([near_ref[...], far_ref[...]], axis=0)
+    keys_ref[...] = dot(pooled, key_ref[...]).astype(BF)
+    values_ref[...] = dot(pooled, value_ref[...]).astype(BF)
+
+
+def stale_pass(near, far, key_weight, value_weight):
     rows, channels = near.shape
     half = key_weight.shape[1]
     whole = pl.BlockSpec(memory_space=pltpu.VMEM)
     return pl.pallas_call(
         stale_kernel,
-        in_specs=[whole] * 3,
+        in_specs=[whole] * 4,
         out_specs=[whole] * 2,
-        out_shape=[jax.ShapeDtypeStruct((rows, half), BF)] * 2,
+        out_shape=[jax.ShapeDtypeStruct((2 * rows, half), BF)] * 2,
         compiler_params=params(16),
         cost_estimate=pl.CostEstimate(
-            flops=4 * rows * channels * half, bytes_accessed=4 * channels * half, transcendentals=0
+            flops=8 * rows * channels * half, bytes_accessed=4 * channels * half, transcendentals=0
         ),
-    )(near, key_weight, value_weight)
+    )(near, far, key_weight, value_weight)
 
 
 def attention_kernel(
     core_ref, mine_ref, theirs_ref, gain_ref, query_ref, key_ref, value_ref, near_keys_ref, near_values_ref,
-    far_ref, out_weight_ref, send_ref, keep_ref, normed_ref, q_ref, k_ref, v_ref, mixed_ref, stale_keys_ref, stale_values_ref,
+    beyond_ref, far_ref, out_weight_ref, send_ref, keep_ref, normed_ref, q_ref, k_ref, v_ref, mixed_ref, stale_keys_ref, stale_values_ref,
 ):
     rows, half = mine_ref.shape
     cells = rows // 2
@@ -472,8 +466,9 @@
     near_rows = near_keys_ref.shape[0]
     stale_keys_ref[:near_rows] = near_keys_ref[...]
     stale_values_ref[:near_rows] = near_values_ref[...]
-    stale_keys_ref[near_rows:] = dot(far_ref[...], key_ref[...]).astype(BF)
-    stale_values_ref[near_rows:] = dot(far_ref[...], value_ref[...]).astype(BF)
+    pooled = jnp.concatenate([beyond_ref[...], far_ref[...]], axis=0)
+    stale_keys_ref[near_rows:] = dot(pooled, key_ref[...]).astype(BF)
+    stale_values_ref[near_rows:] = dot(pooled, value_ref[...]).astype(BF)
     normed = normed_ref[...]
     q_ref[...] = (dot(normed, query_ref[...]).astype(BF) * BF(1.0 / math.sqrt(HEAD_DIM))).astype(BF)
     k_ref[...] = dot(normed, key_ref[...]).astype(BF)
@@ -507,7 +502,7 @@
     keep_ref[...] += dot(mixture[:cells], out_weight_ref[...])
 
 
-def attention_pass(core, mine, theirs, gain, query, key, value, near_keys, near_values, far, out_weight):
+def attention_pass(core, mine, theirs, gain, query, key, value, near_keys, near_values, beyond, far, out_weight):
     rows, half = mine.shape
     channels = 2 * half
     cells = rows // 2
@@ -515,7 +510,7 @@
     small = pl.BlockSpec(memory_space=pltpu.SMEM)
     return pl.pallas_call(
         attention_kernel,
-        in_specs=[small] + [whole] * 10,
+        in_specs=[small] + [whole] * 11,
         out_specs=[whole] * 2,
         out_shape=[
             jax.ShapeDtypeStruct((cells, channels), BF),
@@ -527,11 +522,11 @@
             pltpu.VMEM((rows, half), BF),
             pltpu.VMEM((rows, half), BF),
             pltpu.VMEM((rows, half), BF),
-            pltpu.VMEM((2 * far.shape[0], half), BF),
-            pltpu.VMEM((2 * far.shape[0], half), BF),
+            pltpu.VMEM((4 * far.shape[0], half), BF),
+            pltpu.VMEM((4 * far.shape[0], half), BF),
         ],
         compiler_params=params(28),
-    )(core, mine, theirs, gain, query, key, value, near_keys, near_values, far, out_weight)
+    )(core, mine, theirs, gain, query, key, value, near_keys, near_values, beyond, far, out_weight)
 
 
 def swap(values, axis, step):
@@ -615,6 +610,7 @@
         if last:
             got_border = swap(border, axis, step)
             final = (near, axis, step)
+            far_near = swap(near, "col", 1)
         else:
             payload = jnp.concatenate([border, jnp.pad(near, ((0, 0), (0, LANES)))])
             got = swap(payload, axis, step)
@@ -641,19 +637,19 @@
     parts = jnp.pad(split_sums(sums), ((0, rim.shape[0] - across), (0, 0)))
     partner_rim = swap(jnp.concatenate([rim, parts], axis=1), "col", 1)
     beyond = swap(*final)
+    near_keys, near_values = stale_pass(near, far_near, key, value)
+    sums, near_keys = tie(sums, near_keys)
 
     residual = convolve(
         core, sums, image, partner_image, rim, partner_rim, gain_first[None], shift_first[None],
         bias_first[None], time_shift, weights, members,
     )
     (residual, beyond), token = tie((residual, beyond), token)
-    near = jnp.concatenate([near, beyond])
     partner_residual = swap(residual, "col", 1)
-    far = swap(near, "col", 1)
+    far = swap(beyond, "col", 1)
     out_weight, _ = decode_matrices(core, token, (out_codes,), (out_table,), True)
-    near_keys, near_values = stale_pass(near, key, value)
     send, keep = attention_pass(
-        core, residual, partner_residual, attn_gain[None], query, key, value, near_keys, near_values, far, out_weight
+        core, residual, partner_residual, attn_gain[None], query, key, value, near_keys, near_values, beyond, far, out_weight
     )
     output = keep + swap(send, "col", 1).astype(F32)
     return output.astype(BF).reshape(height, across, channels)

time: 74.1 us -> 71.6 us (0.966)
  Pallas kernels: 55.6 us -> 54 us
  waiting for transfers between devices: 4.57 us -> 3.52 us
    pallas_call x1, Pallas kernels: 15.4 us -> 13.6 us  [convolve(): pl.pallas_call(functools.partial(conv_kernel, members=members), in_specs=...]
    ppermute x10 -> x11, waiting for transfers between devices: 4.57 us -> 3.52 us  [swap(): return lax.ppermute(values, axis, [(i, i ^ step) for i in range(count)])]
    ppermute x10 -> x11, starting transfers between devices: 11.1 us -> 11.4 us  [swap(): return lax.ppermute(values, axis, [(i, i ^ step) for i in range(count)])]
  transfers between devices with their start and end apart: 10 -> 11, of which waited for: 3 -> 3; matrix products, arithmetic and copies ran while one was open for 0% -> 0% of each run, Pallas kernels for 56% -> 56%
where the time goes in v5:
time: 71.6 us; the launch traced here: 71.4 us
  Pallas kernels  54 us (75%)
  starting transfers between devices  11.4 us (16%)
  waiting for transfers between devices  3.52 us (5%)
  other arithmetic  1.3 us (2%)
  between operations  1.1 us (2%)
    pallas_call x3, Pallas kernels, decode_taps(): pl.pallas_call(functools.partial(taps_kernel, start=start, count=count),...  17.3 us
    pallas_call x1, Pallas kernels, convolve(): pl.pallas_call(functools.partial(conv_kernel, members=members), in_specs=...  13.6 us
    pallas_call x1, Pallas kernels, attention_pass(): pl.pallas_call(attention_kernel, in_specs=[small] + [whole] * 11, out_spe...  11.4 us
    ppermute x11, starting transfers between devices, swap(): return lax.ppermute(values, axis, [(i, i ^ step) for i in range(count)])  11.4 us
    pallas_call x2, Pallas kernels, decode_matrices(): pl.pallas_call(functools.partial(matrices_kernel, count=count, by_rows=by...  7.55 us
    ppermute x11, waiting for transfers between devices, swap(): return lax.ppermute(values, axis, [(i, i ^ step) for i in range(count)])  3.52 us
    pallas_call x1, Pallas kernels, first_pass(): pl.pallas_call(first_kernel, grid=(1,), in_specs=[small, small] + [whole_...  2.81 us
  transfers between devices with their start and end apart: 11, of which 3 were waited for; matrix products, arithmetic and copies ran while one was open for 0% of the time, Pallas kernels for 56%

profile of v5, /device:TPU:0, one launch (start us, length us, event | category | flops | bytes accessed | tf_op | source)
XLA Modules:
  0.0 71.4 jit_solution(11026650362364946372)
XLA Ops:
  0.7 0.0 copy-start
  0.7 2.8 %shard_map.181 = (f32[2,128]{1,0:T(2,128)S(1)}, bf16[4,16,1280]{2,1,0:T(8,128)(2,1)S(1)}, bf16[16,1280]{1,0:T(8,128)(2,1)S(1)}, f32[8,1280]{1,0:T(8,128)S(1)}) custom-call(s32[1]{0:T(128)} %bitcast.core_ref, s32[1]{0:T(128)S(6)} %copy.24.step_ref, bf16[16,16,1280]{2,1,0:T(8,128)(2,1)} %mine_ref.1, bf16[16,16,1280]{2,1,0:T(8,128)(2,1)} %first_ref.1, ...), custom_call_target="tpu_custom_call" | custom-call | tf_op jit(solution)/shard_map/pallas_call | solution.py:115
  3.6 2.5 %collective-permute-start = (bf16[32,1408]{1,0:T(8,128)(2,1)S(1)}, bf16[32,1408]{1,0:T(8,128)(2,1)S(1)}, u32[]{:S(2)}, u32[]{:S(2)}) collective-permute-start(bf16[32,1408]{1,0:T(8,128)(2,1)S(1)} %fusion.13), channel_id=1, source_target_pairs={{0,3},{1,2},{2,1},{3,0},{4,7},{5,6},{6,5},{7,4},{8,11},{9,10},{10,... | collective-permute-start | bytes 270344 | tf_op jit(solution)/shard_map/ppermute | solution.py:534
  6.1 0.0 copy-done
  6.1 4.5 %shard_map.182 = (bf16[9,1280,640]{2,1,0:T(8,128)(2,1)}, f32[2,128]{1,0:T(2,128)S(1)}) custom-call(s32[1]{0:T(128)} %bitcast.core_ref, f32[2,128]{1,0:T(2,128)S(1)} %get-tuple-element.50.token_ref, f32[16,1280]{1,0:T(8,128)S(1)} %copy-done, s32[9,320,1280]{2,1,0:T(8,128)} %codes_ref.5), custom_call_target="tpu_custom_call" | custom-call | flops 13107200 | bytes 4915200 | tf_op jit(solution)/shard_map/pallas_call | solution.py:223
  10.6 0.0 collective-permute-done
  10.7 2.8 %collective-permute-start.1 = (bf16[48,1408]{1,0:T(8,128)(2,1)S(1)}, bf16[48,1408]{1,0:T(8,128)(2,1)S(1)}, u32[]{:S(2)}, u32[]{:S(2)}) collective-permute-start(bf16[48,1408]{1,0:T(8,128)(2,1)S(1)} %fusion.11), channel_id=1, source_target_pairs={{0,7},{1,6},{2,5},{3,4},{4,3},{5,2},{6,1},{7,0},{8,15},{9,14},{10,... | collective-permute-start | bytes 405512 | tf_op jit(solution)/shard_map/ppermute | solution.py:534
  13.5 7.0 %shard_map.183 = (bf16[9,1280,640]{2,1,0:T(8,128)(2,1)}, f32[2,128]{1,0:T(2,128)S(1)}) custom-call(s32[1]{0:T(128)} %bitcast.core_ref, f32[2,128]{1,0:T(2,128)S(1)} %get-tuple-element.54.token_ref, f32[16,1280]{1,0:T(8,128)S(1)} %copy-done, s32[9,320,1280]{2,1,0:T(8,128)} %codes_ref.5, ...), custom_call_target="tpu_custom_call", output_to_operand_aliasing={{0}: (4, {})} | custom-call | flops 26214400 | bytes 9830400 | tf_op jit(solution)/shard_map/pallas_call | solution.py:223
  20.6 0.0 collective-permute-done.1
  20.7 1.6 %collective-permute-start.2 = (bf16[96,1408]{1,0:T(8,128)(2,1)S(1)}, bf16[96,1408]{1,0:T(8,128)(2,1)S(1)}, u32[]{:S(2)}, u32[]{:S(2)}) collective-permute-start(bf16[96,1408]{1,0:T(8,128)(2,1)S(1)} %fusion.5), channel_id=1, source_target_pairs={{0,8},{8,0},{16,24},{24,16},{1,9},{9,1},{17,25},{25,17},{2,10},{10... | collective-permute-start | bytes 811016 | tf_op jit(solution)/shard_map/ppermute | solution.py:534
  22.3 0.0 copy-start.1
  22.3 0.0 copy-start.6
  22.3 0.0 copy-start.3
  22.3 0.0 copy-start.4
  22.3 0.0 copy-start.5
  22.3 5.8 %shard_map.184 = (bf16[9,1280,640]{2,1,0:T(8,128)(2,1)}, f32[2,128]{1,0:T(2,128)S(1)}) custom-call(s32[1]{0:T(128)} %bitcast.core_ref, f32[2,128]{1,0:T(2,128)S(1)} %get-tuple-element.59.token_ref, f32[16,1280]{1,0:T(8,128)S(1)} %copy-done, s32[9,320,1280]{2,1,0:T(8,128)} %codes_ref.5, ...), custom_call_target="tpu_custom_call", output_to_operand_aliasing={{0}: (4, {})} | custom-call | flops 19660800 | bytes 7372800 | tf_op jit(solution)/shard_map/pallas_call | solution.py:223
  28.1 1.4 %collective-permute-done.2 = bf16[96,1408]{1,0:T(8,128)(2,1)S(1)} collective-permute-done((bf16[96,1408]{1,0:T(8,128)(2,1)S(1)}, bf16[96,1408]{1,0:T(8,128)(2,1)S(1)}, u32[]{:S(2)}, u32[]{:S(2)}) %collective-permute-start.2) | collective-permute-done | bytes 270368 | tf_op jit(solution)/shard_map/ppermute | solution.py:534
  29.6 2.5 %collective-permute-start.3 = (bf16[32,1408]{1,0:T(8,128)(2,1)S(1)}, bf16[32,1408]{1,0:T(8,128)(2,1)S(1)}, u32[]{:S(2)}, u32[]{:S(2)}) collective-permute-start(bf16[32,1408]{1,0:T(8,128)(2,1)S(1)} %fusion.12), channel_id=1, source_target_pairs={{0,24},{8,16},{16,8},{24,0},{1,25},{9,17},{17,9},{25,1},{2,26},{10... | collective-permute-start | bytes 270344 | tf_op jit(solution)/shard_map/ppermute | solution.py:534
  32.1 0.0 copy-done.1
  32.1 0.0 collective-permute-start.5
  32.1 0.0 copy-done.6
  32.2 0.0 copy-done.7
  32.2 0.0 copy-done.8
  32.2 0.6 collective-permute-start.4
  32.8 0.5 collective-permute-start.7
  33.2 0.0 copy-done.3
  33.2 0.0 copy-done.4
  33.2 0.0 copy-done.5
  33.2 4.8 %shard_map.185 = (bf16[1280,640]{1,0:T(8,128)(2,1)S(1)}, bf16[1280,640]{1,0:T(8,128)(2,1)S(1)}, bf16[1280,640]{1,0:T(8,128)(2,1)S(1)}, f32[2,128]{1,0:T(2,128)S(1)}) custom-call(s32[1]{0:T(128)} %bitcast.core_ref, f32[2,128]{1,0:T(2,128)S(1)} %get-tuple-element.63.token_ref, f32[16,1280]{1,0:T(8,128)S(1)} %copy-done.3, f32[16,1280]{1,0:T(8,128)S(1)} %copy-done.4, ...), custom_call_target="tpu_custom_call" | custom-call | flops 19660800 | bytes 7372800 | tf_op jit(solution)/shard_map/pallas_call | solution.py:283
  38.1 0.0 collective-permute-done.3
  38.2 0.1 collective-permute-start.6
  38.3 0.0 collective-permute-done.4.far_ref
  38.3 1.2 %shard_map.186 = (bf16[256,640]{1,0:T(8,128)(2,1)S(1)}, bf16[256,640]{1,0:T(8,128)(2,1)S(1)}) custom-call(bf16[128,1280]{1,0:T(8,128)(2,1)S(1)} %pad_maximum_fusion.near_ref, bf16[128,1280]{1,0:T(8,128)(2,1)S(1)} %collective-permute-done.4.far_ref, bf16[1280,640]{1,0:T(8,128)(2,1)S(1)} %get-tuple-element.67.key_ref, ...), custom_call_target="tpu_custom_call" | custom-call | flops 838860800 | bytes 3276800 | tf_op jit(solution)/shard_map/pallas_call | solution.py:429
  39.5 0.0 collective-permute-done.5.theirs_ref
  39.6 0.3 collective-permute-done.6.rim_theirs_ref
  39.8 13.6 %shard_map.187.mine_ref = bf16[512,640]{1,0:T(8,128)(2,1)S(1)} custom-call(s32[1]{0:T(128)} %bitcast.core_ref, f32[2,128]{1,0:T(2,128)S(1)} %fusion.20.sums_ref, bf16[16,16,1280]{2,1,0:T(8,128)(2,1)S(1)} %copy-done.1, bf16[16,16,1280]{2,1,0:T(8,128)(2,1)S(1)} %collective-permute-done.5.theirs_ref, bf16[96,1280]{1,0:T(8,128)(2,1)S(1)} %pad_maximum_fusion.1.rim_mine_ref, ...), custom_call_target="tpu_custom_call" | custom-call | flops 7549747200 | bytes 14745600 | tf_op jit(solution)/shard_map/pallas_call | solution.py:399
  53.5 0.0 collective-permute-done.7.beyond_ref
  53.5 0.3 collective-permute-start.8
  53.8 0.3 collective-permute-start.9
  54.1 0.0 copy-done.9
  54.1 0.0 copy-done.2
  54.1 2.7 %shard_map.188 = (bf16[640,1280]{1,0:T(8,128)(2,1)S(1)}, f32[2,128]{1,0:T(2,128)}) custom-call(s32[1]{0:T(128)} %bitcast.core_ref, f32[2,128]{1,0:T(2,128)S(1)} %get-tuple-element.81.token_ref, f32[16,1280]{1,0:T(8,128)S(1)} %copy-done.2, s32[320,1280]{1,0:T(8,128)} %refs_1_.3), custom_call_target="tpu_custom_call" | custom-call | flops 6553600 | bytes 2457600 | tf_op jit(solution)/shard_map/pallas_call | solution.py:283
  56.8 0.0 collective-permute-done.9.far_ref
  56.8 0.0 collective-permute-done.8.theirs_ref
  56.8 11.4 %shard_map.189 = (bf16[256,1280]{1,0:T(8,128)(2,1)S(1)}, f32[256,1280]{1,0:T(8,128)S(1)}) custom-call(s32[1]{0:T(128)} %bitcast.core_ref, bf16[512,640]{1,0:T(8,128)(2,1)S(1)} %shard_map.187.mine_ref, bf16[512,640]{1,0:T(8,128)(2,1)S(1)} %collective-permute-done.8.theirs_ref, f32[1,1280]{1,0:T(1,128)S(1)} %broadcast_in_dim.27.gain_ref, ...), custom_call_target="tpu_custom_call" | custom-call | tf_op jit(solution)/shard_map/pallas_call | solution.py:511
  68.3 0.3 collective-permute-start.10
  68.6 1.9 %collective-permute-done.10 = bf16[256,1280]{1,0:T(8,128)(2,1)S(1)} collective-permute-done((bf16[256,1280]{1,0:T(8,128)(2,1)S(1)}, bf16[256,1280]{1,0:T(8,128)(2,1)S(1)}, u32[]{:S(2)}, u32[]{:S(2)}) %collective-permute-start.10) | collective-permute-done | bytes 655392 | tf_op jit(solution)/shard_map/ppermute | solution.py:534
  70.4 1.0 %add_convert_fusion = bf16[256,1280]{1,0:T(8,128)(2,1)} fusion(f32[256,1280]{1,0:T(8,128)S(1)} %get-tuple-element.83, bf16[256,1280]{1,0:T(8,128)(2,1)S(1)} %collective-permute-done.10), kind=kLoop, calls=%fused_computation | loop fusion | flops 983040 | bytes 2621440 | tf_op jit(solution)/shard_map/convert_element_type | solution.py:655
  (40 shorter events, 0.4 us)
Async XLA Ops:
  0.7 5.4 %copy-start = (f32[16,1280]{1,0:T(8,128)S(1)}, f32[16,1280]{1,0:T(8,128)}, u32[]{:S(2)}) copy-start(f32[16,1280]{1,0:T(8,128)} %table_ref.5) | copy-start | bytes 245764
  3.6 7.0 %collective-permute-start = (bf16[32,1408]{1,0:T(8,128)(2,1)S(1)}, bf16[32,1408]{1,0:T(8,128)(2,1)S(1)}, u32[]{:S(2)}, u32[]{:S(2)}) collective-permute-start(bf16[32,1408]{1,0:T(8,128)(2,1)S(1)} %fusion.13), channel_id=1, source_target_pairs={{0,3},{1,2},{2,1},{3,0},{4,7},{5,6},{6,5},{7,4},{8,11},{9,10},{10,... | collective-permute-start | bytes 270344 | tf_op jit(solution)/shard_map/ppermute | solution.py:534
  10.7 9.9 %collective-permute-start.1 = (bf16[48,1408]{1,0:T(8,128)(2,1)S(1)}, bf16[48,1408]{1,0:T(8,128)(2,1)S(1)}, u32[]{:S(2)}, u32[]{:S(2)}) collective-permute-start(bf16[48,1408]{1,0:T(8,128)(2,1)S(1)} %fusion.11), channel_id=1, source_target_pairs={{0,7},{1,6},{2,5},{3,4},{4,3},{5,2},{6,1},{7,0},{8,15},{9,14},{10,... | collective-permute-start | bytes 405512 | tf_op jit(solution)/shard_map/ppermute | solution.py:534
  20.7 8.8 %collective-permute-start.2 = (bf16[96,1408]{1,0:T(8,128)(2,1)S(1)}, bf16[96,1408]{1,0:T(8,128)(2,1)S(1)}, u32[]{:S(2)}, u32[]{:S(2)}) collective-permute-start(bf16[96,1408]{1,0:T(8,128)(2,1)S(1)} %fusion.5), channel_id=1, source_target_pairs={{0,8},{8,0},{16,24},{24,16},{1,9},{9,1},{17,25},{25,17},{2,10},{10... | collective-permute-start | bytes 811016 | tf_op jit(solution)/shard_map/ppermute | solution.py:534
  22.3 9.9 %copy-start.1 = (bf16[16,16,1280]{2,1,0:T(8,128)(2,1)S(1)}, bf16[16,16,1280]{2,1,0:T(8,128)(2,1)}, u32[]{:S(2)}) copy-start(bf16[16,16,1280]{2,1,0:T(8,128)(2,1)} %mine_ref.1) | copy-start | bytes 1966084
  22.3 9.9 %copy-start.6 = (f32[1280]{0:T(1024)S(1)}, f32[1280]{0:T(1024)}, u32[]{:S(2)}) copy-start(f32[1280]{0:T(1024)} %param.24) | copy-start | bytes 15364
  22.3 9.9 %copy-start.7 = (f32[1280]{0:T(1024)S(1)}, f32[1280]{0:T(1024)}, u32[]{:S(2)}) copy-start(f32[1280]{0:T(1024)} %param.25) | copy-start | bytes 15364
  22.3 9.9 %copy-start.8 = (f32[1280]{0:T(1024)S(1)}, f32[1280]{0:T(1024)}, u32[]{:S(2)}) copy-start(f32[1280]{0:T(1024)} %param.28) | copy-start | bytes 15364
  22.3 11.0 %copy-start.3 = (f32[16,1280]{1,0:T(8,128)S(1)}, f32[16,1280]{1,0:T(8,128)}, u32[]{:S(2)}) copy-start(f32[16,1280]{1,0:T(8,128)} %refs_0_.2) | copy-start | bytes 245764
  22.3 10.9 %copy-start.4 = (f32[16,1280]{1,0:T(8,128)S(1)}, f32[16,1280]{1,0:T(8,128)}, u32[]{:S(2)}) copy-start(f32[16,1280]{1,0:T(8,128)} %refs_1_.2) | copy-start | bytes 245764
  22.3 10.9 %copy-start.5 = (f32[16,1280]{1,0:T(8,128)S(1)}, f32[16,1280]{1,0:T(8,128)}, u32[]{:S(2)}) copy-start(f32[16,1280]{1,0:T(8,128)} %refs_2_.1) | copy-start | bytes 245764
  29.6 8.5 %collective-permute-start.3 = (bf16[32,1408]{1,0:T(8,128)(2,1)S(1)}, bf16[32,1408]{1,0:T(8,128)(2,1)S(1)}, u32[]{:S(2)}, u32[]{:S(2)}) collective-permute-start(bf16[32,1408]{1,0:T(8,128)(2,1)S(1)} %fusion.12), channel_id=1, source_target_pairs={{0,24},{8,16},{16,8},{24,0},{1,25},{9,17},{17,9},{25,1},{2,26},{10... | collective-permute-start | bytes 270344 | tf_op jit(solution)/shard_map/ppermute | solution.py:534
  32.1 7.4 %collective-permute-start.5 = (bf16[16,16,1280]{2,1,0:T(8,128)(2,1)S(1)}, bf16[16,16,1280]{2,1,0:T(8,128)(2,1)S(1)}, u32[]{:S(2)}, u32[]{:S(2)}) collective-permute-start(bf16[16,16,1280]{2,1,0:T(8,128)(2,1)S(1)} %copy-done.1), channel_id=1, source_target_pairs={{0,1},{1,0},{2,3},{3,2},{4,5},{5,4},{6,7},{7,6},{8,9},{9,8},{10,11... | collective-permute-start | bytes 1966088 | tf_op jit(solution)/shard_map/ppermute | solution.py:534
  32.2 6.1 %collective-permute-start.4 = (bf16[128,1280]{1,0:T(8,128)(2,1)S(1)}, bf16[128,1280]{1,0:T(8,128)(2,1)S(1)}, u32[]{:S(2)}, u32[]{:S(2)}) collective-permute-start(bf16[128,1280]{1,0:T(8,128)(2,1)S(1)} %pad_maximum_fusion.near_ref), channel_id=1, source_target_pairs={{0,1},{1,0},{2,3},{3,2},{4,5},{5,4},{6,7},{7,6},{8,9},{9,8},{10,11... | collective-permute-start | bytes 983048 | tf_op jit(solution)/shard_map/ppermute | solution.py:534
  32.8 20.7 %collective-permute-start.7 = (bf16[128,1280]{1,0:T(8,128)(2,1)S(1)}, bf16[128,1280]{1,0:T(8,128)(2,1)S(1)}, u32[]{:S(2)}, u32[]{:S(2)}) collective-permute-start(bf16[128,1280]{1,0:T(8,128)(2,1)S(1)} %pad_maximum_fusion.near_ref), channel_id=1, source_target_pairs={{0,24},{8,16},{16,8},{24,0},{1,25},{9,17},{17,9},{25,1},{2,26},{10... | collective-permute-start | bytes 983048 | tf_op jit(solution)/shard_map/ppermute | solution.py:534
  38.2 1.6 %collective-permute-start.6 = (bf16[96,1408]{1,0:T(8,128)(2,1)S(1)}, bf16[96,1408]{1,0:T(8,128)(2,1)S(1)}, u32[]{:S(2)}, u32[]{:S(2)}) collective-permute-start(bf16[96,1408]{1,0:T(8,128)(2,1)S(1)} %fusion.7), channel_id=1, source_target_pairs={{0,1},{1,0},{2,3},{3,2},{4,5},{5,4},{6,7},{7,6},{8,9},{9,8},{10,11... | collective-permute-start | bytes 811016 | tf_op jit(solution)/shard_map/ppermute | solution.py:534
  39.8 14.2 %copy-start.9 = (f32[1280]{0:T(1024)S(1)}, f32[1280]{0:T(1024)}, u32[]{:S(2)}) copy-start(f32[1280]{0:T(1024)} %param.29) | copy-start | bytes 15364
  39.8 14.2 %copy-start.2 = (f32[16,1280]{1,0:T(8,128)S(1)}, f32[16,1280]{1,0:T(8,128)}, u32[]{:S(2)}) copy-start(f32[16,1280]{1,0:T(8,128)} %refs_0_.3) | copy-start | bytes 245764
  53.5 3.3 %collective-permute-start.8 = (bf16[512,640]{1,0:T(8,128)(2,1)S(1)}, bf16[512,640]{1,0:T(8,128)(2,1)S(1)}, u32[]{:S(2)}, u32[]{:S(2)}) collective-permute-start(bf16[512,640]{1,0:T(8,128)(2,1)S(1)} %shard_map.187.mine_ref), channel_id=1, source_target_pairs={{0,1},{1,0},{2,3},{3,2},{4,5},{5,4},{6,7},{7,6},{8,9},{9,8},{10,11... | collective-permute-start | bytes 1966088 | tf_op jit(solution)/shard_map/ppermute | solution.py:534
  53.8 3.0 %collective-permute-start.9 = (bf16[128,1280]{1,0:T(8,128)(2,1)S(1)}, bf16[128,1280]{1,0:T(8,128)(2,1)S(1)}, u32[]{:S(2)}, u32[]{:S(2)}) collective-permute-start(bf16[128,1280]{1,0:T(8,128)(2,1)S(1)} %collective-permute-done.7.beyond_ref), channel_id=1, source_target_pairs={{0,1},{1,0},{2,3},{3,2},{4,5},{5,4},{6,7},{7,6},{8,9},{9,8},{10,11... | collective-permute-start | bytes 983048 | tf_op jit(solution)/shard_map/ppermute | solution.py:534
  68.3 2.2 %collective-permute-start.10 = (bf16[256,1280]{1,0:T(8,128)(2,1)S(1)}, bf16[256,1280]{1,0:T(8,128)(2,1)S(1)}, u32[]{:S(2)}, u32[]{:S(2)}) collective-permute-start(bf16[256,1280]{1,0:T(8,128)(2,1)S(1)} %get-tuple-element.84), channel_id=1, source_target_pairs={{0,1},{1,0},{2,3},{3,2},{4,5},{5,4},{6,7},{7,6},{8,9},{9,8},{10,11... | collective-permute-start | bytes 1966088 | tf_op jit(solution)/shard_map/ppermute | solution.py:534

commit v6 on v5

--- a/solution.py
+++ b/solution.py
@@ -323,7 +323,8 @@
     average = spread[0:1] / members
     mean_square = spread[1:2] / members
     scale = lax.rsqrt(mean_square - average * average + 1e-05) * gain_ref[...]
-    offset = shift_ref[...] - average * scale
+    offset = 0.5 * (shift_ref[...] - average * scale)
+    scale = 0.5 * scale
     size = 256
     matrix = shuffle_matrix(64)
     for side, ref in enumerate((mine_ref, theirs_ref)):
@@ -331,7 +332,7 @@
             lanes = slice(k, k + size)
             value = ref[:, :, lanes].reshape(cells, size).astype(F32)
             value = value * scale[:, lanes] + offset[:, lanes]
-            value = (0.5 * value) * (1.0 + jnp.tanh(0.5 * value))
+            value = value + value * jnp.tanh(value)
             act_ref[side, :, lanes] = dot(value.astype(BF), matrix)
     for side, ref in enumerate((rim_mine_ref, rim_theirs_ref)):
         for k in range(0, channels, size):
@@ -361,7 +362,7 @@
         outer_at = 4 * across
         inner_at = 4 * across + height
 
-        @pl.loop(0, height, unroll=4)
+        @pl.loop(0, height, unroll=height)
         def _(r):
             outer = rim_ref[side, pl.ds(outer_at + r, 1)]
             inner = rim_ref[other, pl.ds(inner_at + r, 1)]
@@ -488,15 +489,15 @@
             )
             fresh = dot_t(stacked, k_ref[at, lanes])
             stale = dot_t(stacked, stale_keys_ref[:, lanes])
-            highest = jnp.maximum(
-                jnp.max(fresh, axis=1, keepdims=True), jnp.max(stale, axis=1, keepdims=True)
-            )
+            blocks = [x[:, k : k + LANES] for x in (fresh, stale) for k in range(0, x.shape[1], LANES)]
+            highest = jnp.max(functools.reduce(jnp.maximum, blocks), axis=1, keepdims=True)
             fresh = jnp.exp(fresh - highest).astype(BF)
             stale = jnp.exp(stale - highest).astype(BF)
             mixed = dot(fresh, jnp.concatenate([v_ref[at, lanes], ones], axis=1))
             mixed += dot(stale, jnp.concatenate([stale_values_ref[:, lanes], stale_ones], axis=1))
-            mixed = mixed[:, :LANES] / mixed[:, LANES:]
-            mixed_ref[at, lanes] = jnp.where(lane < HEAD_DIM, mixed[:cells], mixed[cells:]).astype(BF)
+            merged = jnp.where(lane < HEAD_DIM, mixed[:cells, :LANES], mixed[cells:, :LANES])
+            weight = jnp.where(lane < HEAD_DIM, mixed[:cells, LANES:], mixed[cells:, LANES:])
+            mixed_ref[at, lanes] = (merged / weight).astype(BF)
     mixture = shuffle(mixed_ref[...], 32).astype(BF)
     send_ref[...] = dot(mixture[cells:], out_weight_ref[...]).astype(BF)
     keep_ref[...] += dot(mixture[:cells], out_weight_ref[...])

time: 71.6 us -> 70.5 us (0.985)
  Pallas kernels: 54 us -> 52.9 us
    pallas_call x1, Pallas kernels: 13.6 us -> 12.5 us  [convolve(): pl.pallas_call(functools.partial(conv_kernel, members=members), in_specs=...]
  transfers between devices with their start and end apart: 11 -> 11, of which waited for: 3 -> 3; matrix products, arithmetic and copies ran while one was open for 0% -> 0% of each run, Pallas kernels for 56% -> 55%
where the time goes in v6:
time: 70.5 us; the launch traced here: 70.3 us
  Pallas kernels  52.9 us (75%)
  starting transfers between devices  11.4 us (16%)
  waiting for transfers between devices  3.52 us (5%)
  other arithmetic  1.3 us (2%)
  between operations  1.1 us (2%)
    pallas_call x3, Pallas kernels, decode_taps(): pl.pallas_call(functools.partial(taps_kernel, start=start, count=count),...  17.3 us
    pallas_call x1, Pallas kernels, convolve(): pl.pallas_call(functools.partial(conv_kernel, members=members), in_specs=...  12.5 us
    pallas_call x1, Pallas kernels, attention_pass(): pl.pallas_call(attention_kernel, in_specs=[small] + [whole] * 11, out_spe...  11.5 us
    ppermute x11, starting transfers between devices, swap(): return lax.ppermute(values, axis, [(i, i ^ step) for i in range(count)])  11.4 us
    pallas_call x2, Pallas kernels, decode_matrices(): pl.pallas_call(functools.partial(matrices_kernel, count=count, by_rows=by...  7.55 us
    ppermute x11, waiting for transfers between devices, swap(): return lax.ppermute(values, axis, [(i, i ^ step) for i in range(count)])  3.52 us
    pallas_call x1, Pallas kernels, first_pass(): pl.pallas_call(first_kernel, grid=(1,), in_specs=[small, small] + [whole_...  2.81 us
  transfers between devices with their start and end apart: 11, of which 3 were waited for; matrix products, arithmetic and copies ran while one was open for 0% of the time, Pallas kernels for 55%

profile of v6, /device:TPU:0, one launch (start us, length us, event | category | flops | bytes accessed | tf_op | source)
XLA Modules:
  0.0 70.3 jit_solution(9128877218443503009)
XLA Ops:
  0.7 0.0 copy-start
  0.7 2.8 %shard_map.181 = (f32[2,128]{1,0:T(2,128)S(1)}, bf16[4,16,1280]{2,1,0:T(8,128)(2,1)S(1)}, bf16[16,1280]{1,0:T(8,128)(2,1)S(1)}, f32[8,1280]{1,0:T(8,128)S(1)}) custom-call(s32[1]{0:T(128)} %bitcast.core_ref, s32[1]{0:T(128)S(6)} %copy.24.step_ref, bf16[16,16,1280]{2,1,0:T(8,128)(2,1)} %mine_ref.1, bf16[16,16,1280]{2,1,0:T(8,128)(2,1)} %first_ref.1, ...), custom_call_target="tpu_custom_call" | custom-call | tf_op jit(solution)/shard_map/pallas_call | solution.py:115
  3.6 2.5 %collective-permute-start = (bf16[32,1408]{1,0:T(8,128)(2,1)S(1)}, bf16[32,1408]{1,0:T(8,128)(2,1)S(1)}, u32[]{:S(2)}, u32[]{:S(2)}) collective-permute-start(bf16[32,1408]{1,0:T(8,128)(2,1)S(1)} %fusion.13), channel_id=1, source_target_pairs={{0,3},{1,2},{2,1},{3,0},{4,7},{5,6},{6,5},{7,4},{8,11},{9,10},{10,... | collective-permute-start | bytes 270344 | tf_op jit(solution)/shard_map/ppermute | solution.py:535
  6.1 0.0 copy-done
  6.1 4.5 %shard_map.182 = (bf16[9,1280,640]{2,1,0:T(8,128)(2,1)}, f32[2,128]{1,0:T(2,128)S(1)}) custom-call(s32[1]{0:T(128)} %bitcast.core_ref, f32[2,128]{1,0:T(2,128)S(1)} %get-tuple-element.50.token_ref, f32[16,1280]{1,0:T(8,128)S(1)} %copy-done, s32[9,320,1280]{2,1,0:T(8,128)} %codes_ref.5), custom_call_target="tpu_custom_call" | custom-call | flops 13107200 | bytes 4915200 | tf_op jit(solution)/shard_map/pallas_call | solution.py:223
  10.6 0.0 collective-permute-done
  10.7 2.8 %collective-permute-start.1 = (bf16[48,1408]{1,0:T(8,128)(2,1)S(1)}, bf16[48,1408]{1,0:T(8,128)(2,1)S(1)}, u32[]{:S(2)}, u32[]{:S(2)}) collective-permute-start(bf16[48,1408]{1,0:T(8,128)(2,1)S(1)} %fusion.11), channel_id=1, source_target_pairs={{0,7},{1,6},{2,5},{3,4},{4,3},{5,2},{6,1},{7,0},{8,15},{9,14},{10,... | collective-permute-start | bytes 405512 | tf_op jit(solution)/shard_map/ppermute | solution.py:535
  13.5 7.0 %shard_map.183 = (bf16[9,1280,640]{2,1,0:T(8,128)(2,1)}, f32[2,128]{1,0:T(2,128)S(1)}) custom-call(s32[1]{0:T(128)} %bitcast.core_ref, f32[2,128]{1,0:T(2,128)S(1)} %get-tuple-element.54.token_ref, f32[16,1280]{1,0:T(8,128)S(1)} %copy-done, s32[9,320,1280]{2,1,0:T(8,128)} %codes_ref.5, ...), custom_call_target="tpu_custom_call", output_to_operand_aliasing={{0}: (4, {})} | custom-call | flops 26214400 | bytes 9830400 | tf_op jit(solution)/shard_map/pallas_call | solution.py:223
  20.6 0.0 collective-permute-done.1
  20.7 1.6 %collective-permute-start.2 = (bf16[96,1408]{1,0:T(8,128)(2,1)S(1)}, bf16[96,1408]{1,0:T(8,128)(2,1)S(1)}, u32[]{:S(2)}, u32[]{:S(2)}) collective-permute-start(bf16[96,1408]{1,0:T(8,128)(2,1)S(1)} %fusion.5), channel_id=1, source_target_pairs={{0,8},{8,0},{16,24},{24,16},{1,9},{9,1},{17,25},{25,17},{2,10},{10... | collective-permute-start | bytes 811016 | tf_op jit(solution)/shard_map/ppermute | solution.py:535
  22.3 0.0 copy-start.1
  22.3 0.0 copy-start.6
  22.3 0.0 copy-start.3
  22.3 0.0 copy-start.4
  22.3 0.0 copy-start.5
  22.3 5.8 %shard_map.184 = (bf16[9,1280,640]{2,1,0:T(8,128)(2,1)}, f32[2,128]{1,0:T(2,128)S(1)}) custom-call(s32[1]{0:T(128)} %bitcast.core_ref, f32[2,128]{1,0:T(2,128)S(1)} %get-tuple-element.59.token_ref, f32[16,1280]{1,0:T(8,128)S(1)} %copy-done, s32[9,320,1280]{2,1,0:T(8,128)} %codes_ref.5, ...), custom_call_target="tpu_custom_call", output_to_operand_aliasing={{0}: (4, {})} | custom-call | flops 19660800 | bytes 7372800 | tf_op jit(solution)/shard_map/pallas_call | solution.py:223
  28.1 1.4 %collective-permute-done.2 = bf16[96,1408]{1,0:T(8,128)(2,1)S(1)} collective-permute-done((bf16[96,1408]{1,0:T(8,128)(2,1)S(1)}, bf16[96,1408]{1,0:T(8,128)(2,1)S(1)}, u32[]{:S(2)}, u32[]{:S(2)}) %collective-permute-start.2) | collective-permute-done | bytes 270368 | tf_op jit(solution)/shard_map/ppermute | solution.py:535
  29.6 2.5 %collective-permute-start.3 = (bf16[32,1408]{1,0:T(8,128)(2,1)S(1)}, bf16[32,1408]{1,0:T(8,128)(2,1)S(1)}, u32[]{:S(2)}, u32[]{:S(2)}) collective-permute-start(bf16[32,1408]{1,0:T(8,128)(2,1)S(1)} %fusion.12), channel_id=1, source_target_pairs={{0,24},{8,16},{16,8},{24,0},{1,25},{9,17},{17,9},{25,1},{2,26},{10... | collective-permute-start | bytes 270344 | tf_op jit(solution)/shard_map/ppermute | solution.py:535
  32.1 0.0 copy-done.1
  32.1 0.0 collective-permute-start.5
  32.1 0.0 copy-done.6
  32.2 0.0 copy-done.7
  32.2 0.0 copy-done.8
  32.2 0.6 collective-permute-start.4
  32.8 0.5 collective-permute-start.7
  33.2 0.0 copy-done.3
  33.2 0.0 copy-done.4
  33.2 0.0 copy-done.5
  33.2 4.8 %shard_map.185 = (bf16[1280,640]{1,0:T(8,128)(2,1)S(1)}, bf16[1280,640]{1,0:T(8,128)(2,1)S(1)}, bf16[1280,640]{1,0:T(8,128)(2,1)S(1)}, f32[2,128]{1,0:T(2,128)S(1)}) custom-call(s32[1]{0:T(128)} %bitcast.core_ref, f32[2,128]{1,0:T(2,128)S(1)} %get-tuple-element.63.token_ref, f32[16,1280]{1,0:T(8,128)S(1)} %copy-done.3, f32[16,1280]{1,0:T(8,128)S(1)} %copy-done.4, ...), custom_call_target="tpu_custom_call" | custom-call | flops 19660800 | bytes 7372800 | tf_op jit(solution)/shard_map/pallas_call | solution.py:283
  38.1 0.0 collective-permute-done.3
  38.2 0.1 collective-permute-start.6
  38.3 0.0 collective-permute-done.4.far_ref
  38.3 1.2 %shard_map.186 = (bf16[256,640]{1,0:T(8,128)(2,1)S(1)}, bf16[256,640]{1,0:T(8,128)(2,1)S(1)}) custom-call(bf16[128,1280]{1,0:T(8,128)(2,1)S(1)} %pad_maximum_fusion.near_ref, bf16[128,1280]{1,0:T(8,128)(2,1)S(1)} %collective-permute-done.4.far_ref, bf16[1280,640]{1,0:T(8,128)(2,1)S(1)} %get-tuple-element.67.key_ref, ...), custom_call_target="tpu_custom_call" | custom-call | flops 838860800 | bytes 3276800 | tf_op jit(solution)/shard_map/pallas_call | solution.py:430
  39.5 0.0 collective-permute-done.5.theirs_ref
  39.6 0.3 collective-permute-done.6.rim_theirs_ref
  39.8 12.5 %shard_map.187.mine_ref = bf16[512,640]{1,0:T(8,128)(2,1)S(1)} custom-call(s32[1]{0:T(128)} %bitcast.core_ref, f32[2,128]{1,0:T(2,128)S(1)} %fusion.20.sums_ref, bf16[16,16,1280]{2,1,0:T(8,128)(2,1)S(1)} %copy-done.1, bf16[16,16,1280]{2,1,0:T(8,128)(2,1)S(1)} %collective-permute-done.5.theirs_ref, bf16[96,1280]{1,0:T(8,128)(2,1)S(1)} %pad_maximum_fusion.1.rim_mine_ref, ...), custom_call_target="tpu_custom_call" | custom-call | flops 7549747200 | bytes 14745600 | tf_op jit(solution)/shard_map/pallas_call | solution.py:400
  52.4 0.0 collective-permute-done.7.beyond_ref
  52.4 0.3 collective-permute-start.8
  52.7 0.3 collective-permute-start.9
  53.0 0.0 copy-done.9
  53.0 0.0 copy-done.2
  53.0 2.7 %shard_map.188 = (bf16[640,1280]{1,0:T(8,128)(2,1)S(1)}, f32[2,128]{1,0:T(2,128)}) custom-call(s32[1]{0:T(128)} %bitcast.core_ref, f32[2,128]{1,0:T(2,128)S(1)} %get-tuple-element.81.token_ref, f32[16,1280]{1,0:T(8,128)S(1)} %copy-done.2, s32[320,1280]{1,0:T(8,128)} %refs_1_.3), custom_call_target="tpu_custom_call" | custom-call | flops 6553600 | bytes 2457600 | tf_op jit(solution)/shard_map/pallas_call | solution.py:283
  55.7 0.0 collective-permute-done.9.far_ref
  55.7 0.0 collective-permute-done.8.theirs_ref
  55.7 11.5 %shard_map.189 = (bf16[256,1280]{1,0:T(8,128)(2,1)S(1)}, f32[256,1280]{1,0:T(8,128)S(1)}) custom-call(s32[1]{0:T(128)} %bitcast.core_ref, bf16[512,640]{1,0:T(8,128)(2,1)S(1)} %shard_map.187.mine_ref, bf16[512,640]{1,0:T(8,128)(2,1)S(1)} %collective-permute-done.8.theirs_ref, f32[1,1280]{1,0:T(1,128)S(1)} %broadcast_in_dim.27.gain_ref, ...), custom_call_target="tpu_custom_call" | custom-call | tf_op jit(solution)/shard_map/pallas_call | solution.py:512
  67.2 0.3 collective-permute-start.10
  67.5 1.9 %collective-permute-done.10 = bf16[256,1280]{1,0:T(8,128)(2,1)S(1)} collective-permute-done((bf16[256,1280]{1,0:T(8,128)(2,1)S(1)}, bf16[256,1280]{1,0:T(8,128)(2,1)S(1)}, u32[]{:S(2)}, u32[]{:S(2)}) %collective-permute-start.10) | collective-permute-done | bytes 655392 | tf_op jit(solution)/shard_map/ppermute | solution.py:535
  69.3 1.0 %add_convert_fusion = bf16[256,1280]{1,0:T(8,128)(2,1)} fusion(f32[256,1280]{1,0:T(8,128)S(1)} %get-tuple-element.83, bf16[256,1280]{1,0:T(8,128)(2,1)S(1)} %collective-permute-done.10), kind=kLoop, calls=%fused_computation | loop fusion | flops 983040 | bytes 2621440 | tf_op jit(solution)/shard_map/convert_element_type | solution.py:656
  (40 shorter events, 0.4 us)
Async XLA Ops:
  0.7 5.4 %copy-start = (f32[16,1280]{1,0:T(8,128)S(1)}, f32[16,1280]{1,0:T(8,128)}, u32[]{:S(2)}) copy-start(f32[16,1280]{1,0:T(8,128)} %table_ref.5) | copy-start | bytes 245764
  3.6 7.0 %collective-permute-start = (bf16[32,1408]{1,0:T(8,128)(2,1)S(1)}, bf16[32,1408]{1,0:T(8,128)(2,1)S(1)}, u32[]{:S(2)}, u32[]{:S(2)}) collective-permute-start(bf16[32,1408]{1,0:T(8,128)(2,1)S(1)} %fusion.13), channel_id=1, source_target_pairs={{0,3},{1,2},{2,1},{3,0},{4,7},{5,6},{6,5},{7,4},{8,11},{9,10},{10,... | collective-permute-start | bytes 270344 | tf_op jit(solution)/shard_map/ppermute | solution.py:535
  10.7 9.9 %collective-permute-start.1 = (bf16[48,1408]{1,0:T(8,128)(2,1)S(1)}, bf16[48,1408]{1,0:T(8,128)(2,1)S(1)}, u32[]{:S(2)}, u32[]{:S(2)}) collective-permute-start(bf16[48,1408]{1,0:T(8,128)(2,1)S(1)} %fusion.11), channel_id=1, source_target_pairs={{0,7},{1,6},{2,5},{3,4},{4,3},{5,2},{6,1},{7,0},{8,15},{9,14},{10,... | collective-permute-start | bytes 405512 | tf_op jit(solution)/shard_map/ppermute | solution.py:535
  20.7 8.8 %collective-permute-start.2 = (bf16[96,1408]{1,0:T(8,128)(2,1)S(1)}, bf16[96,1408]{1,0:T(8,128)(2,1)S(1)}, u32[]{:S(2)}, u32[]{:S(2)}) collective-permute-start(bf16[96,1408]{1,0:T(8,128)(2,1)S(1)} %fusion.5), channel_id=1, source_target_pairs={{0,8},{8,0},{16,24},{24,16},{1,9},{9,1},{17,25},{25,17},{2,10},{10... | collective-permute-start | bytes 811016 | tf_op jit(solution)/shard_map/ppermute | solution.py:535
  22.3 9.9 %copy-start.1 = (bf16[16,16,1280]{2,1,0:T(8,128)(2,1)S(1)}, bf16[16,16,1280]{2,1,0:T(8,128)(2,1)}, u32[]{:S(2)}) copy-start(bf16[16,16,1280]{2,1,0:T(8,128)(2,1)} %mine_ref.1) | copy-start | bytes 1966084
  22.3 9.9 %copy-start.6 = (f32[1280]{0:T(1024)S(1)}, f32[1280]{0:T(1024)}, u32[]{:S(2)}) copy-start(f32[1280]{0:T(1024)} %param.24) | copy-start | bytes 15364
  22.3 9.9 %copy-start.7 = (f32[1280]{0:T(1024)S(1)}, f32[1280]{0:T(1024)}, u32[]{:S(2)}) copy-start(f32[1280]{0:T(1024)} %param.25) | copy-start | bytes 15364
  22.3 9.9 %copy-start.8 = (f32[1280]{0:T(1024)S(1)}, f32[1280]{0:T(1024)}, u32[]{:S(2)}) copy-start(f32[1280]{0:T(1024)} %param.28) | copy-start | bytes 15364
  22.3 11.0 %copy-start.3 = (f32[16,1280]{1,0:T(8,128)S(1)}, f32[16,1280]{1,0:T(8,128)}, u32[]{:S(2)}) copy-start(f32[16,1280]{1,0:T(8,128)} %refs_0_.2) | copy-start | bytes 245764
  22.3 10.9 %copy-start.4 = (f32[16,1280]{1,0:T(8,128)S(1)}, f32[16,1280]{1,0:T(8,128)}, u32[]{:S(2)}) copy-start(f32[16,1280]{1,0:T(8,128)} %refs_1_.2) | copy-start | bytes 245764
  22.3 10.9 %copy-start.5 = (f32[16,1280]{1,0:T(8,128)S(1)}, f32[16,1280]{1,0:T(8,128)}, u32[]{:S(2)}) copy-start(f32[16,1280]{1,0:T(8,128)} %refs_2_.1) | copy-start | bytes 245764
  29.6 8.5 %collective-permute-start.3 = (bf16[32,1408]{1,0:T(8,128)(2,1)S(1)}, bf16[32,1408]{1,0:T(8,128)(2,1)S(1)}, u32[]{:S(2)}, u32[]{:S(2)}) collective-permute-start(bf16[32,1408]{1,0:T(8,128)(2,1)S(1)} %fusion.12), channel_id=1, source_target_pairs={{0,24},{8,16},{16,8},{24,0},{1,25},{9,17},{17,9},{25,1},{2,26},{10... | collective-permute-start | bytes 270344 | tf_op jit(solution)/shard_map/ppermute | solution.py:535
  32.1 7.4 %collective-permute-start.5 = (bf16[16,16,1280]{2,1,0:T(8,128)(2,1)S(1)}, bf16[16,16,1280]{2,1,0:T(8,128)(2,1)S(1)}, u32[]{:S(2)}, u32[]{:S(2)}) collective-permute-start(bf16[16,16,1280]{2,1,0:T(8,128)(2,1)S(1)} %copy-done.1), channel_id=1, source_target_pairs={{0,1},{1,0},{2,3},{3,2},{4,5},{5,4},{6,7},{7,6},{8,9},{9,8},{10,11... | collective-permute-start | bytes 1966088 | tf_op jit(solution)/shard_map/ppermute | solution.py:535
  32.2 6.1 %collective-permute-start.4 = (bf16[128,1280]{1,0:T(8,128)(2,1)S(1)}, bf16[128,1280]{1,0:T(8,128)(2,1)S(1)}, u32[]{:S(2)}, u32[]{:S(2)}) collective-permute-start(bf16[128,1280]{1,0:T(8,128)(2,1)S(1)} %pad_maximum_fusion.near_ref), channel_id=1, source_target_pairs={{0,1},{1,0},{2,3},{3,2},{4,5},{5,4},{6,7},{7,6},{8,9},{9,8},{10,11... | collective-permute-start | bytes 983048 | tf_op jit(solution)/shard_map/ppermute | solution.py:535
  32.8 19.6 %collective-permute-start.7 = (bf16[128,1280]{1,0:T(8,128)(2,1)S(1)}, bf16[128,1280]{1,0:T(8,128)(2,1)S(1)}, u32[]{:S(2)}, u32[]{:S(2)}) collective-permute-start(bf16[128,1280]{1,0:T(8,128)(2,1)S(1)} %pad_maximum_fusion.near_ref), channel_id=1, source_target_pairs={{0,24},{8,16},{16,8},{24,0},{1,25},{9,17},{17,9},{25,1},{2,26},{10... | collective-permute-start | bytes 983048 | tf_op jit(solution)/shard_map/ppermute | solution.py:535
  38.2 1.6 %collective-permute-start.6 = (bf16[96,1408]{1,0:T(8,128)(2,1)S(1)}, bf16[96,1408]{1,0:T(8,128)(2,1)S(1)}, u32[]{:S(2)}, u32[]{:S(2)}) collective-permute-start(bf16[96,1408]{1,0:T(8,128)(2,1)S(1)} %fusion.7), channel_id=1, source_target_pairs={{0,1},{1,0},{2,3},{3,2},{4,5},{5,4},{6,7},{7,6},{8,9},{9,8},{10,11... | collective-permute-start | bytes 811016 | tf_op jit(solution)/shard_map/ppermute | solution.py:535
  39.8 13.1 %copy-start.9 = (f32[1280]{0:T(1024)S(1)}, f32[1280]{0:T(1024)}, u32[]{:S(2)}) copy-start(f32[1280]{0:T(1024)} %param.29) | copy-start | bytes 15364
  39.8 13.1 %copy-start.2 = (f32[16,1280]{1,0:T(8,128)S(1)}, f32[16,1280]{1,0:T(8,128)}, u32[]{:S(2)}) copy-start(f32[16,1280]{1,0:T(8,128)} %refs_0_.3) | copy-start | bytes 245764
  52.4 3.3 %collective-permute-start.8 = (bf16[512,640]{1,0:T(8,128)(2,1)S(1)}, bf16[512,640]{1,0:T(8,128)(2,1)S(1)}, u32[]{:S(2)}, u32[]{:S(2)}) collective-permute-start(bf16[512,640]{1,0:T(8,128)(2,1)S(1)} %shard_map.187.mine_ref), channel_id=1, source_target_pairs={{0,1},{1,0},{2,3},{3,2},{4,5},{5,4},{6,7},{7,6},{8,9},{9,8},{10,11... | collective-permute-start | bytes 1966088 | tf_op jit(solution)/shard_map/ppermute | solution.py:535
  52.7 3.0 %collective-permute-start.9 = (bf16[128,1280]{1,0:T(8,128)(2,1)S(1)}, bf16[128,1280]{1,0:T(8,128)(2,1)S(1)}, u32[]{:S(2)}, u32[]{:S(2)}) collective-permute-start(bf16[128,1280]{1,0:T(8,128)(2,1)S(1)} %collective-permute-done.7.beyond_ref), channel_id=1, source_target_pairs={{0,1},{1,0},{2,3},{3,2},{4,5},{5,4},{6,7},{7,6},{8,9},{9,8},{10,11... | collective-permute-start | bytes 983048 | tf_op jit(solution)/shard_map/ppermute | solution.py:535
  67.2 2.2 %collective-permute-start.10 = (bf16[256,1280]{1,0:T(8,128)(2,1)S(1)}, bf16[256,1280]{1,0:T(8,128)(2,1)S(1)}, u32[]{:S(2)}, u32[]{:S(2)}) collective-permute-start(bf16[256,1280]{1,0:T(8,128)(2,1)S(1)} %get-tuple-element.84), channel_id=1, source_target_pairs={{0,1},{1,0},{2,3},{3,2},{4,5},{5,4},{6,7},{7,6},{8,9},{9,8},{10,11... | collective-permute-start | bytes 1966088 | tf_op jit(solution)/shard_map/ppermute | solution.py:535

commit v7 on v6

--- a/solution.py
+++ b/solution.py
@@ -243,8 +243,7 @@
 def matrices_kernel(core_ref, token_ref, *refs, count, by_rows, block):
     tables = refs[:count]
     codes = refs[count : 2 * count]
-    weights = refs[2 * count : 3 * count]
-    token_out_ref, words_ref, came = refs[3 * count :]
+    weight_ref, token_out_ref, words_ref, came = refs[2 * count :]
     token_out_ref[...] = token_ref[...]
     rows = words_ref.shape[1]
     blocks = words_ref.shape[2] // LANES
@@ -270,7 +269,7 @@
                 words_ref.at[k, :, lanes_at(at)],
                 tables[k][0:8, far_lanes(at)],
                 tables[k][8:16, far_lanes(at)],
-                weights[k].at[:, lanes_at(at)],
+                weight_ref.at[:, lanes_at(k * blocks + at)],
                 block,
             )
 
@@ -285,8 +284,8 @@
         in_specs=[pl.BlockSpec(memory_space=pltpu.SMEM)]
         + [whole] * (1 + count)
         + [pl.BlockSpec(memory_space=pl.ANY)] * count,
-        out_specs=[whole] * (count + 1),
-        out_shape=[jax.ShapeDtypeStruct((4 * rows, columns), BF)] * count
+        out_specs=[whole] * 2,
+        out_shape=[jax.ShapeDtypeStruct((4 * rows, count * columns), BF)]
         + [jax.ShapeDtypeStruct(token.shape, token.dtype)],
         scratch_shapes=[
             pltpu.VMEM((count, rows, columns), jnp.int32),
@@ -417,30 +416,32 @@
     )(core, sums, mine, theirs, rim_mine, rim_theirs, gain, shift, bias, time_shift, from_hbm(weights))
 
 
-def stale_kernel(near_ref, far_ref, key_ref, value_ref, keys_ref, values_ref):
+def stale_kernel(near_ref, far_ref, weight_ref, keys_ref, values_ref):
     pooled = jnp.concatenate([near_ref[...], far_ref[...]], axis=0)
-    keys_ref[...] = dot(pooled, key_ref[...]).astype(BF)
-    values_ref[...] = dot(pooled, value_ref[...]).astype(BF)
-
-
-def stale_pass(near, far, key_weight, value_weight):
+    half = keys_ref.shape[1]
+    both = dot(pooled, weight_ref[:, half:]).astype(BF)
+    keys_ref[...] = both[:, :half]
+    values_ref[...] = both[:, half:]
+
+
+def stale_pass(near, far, weight):
     rows, channels = near.shape
-    half = key_weight.shape[1]
+    half = weight.shape[1] // 3
     whole = pl.BlockSpec(memory_space=pltpu.VMEM)
     return pl.pallas_call(
         stale_kernel,
-        in_specs=[whole] * 4,
+        in_specs=[whole] * 3,
         out_specs=[whole] * 2,
         out_shape=[jax.ShapeDtypeStruct((2 * rows, half), BF)] * 2,
         compiler_params=params(16),
         cost_estimate=pl.CostEstimate(
             flops=8 * rows * channels * half, bytes_accessed=4 * channels * half, transcendentals=0
         ),
-    )(near, far, key_weight, value_weight)
+    )(near, far, weight)
 
 
 def attention_kernel(
-    core_ref, mine_ref, theirs_ref, gain_ref, query_ref, key_ref, value_ref, near_keys_ref, near_values_ref,
+    core_ref, mine_ref, theirs_ref, gain_ref, weight_ref, near_keys_ref, near_values_ref,
     beyond_ref, far_ref, out_weight_ref, send_ref, keep_ref, normed_ref, q_ref, k_ref, v_ref, mixed_ref, stale_keys_ref, stale_values_ref,
 ):
     rows, half = mine_ref.shape
@@ -468,12 +469,14 @@
     stale_keys_ref[:near_rows] = near_keys_ref[...]
     stale_values_ref[:near_rows] = near_values_ref[...]
     pooled = jnp.concatenate([beyond_ref[...], far_ref[...]], axis=0)
-    stale_keys_ref[near_rows:] = dot(pooled, key_ref[...]).astype(BF)
-    stale_values_ref[near_rows:] = dot(pooled, value_ref[...]).astype(BF)
+    both = dot(pooled, weight_ref[:, half:]).astype(BF)
+    stale_keys_ref[near_rows:] = both[:, :half]
+    stale_values_ref[near_rows:] = both[:, half:]
     normed = normed_ref[...]
-    q_ref[...] = (dot(normed, query_ref[...]).astype(BF) * BF(1.0 / math.sqrt(HEAD_DIM))).astype(BF)
-    k_ref[...] = dot(normed, key_ref[...]).astype(BF)
-    v_ref[...] = dot(normed, value_ref[...]).astype(BF)
+    projected = dot(normed, weight_ref[...]).astype(BF)
+    q_ref[...] = projected[:, :half] * BF(1.0 / math.sqrt(HEAD_DIM))
+    k_ref[...] = projected[:, half : 2 * half]
+    v_ref[...] = projected[:, 2 * half :]
 
     ones = jnp.ones((cells, LANES), BF)
     stale_ones = jnp.ones((stale_keys_ref.shape[0], LANES), BF)
@@ -503,7 +506,7 @@
     keep_ref[...] += dot(mixture[:cells], out_weight_ref[...])
 
 
-def attention_pass(core, mine, theirs, gain, query, key, value, near_keys, near_values, beyond, far, out_weight):
+def attention_pass(core, mine, theirs, gain, projections, near_keys, near_values, beyond, far, out_weight):
     rows, half = mine.shape
     channels = 2 * half
     cells = rows // 2
@@ -511,7 +514,7 @@
     small = pl.BlockSpec(memory_space=pltpu.SMEM)
     return pl.pallas_call(
         attention_kernel,
-        in_specs=[small] + [whole] * 11,
+        in_specs=[small] + [whole] * 9,
         out_specs=[whole] * 2,
         out_shape=[
             jax.ShapeDtypeStruct((cells, channels), BF),
@@ -527,7 +530,7 @@
             pltpu.VMEM((4 * far.shape[0], half), BF),
         ],
         compiler_params=params(28),
-    )(core, mine, theirs, gain, query, key, value, near_keys, near_values, beyond, far, out_weight)
+    )(core, mine, theirs, gain, projections, near_keys, near_values, beyond, far, out_weight)
 
 
 def swap(values, axis, step):
@@ -621,7 +624,7 @@
         if at < len(chunks):
             weights, token = decode_taps(core, token, codes_first, table_first, weights, *chunks[at])
         elif at == len(chunks):
-            query, key, value, token = decode_matrices(
+            projections, token = decode_matrices(
                 core, token, (query_codes, key_codes, value_codes), (query_table, key_table, value_table), False
             )
         sums = sums + join_sums(got_border[:across, channels:])
@@ -638,7 +641,7 @@
     parts = jnp.pad(split_sums(sums), ((0, rim.shape[0] - across), (0, 0)))
     partner_rim = swap(jnp.concatenate([rim, parts], axis=1), "col", 1)
     beyond = swap(*final)
-    near_keys, near_values = stale_pass(near, far_near, key, value)
+    near_keys, near_values = stale_pass(near, far_near, projections)
     sums, near_keys = tie(sums, near_keys)
 
     residual = convolve(
@@ -650,7 +653,7 @@
     far = swap(beyond, "col", 1)
     out_weight, _ = decode_matrices(core, token, (out_codes,), (out_table,), True)
     send, keep = attention_pass(
-        core, residual, partner_residual, attn_gain[None], query, key, value, near_keys, near_values, beyond, far, out_weight
+        core, residual, partner_residual, attn_gain[None], projections, near_keys, near_values, beyond, far, out_weight
     )
     output = keep + swap(send, "col", 1).astype(F32)
     return output.astype(BF).reshape(height, across, channels)

time: 70.5 us -> 69.8 us (0.990)
  Pallas kernels: 52.9 us -> 52 us
    pallas_call x2, Pallas kernels: 12.7 us -> 11.8 us  [the longest x1 10.7 us: attention_pass(): pl.pallas_call(attention_kernel, in_specs=[small] + [whole] * 9, out_spec...]
where the time goes in v7:
time: 69.8 us; the launch traced here: 69.6 us
  Pallas kernels  52 us (74%)
  starting transfers between devices  11.3 us (16%)
  waiting for transfers between devices  3.78 us (5%)
  other arithmetic  1.3 us (2%)
  between operations  1.11 us (2%)
    pallas_call x3, Pallas kernels, decode_taps(): pl.pallas_call(functools.partial(taps_kernel, start=start, count=count),...  17.3 us
    pallas_call x1, Pallas kernels, convolve(): pl.pallas_call(functools.partial(conv_kernel, members=members), in_specs=...  12.5 us
    ppermute x11, starting transfers between devices, swap(): return lax.ppermute(values, axis, [(i, i ^ step) for i in range(count)])  11.3 us
    pallas_call x1, Pallas kernels, attention_pass(): pl.pallas_call(attention_kernel, in_specs=[small] + [whole] * 9, out_spec...  10.7 us
    pallas_call x2, Pallas kernels, decode_matrices(): pl.pallas_call(functools.partial(matrices_kernel, count=count, by_rows=by...  7.55 us
    ppermute x11, waiting for transfers between devices, swap(): return lax.ppermute(values, axis, [(i, i ^ step) for i in range(count)])  3.78 us
    pallas_call x1, Pallas kernels, first_pass(): pl.pallas_call(first_kernel, grid=(1,), in_specs=[small, small] + [whole_...  2.81 us
  transfers between devices with their start and end apart: 11, of which 3 were waited for; matrix products, arithmetic and copies ran while one was open for 0% of the time, Pallas kernels for 55%

profile of v7, /device:TPU:0, one launch (start us, length us, event | category | flops | bytes accessed | tf_op | source)
XLA Modules:
  0.0 69.6 jit_solution(8990224091623736223)
XLA Ops:
  0.7 0.0 copy-start
  0.7 2.8 %shard_map.181 = (f32[2,128]{1,0:T(2,128)S(1)}, bf16[4,16,1280]{2,1,0:T(8,128)(2,1)S(1)}, bf16[16,1280]{1,0:T(8,128)(2,1)S(1)}, f32[8,1280]{1,0:T(8,128)S(1)}) custom-call(s32[1]{0:T(128)} %bitcast.core_ref, s32[1]{0:T(128)S(6)} %copy.24.step_ref, bf16[16,16,1280]{2,1,0:T(8,128)(2,1)} %mine_ref.1, bf16[16,16,1280]{2,1,0:T(8,128)(2,1)} %first_ref.1, ...), custom_call_target="tpu_custom_call" | custom-call | tf_op jit(solution)/shard_map/pallas_call | solution.py:115
  3.6 2.5 %collective-permute-start = (bf16[32,1408]{1,0:T(8,128)(2,1)S(1)}, bf16[32,1408]{1,0:T(8,128)(2,1)S(1)}, u32[]{:S(2)}, u32[]{:S(2)}) collective-permute-start(bf16[32,1408]{1,0:T(8,128)(2,1)S(1)} %fusion.13), channel_id=1, source_target_pairs={{0,3},{1,2},{2,1},{3,0},{4,7},{5,6},{6,5},{7,4},{8,11},{9,10},{10,... | collective-permute-start | bytes 270344 | tf_op jit(solution)/shard_map/ppermute | solution.py:538
  6.1 0.0 copy-done
  6.1 4.5 %shard_map.182 = (bf16[9,1280,640]{2,1,0:T(8,128)(2,1)}, f32[2,128]{1,0:T(2,128)S(1)}) custom-call(s32[1]{0:T(128)} %bitcast.core_ref, f32[2,128]{1,0:T(2,128)S(1)} %get-tuple-element.48.token_ref, f32[16,1280]{1,0:T(8,128)S(1)} %copy-done, s32[9,320,1280]{2,1,0:T(8,128)} %codes_ref.5), custom_call_target="tpu_custom_call" | custom-call | flops 13107200 | bytes 4915200 | tf_op jit(solution)/shard_map/pallas_call | solution.py:223
  10.6 0.0 collective-permute-done
  10.7 2.8 %collective-permute-start.1 = (bf16[48,1408]{1,0:T(8,128)(2,1)S(1)}, bf16[48,1408]{1,0:T(8,128)(2,1)S(1)}, u32[]{:S(2)}, u32[]{:S(2)}) collective-permute-start(bf16[48,1408]{1,0:T(8,128)(2,1)S(1)} %fusion.11), channel_id=1, source_target_pairs={{0,7},{1,6},{2,5},{3,4},{4,3},{5,2},{6,1},{7,0},{8,15},{9,14},{10,... | collective-permute-start | bytes 405512 | tf_op jit(solution)/shard_map/ppermute | solution.py:538
  13.5 7.0 %shard_map.183 = (bf16[9,1280,640]{2,1,0:T(8,128)(2,1)}, f32[2,128]{1,0:T(2,128)S(1)}) custom-call(s32[1]{0:T(128)} %bitcast.core_ref, f32[2,128]{1,0:T(2,128)S(1)} %get-tuple-element.52.token_ref, f32[16,1280]{1,0:T(8,128)S(1)} %copy-done, s32[9,320,1280]{2,1,0:T(8,128)} %codes_ref.5, ...), custom_call_target="tpu_custom_call", output_to_operand_aliasing={{0}: (4, {})} | custom-call | flops 26214400 | bytes 9830400 | tf_op jit(solution)/shard_map/pallas_call | solution.py:223
  20.6 0.0 collective-permute-done.1
  20.7 1.6 %collective-permute-start.2 = (bf16[96,1408]{1,0:T(8,128)(2,1)S(1)}, bf16[96,1408]{1,0:T(8,128)(2,1)S(1)}, u32[]{:S(2)}, u32[]{:S(2)}) collective-permute-start(bf16[96,1408]{1,0:T(8,128)(2,1)S(1)} %fusion.5), channel_id=1, source_target_pairs={{0,8},{8,0},{16,24},{24,16},{1,9},{9,1},{17,25},{25,17},{2,10},{10... | collective-permute-start | bytes 811016 | tf_op jit(solution)/shard_map/ppermute | solution.py:538
  22.3 0.0 copy-start.1
  22.3 0.0 copy-start.6
  22.3 0.0 copy-start.3
  22.3 0.0 copy-start.4
  22.3 0.0 copy-start.5
  22.3 5.8 %shard_map.184 = (bf16[9,1280,640]{2,1,0:T(8,128)(2,1)}, f32[2,128]{1,0:T(2,128)S(1)}) custom-call(s32[1]{0:T(128)} %bitcast.core_ref, f32[2,128]{1,0:T(2,128)S(1)} %get-tuple-element.57.token_ref, f32[16,1280]{1,0:T(8,128)S(1)} %copy-done, s32[9,320,1280]{2,1,0:T(8,128)} %codes_ref.5, ...), custom_call_target="tpu_custom_call", output_to_operand_aliasing={{0}: (4, {})} | custom-call | flops 19660800 | bytes 7372800 | tf_op jit(solution)/shard_map/pallas_call | solution.py:223
  28.1 1.4 %collective-permute-done.2 = bf16[96,1408]{1,0:T(8,128)(2,1)S(1)} collective-permute-done((bf16[96,1408]{1,0:T(8,128)(2,1)S(1)}, bf16[96,1408]{1,0:T(8,128)(2,1)S(1)}, u32[]{:S(2)}, u32[]{:S(2)}) %collective-permute-start.2) | collective-permute-done | bytes 270368 | tf_op jit(solution)/shard_map/ppermute | solution.py:538
  29.6 2.5 %collective-permute-start.3 = (bf16[32,1408]{1,0:T(8,128)(2,1)S(1)}, bf16[32,1408]{1,0:T(8,128)(2,1)S(1)}, u32[]{:S(2)}, u32[]{:S(2)}) collective-permute-start(bf16[32,1408]{1,0:T(8,128)(2,1)S(1)} %fusion.12), channel_id=1, source_target_pairs={{0,24},{8,16},{16,8},{24,0},{1,25},{9,17},{17,9},{25,1},{2,26},{10... | collective-permute-start | bytes 270344 | tf_op jit(solution)/shard_map/ppermute | solution.py:538
  32.1 0.0 copy-done.1
  32.1 0.0 collective-permute-start.5
  32.1 0.0 copy-done.6
  32.2 0.0 copy-done.7
  32.2 0.0 copy-done.8
  32.2 0.6 collective-permute-start.4
  32.8 0.5 collective-permute-start.7
  33.2 0.0 copy-done.3
  33.2 0.0 copy-done.4
  33.2 0.0 copy-done.5
  33.2 4.8 %shard_map.185 = (bf16[1280,1920]{1,0:T(8,128)(2,1)S(1)}, f32[2,128]{1,0:T(2,128)S(1)}) custom-call(s32[1]{0:T(128)} %bitcast.core_ref, f32[2,128]{1,0:T(2,128)S(1)} %get-tuple-element.61.token_ref, f32[16,1280]{1,0:T(8,128)S(1)} %copy-done.3, f32[16,1280]{1,0:T(8,128)S(1)} %copy-done.4, f32[16,1280]{1,0:T(8,128)S(1)} %copy-done.5, s32[320,1280]{1,0:T(8,128)} %refs_3_.1, ...), custom_call_target="tpu_custom_call" | custom-call | flops 19660800 | bytes 7372800 | tf_op jit(solution)/shard_map/pallas_call | solution.py:282
  38.1 0.0 collective-permute-done.3
  38.2 0.1 collective-permute-start.6
  38.3 0.0 collective-permute-done.4.far_ref
  38.3 1.0 %shard_map.186 = (bf16[256,640]{1,0:T(8,128)(2,1)S(1)}, bf16[256,640]{1,0:T(8,128)(2,1)S(1)}) custom-call(bf16[128,1280]{1,0:T(8,128)(2,1)S(1)} %pad_maximum_fusion.near_ref, bf16[128,1280]{1,0:T(8,128)(2,1)S(1)} %collective-permute-done.4.far_ref, bf16[1280,1920]{1,0:T(8,128)(2,1)S(1)} %get-tuple-element.65.weight_ref), custom_call_target="tpu_custom_call" | custom-call | flops 838860800 | bytes 3276800 | tf_op jit(solution)/shard_map/pallas_call | solution.py:431
  39.4 0.0 collective-permute-done.5.theirs_ref
  39.4 0.4 collective-permute-done.6.rim_theirs_ref
  39.8 12.5 %shard_map.187.mine_ref = bf16[512,640]{1,0:T(8,128)(2,1)S(1)} custom-call(s32[1]{0:T(128)} %bitcast.core_ref, f32[2,128]{1,0:T(2,128)S(1)} %fusion.20.sums_ref, bf16[16,16,1280]{2,1,0:T(8,128)(2,1)S(1)} %copy-done.1, bf16[16,16,1280]{2,1,0:T(8,128)(2,1)S(1)} %collective-permute-done.5.theirs_ref, bf16[96,1280]{1,0:T(8,128)(2,1)S(1)} %pad_maximum_fusion.1.rim_mine_ref, ...), custom_call_target="tpu_custom_call" | custom-call | flops 7549747200 | bytes 14745600 | tf_op jit(solution)/shard_map/pallas_call | solution.py:399
  52.4 0.0 collective-permute-done.7.beyond_ref
  52.4 0.2 collective-permute-start.8
  52.6 0.4 collective-permute-start.9
  52.9 0.0 copy-done.9
  53.0 0.0 copy-done.2
  53.0 2.7 %shard_map.188 = (bf16[640,1280]{1,0:T(8,128)(2,1)S(1)}, f32[2,128]{1,0:T(2,128)}) custom-call(s32[1]{0:T(128)} %bitcast.core_ref, f32[2,128]{1,0:T(2,128)S(1)} %get-tuple-element.77.token_ref, f32[16,1280]{1,0:T(8,128)S(1)} %copy-done.2, s32[320,1280]{1,0:T(8,128)} %refs_1_.3), custom_call_target="tpu_custom_call" | custom-call | flops 6553600 | bytes 2457600 | tf_op jit(solution)/shard_map/pallas_call | solution.py:282
  55.7 0.0 collective-permute-done.9.far_ref
  55.7 0.0 collective-permute-done.8.theirs_ref
  55.7 10.7 %shard_map.189 = (bf16[256,1280]{1,0:T(8,128)(2,1)S(1)}, f32[256,1280]{1,0:T(8,128)S(1)}) custom-call(s32[1]{0:T(128)} %bitcast.core_ref, bf16[512,640]{1,0:T(8,128)(2,1)S(1)} %shard_map.187.mine_ref, bf16[512,640]{1,0:T(8,128)(2,1)S(1)} %collective-permute-done.8.theirs_ref, f32[1,1280]{1,0:T(1,128)S(1)} %broadcast_in_dim.27.gain_ref, ...), custom_call_target="tpu_custom_call" | custom-call | tf_op jit(solution)/shard_map/pallas_call | solution.py:515
  66.4 0.2 collective-permute-start.10
  66.6 2.0 %collective-permute-done.10 = bf16[256,1280]{1,0:T(8,128)(2,1)S(1)} collective-permute-done((bf16[256,1280]{1,0:T(8,128)(2,1)S(1)}, bf16[256,1280]{1,0:T(8,128)(2,1)S(1)}, u32[]{:S(2)}, u32[]{:S(2)}) %collective-permute-start.10) | collective-permute-done | bytes 655392 | tf_op jit(solution)/shard_map/ppermute | solution.py:538
  68.6 1.0 %add_convert_fusion = bf16[256,1280]{1,0:T(8,128)(2,1)} fusion(f32[256,1280]{1,0:T(8,128)S(1)} %get-tuple-element.79, bf16[256,1280]{1,0:T(8,128)(2,1)S(1)} %collective-permute-done.10), kind=kLoop, calls=%fused_computation | loop fusion | flops 983040 | bytes 2621440 | tf_op jit(solution)/shard_map/convert_element_type | solution.py:659
  (40 shorter events, 0.4 us)
Async XLA Ops:
  0.7 5.4 %copy-start = (f32[16,1280]{1,0:T(8,128)S(1)}, f32[16,1280]{1,0:T(8,128)}, u32[]{:S(2)}) copy-start(f32[16,1280]{1,0:T(8,128)} %table_ref.5) | copy-start | bytes 245764
  3.6 7.0 %collective-permute-start = (bf16[32,1408]{1,0:T(8,128)(2,1)S(1)}, bf16[32,1408]{1,0:T(8,128)(2,1)S(1)}, u32[]{:S(2)}, u32[]{:S(2)}) collective-permute-start(bf16[32,1408]{1,0:T(8,128)(2,1)S(1)} %fusion.13), channel_id=1, source_target_pairs={{0,3},{1,2},{2,1},{3,0},{4,7},{5,6},{6,5},{7,4},{8,11},{9,10},{10,... | collective-permute-start | bytes 270344 | tf_op jit(solution)/shard_map/ppermute | solution.py:538
  10.7 9.9 %collective-permute-start.1 = (bf16[48,1408]{1,0:T(8,128)(2,1)S(1)}, bf16[48,1408]{1,0:T(8,128)(2,1)S(1)}, u32[]{:S(2)}, u32[]{:S(2)}) collective-permute-start(bf16[48,1408]{1,0:T(8,128)(2,1)S(1)} %fusion.11), channel_id=1, source_target_pairs={{0,7},{1,6},{2,5},{3,4},{4,3},{5,2},{6,1},{7,0},{8,15},{9,14},{10,... | collective-permute-start | bytes 405512 | tf_op jit(solution)/shard_map/ppermute | solution.py:538
  20.7 8.8 %collective-permute-start.2 = (bf16[96,1408]{1,0:T(8,128)(2,1)S(1)}, bf16[96,1408]{1,0:T(8,128)(2,1)S(1)}, u32[]{:S(2)}, u32[]{:S(2)}) collective-permute-start(bf16[96,1408]{1,0:T(8,128)(2,1)S(1)} %fusion.5), channel_id=1, source_target_pairs={{0,8},{8,0},{16,24},{24,16},{1,9},{9,1},{17,25},{25,17},{2,10},{10... | collective-permute-start | bytes 811016 | tf_op jit(solution)/shard_map/ppermute | solution.py:538
  22.3 9.9 %copy-start.1 = (bf16[16,16,1280]{2,1,0:T(8,128)(2,1)S(1)}, bf16[16,16,1280]{2,1,0:T(8,128)(2,1)}, u32[]{:S(2)}) copy-start(bf16[16,16,1280]{2,1,0:T(8,128)(2,1)} %mine_ref.1) | copy-start | bytes 1966084
  22.3 9.9 %copy-start.6 = (f32[1280]{0:T(1024)S(1)}, f32[1280]{0:T(1024)}, u32[]{:S(2)}) copy-start(f32[1280]{0:T(1024)} %param.24) | copy-start | bytes 15364
  22.3 9.9 %copy-start.7 = (f32[1280]{0:T(1024)S(1)}, f32[1280]{0:T(1024)}, u32[]{:S(2)}) copy-start(f32[1280]{0:T(1024)} %param.25) | copy-start | bytes 15364
  22.3 9.9 %copy-start.8 = (f32[1280]{0:T(1024)S(1)}, f32[1280]{0:T(1024)}, u32[]{:S(2)}) copy-start(f32[1280]{0:T(1024)} %param.28) | copy-start | bytes 15364
  22.3 11.0 %copy-start.3 = (f32[16,1280]{1,0:T(8,128)S(1)}, f32[16,1280]{1,0:T(8,128)}, u32[]{:S(2)}) copy-start(f32[16,1280]{1,0:T(8,128)} %refs_0_.2) | copy-start | bytes 245764
  22.3 10.9 %copy-start.4 = (f32[16,1280]{1,0:T(8,128)S(1)}, f32[16,1280]{1,0:T(8,128)}, u32[]{:S(2)}) copy-start(f32[16,1280]{1,0:T(8,128)} %refs_1_.2) | copy-start | bytes 245764
  22.3 10.9 %copy-start.5 = (f32[16,1280]{1,0:T(8,128)S(1)}, f32[16,1280]{1,0:T(8,128)}, u32[]{:S(2)}) copy-start(f32[16,1280]{1,0:T(8,128)} %refs_2_.1) | copy-start | bytes 245764
  29.6 8.5 %collective-permute-start.3 = (bf16[32,1408]{1,0:T(8,128)(2,1)S(1)}, bf16[32,1408]{1,0:T(8,128)(2,1)S(1)}, u32[]{:S(2)}, u32[]{:S(2)}) collective-permute-start(bf16[32,1408]{1,0:T(8,128)(2,1)S(1)} %fusion.12), channel_id=1, source_target_pairs={{0,24},{8,16},{16,8},{24,0},{1,25},{9,17},{17,9},{25,1},{2,26},{10... | collective-permute-start | bytes 270344 | tf_op jit(solution)/shard_map/ppermute | solution.py:538
  32.1 7.3 %collective-permute-start.5 = (bf16[16,16,1280]{2,1,0:T(8,128)(2,1)S(1)}, bf16[16,16,1280]{2,1,0:T(8,128)(2,1)S(1)}, u32[]{:S(2)}, u32[]{:S(2)}) collective-permute-start(bf16[16,16,1280]{2,1,0:T(8,128)(2,1)S(1)} %copy-done.1), channel_id=1, source_target_pairs={{0,1},{1,0},{2,3},{3,2},{4,5},{5,4},{6,7},{7,6},{8,9},{9,8},{10,11... | collective-permute-start | bytes 1966088 | tf_op jit(solution)/shard_map/ppermute | solution.py:538
  32.2 6.1 %collective-permute-start.4 = (bf16[128,1280]{1,0:T(8,128)(2,1)S(1)}, bf16[128,1280]{1,0:T(8,128)(2,1)S(1)}, u32[]{:S(2)}, u32[]{:S(2)}) collective-permute-start(bf16[128,1280]{1,0:T(8,128)(2,1)S(1)} %pad_maximum_fusion.near_ref), channel_id=1, source_target_pairs={{0,1},{1,0},{2,3},{3,2},{4,5},{5,4},{6,7},{7,6},{8,9},{9,8},{10,11... | collective-permute-start | bytes 983048 | tf_op jit(solution)/shard_map/ppermute | solution.py:538
  32.8 19.6 %collective-permute-start.7 = (bf16[128,1280]{1,0:T(8,128)(2,1)S(1)}, bf16[128,1280]{1,0:T(8,128)(2,1)S(1)}, u32[]{:S(2)}, u32[]{:S(2)}) collective-permute-start(bf16[128,1280]{1,0:T(8,128)(2,1)S(1)} %pad_maximum_fusion.near_ref), channel_id=1, source_target_pairs={{0,24},{8,16},{16,8},{24,0},{1,25},{9,17},{17,9},{25,1},{2,26},{10... | collective-permute-start | bytes 983048 | tf_op jit(solution)/shard_map/ppermute | solution.py:538
  38.2 1.6 %collective-permute-start.6 = (bf16[96,1408]{1,0:T(8,128)(2,1)S(1)}, bf16[96,1408]{1,0:T(8,128)(2,1)S(1)}, u32[]{:S(2)}, u32[]{:S(2)}) collective-permute-start(bf16[96,1408]{1,0:T(8,128)(2,1)S(1)} %fusion.7), channel_id=1, source_target_pairs={{0,1},{1,0},{2,3},{3,2},{4,5},{5,4},{6,7},{7,6},{8,9},{9,8},{10,11... | collective-permute-start | bytes 811016 | tf_op jit(solution)/shard_map/ppermute | solution.py:538
  39.8 13.1 %copy-start.9 = (f32[1280]{0:T(1024)S(1)}, f32[1280]{0:T(1024)}, u32[]{:S(2)}) copy-start(f32[1280]{0:T(1024)} %param.29) | copy-start | bytes 15364
  39.8 13.1 %copy-start.2 = (f32[16,1280]{1,0:T(8,128)S(1)}, f32[16,1280]{1,0:T(8,128)}, u32[]{:S(2)}) copy-start(f32[16,1280]{1,0:T(8,128)} %refs_0_.3) | copy-start | bytes 245764
  52.4 3.3 %collective-permute-start.8 = (bf16[512,640]{1,0:T(8,128)(2,1)S(1)}, bf16[512,640]{1,0:T(8,128)(2,1)S(1)}, u32[]{:S(2)}, u32[]{:S(2)}) collective-permute-start(bf16[512,640]{1,0:T(8,128)(2,1)S(1)} %shard_map.187.mine_ref), channel_id=1, source_target_pairs={{0,1},{1,0},{2,3},{3,2},{4,5},{5,4},{6,7},{7,6},{8,9},{9,8},{10,11... | collective-permute-start | bytes 1966088 | tf_op jit(solution)/shard_map/ppermute | solution.py:538
  52.6 3.1 %collective-permute-start.9 = (bf16[128,1280]{1,0:T(8,128)(2,1)S(1)}, bf16[128,1280]{1,0:T(8,128)(2,1)S(1)}, u32[]{:S(2)}, u32[]{:S(2)}) collective-permute-start(bf16[128,1280]{1,0:T(8,128)(2,1)S(1)} %collective-permute-done.7.beyond_ref), channel_id=1, source_target_pairs={{0,1},{1,0},{2,3},{3,2},{4,5},{5,4},{6,7},{7,6},{8,9},{9,8},{10,11... | collective-permute-start | bytes 983048 | tf_op jit(solution)/shard_map/ppermute | solution.py:538
  66.4 2.2 %collective-permute-start.10 = (bf16[256,1280]{1,0:T(8,128)(2,1)S(1)}, bf16[256,1280]{1,0:T(8,128)(2,1)S(1)}, u32[]{:S(2)}, u32[]{:S(2)}) collective-permute-start(bf16[256,1280]{1,0:T(8,128)(2,1)S(1)} %get-tuple-element.80), channel_id=1, source_target_pairs={{0,1},{1,0},{2,3},{3,2},{4,5},{5,4},{6,7},{7,6},{8,9},{9,8},{10,11... | collective-permute-start | bytes 1966088 | tf_op jit(solution)/shard_map/ppermute | solution.py:538
